TPU v7x, 128 devices: a whole 4x4x4 slice. The times are simulated.
128 devices in a mesh: wide: 16 (over x_hi, z, core), narrow: 8 (over x_lo, y).
Axes of the slice: x: 4 (x_hi: 2, x_lo: 2; x = x_hi * 2 + x_lo), y: 4, z: 4, core: 2. Of those that a mesh axis runs over, the one named last changes fastest.
Arguments:
- alignment: bfloat16 [128, 1536, 256], P(('wide', 'narrow')), may hold values from -6 to 6
- w_query: bfloat16 [256, 256], replicated, may hold values from -0.375 to 0.375
- w_key: bfloat16 [256, 256], replicated, may hold values from -0.375 to 0.375
- w_value: bfloat16 [256, 256], replicated, may hold values from -0.375 to 0.375
- w_gate: bfloat16 [256, 256], replicated, may hold values from -0.375 to 0.375
- w_attend: bfloat16 [256, 256], replicated, may hold values from -0.75 to 0.75
- w_left: bfloat16 [256, 32], replicated, may hold values from -0.375 to 0.375
- w_right: bfloat16 [256, 32], replicated, may hold values from -0.375 to 0.375
- w_pair: bfloat16 [1024, 128], replicated, may hold values from -1.5 to 1.5
Outputs:
- alignment_out: bfloat16 [128, 1536, 256], P(('wide', 'narrow'))
- pair_update: bfloat16 [1536, 1536, 128], P('wide', 'narrow')
All inputs are finite; a program needn't handle non-finite values.
Results may differ from a plain program's by a relative error of at most 0.02.
Values may be sent and summed in bfloat16 or wider, within the bound.
No kernel may reach another device: no remote copies, remote signals or barrier semaphores. Data moves between devices by JAX's collectives and lax.ppermute only.
A program may use at most 128 MiB of HBM per device.

v0:
```python
import jax
import jax.numpy as jnp
from jax import lax
from jax.sharding import PartitionSpec as P

HEADS = 8
HEAD_DIM = 32


def layer_norm(values):
    values = values.astype(jnp.float32)
    average = jnp.mean(values, axis=-1, keepdims=True)
    centered = values - average
    variance = jnp.mean(centered * centered, axis=-1, keepdims=True)
    return (centered * lax.rsqrt(variance + 1e-05)).astype(jnp.bfloat16)


def project(normed, weight):
    return jnp.dot(normed, weight, preferred_element_type=jnp.float32).astype(jnp.bfloat16)


def attention_setup(blocks, w_query, w_gate):
    seq_loc, res_loc, width = blocks.shape
    normed = layer_norm(blocks)
    query_heads = project(normed, w_query).reshape(seq_loc, res_loc, HEADS, HEAD_DIM)
    gate_act = jax.nn.sigmoid(jnp.dot(normed, w_gate, preferred_element_type=jnp.float32))
    gate_heads = gate_act.reshape(seq_loc, res_loc, HEADS, HEAD_DIM)

    def attend(totals, key_piece, value_piece):
        count = key_piece.shape[0]
        key_heads = key_piece.reshape(count, res_loc, HEADS, HEAD_DIM)
        value_heads = value_piece.reshape(count, res_loc, HEADS, HEAD_DIM)
        scores = jnp.einsum(
            "srhd,trhd->rhst", query_heads, key_heads, preferred_element_type=jnp.float32
        ) * HEAD_DIM ** (-0.5)
        weighted = jnp.exp(scores).astype(jnp.bfloat16)
        denominator = jnp.sum(weighted.astype(jnp.float32), axis=-1)
        numerator = jnp.einsum(
            "rhst,trhd->srhd", weighted, value_heads, preferred_element_type=jnp.float32
        )
        return (numerator, denominator)

    initial = (
        jnp.zeros((seq_loc, res_loc, HEADS, HEAD_DIM), jnp.float32),
        jnp.zeros((res_loc, HEADS, seq_loc), jnp.float32),
    )
    return (normed, gate_heads, attend, initial)


def finish(blocks, gate_heads, numerator, denominator, w_attend):
    seq_loc, res_loc, width = blocks.shape
    attended = gate_heads * numerator / jnp.transpose(denominator, (2, 0, 1))[..., None]
    attended = attended.reshape(seq_loc, res_loc, width).astype(jnp.bfloat16)
    return (
        blocks.astype(jnp.float32) + jnp.dot(attended, w_attend, preferred_element_type=jnp.float32)
    ).astype(jnp.bfloat16)


def pair_grid(left_all, right_all, w_pair):
    seq_all, row_count, opm = left_all.shape
    col_count = right_all.shape[1]
    left_blocks = left_all.reshape(seq_all, row_count // 8, 8, opm).transpose(1, 0, 2, 3)

    def pair_block(left_block):
        outer_prod = (
            jnp.einsum("sic,sje->ijce", left_block, right_all, preferred_element_type=jnp.float32)
            / seq_all
        )
        outer_prod = outer_prod.astype(jnp.bfloat16).reshape(8, col_count, opm * opm)
        return jnp.dot(outer_prod, w_pair, preferred_element_type=jnp.float32).astype(jnp.bfloat16)

    return lax.map(pair_block, left_blocks).reshape(row_count, col_count, w_pair.shape[1])


def body(alignment, w_query, w_key, w_value, w_gate, w_attend, w_left, w_right, w_pair):
    blocks = lax.all_to_all(alignment, "wide", split_axis=1, concat_axis=0, tiled=True)
    normed, gate_heads, attend, initial = attention_setup(blocks, w_query, w_gate)
    key_rows = project(normed, w_key)
    value_rows = project(normed, w_value)
    numerator, denominator = attend(
        initial,
        lax.all_gather(key_rows, "narrow", axis=0, tiled=True),
        lax.all_gather(value_rows, "narrow", axis=0, tiled=True),
    )
    updated = finish(blocks, gate_heads, numerator, denominator, w_attend)
    alignment_out = lax.all_to_all(updated, "wide", split_axis=0, concat_axis=1, tiled=True)
    normed_two = layer_norm(updated)
    left_all = lax.all_gather(project(normed_two, w_left), "narrow", axis=0, tiled=True)
    right_wide = lax.all_gather(project(normed_two, w_right), "wide", axis=1, tiled=True)
    right_all = lax.all_to_all(right_wide, "narrow", split_axis=1, concat_axis=0, tiled=True)
    return (alignment_out, pair_grid(left_all, right_all, w_pair))


def solution(mesh):
    placed = (P(("wide", "narrow"), None, None), P(), P(), P(), P(), P(), P(), P(), P())
    return jax.shard_map(
        body,
        mesh=mesh,
        in_specs=placed,
        out_specs=(P(("wide", "narrow"), None, None), P("wide", "narrow", None)),
        check_vma=False,
    )
```

profile of v0, /device:TPU:1, one launch (start us, length us, event | category | flops | bytes accessed | tf_op | source)
XLA Modules:
  0.0 452.4 jit_solution(4672268286071247428)
XLA Ops:
  7.2 2.8 copy.101
  10.5 8.1 %reduce.2 = bf16[1536,256]{1,0:T(8,128)(2,1)S(1)} reduce(bf16[1536,1,256]{2,1,0:T(2,128)(2,1)S(1)} %bitcast.105, bf16[]{:T(256)} %broadcast.74), dimensions={1}, to_apply=%bitcast.79.reduce_sub_computation | reduce | bytes 1572866
  18.8 23.4 %all_to_all.39 = bf16[16,2,12288]{2,1,0:T(2,128)(2,1)S(1)} all-to-all(bf16[16,2,12288]{2,1,0:T(2,128)(2,1)S(1)} %reshape.87), channel_id=1, replica_groups=mesh['wide'=16,'narrow'=8] {'wide'}, dimensions={0} | all-to-all | bytes 1572864 | tf_op jit(solution)/shard_map/all_to_all | solution.py:76
  49.0 4.7 %copy.84 = bf16[16,96,8,32]{3,0,2,1:T(8,128)(2,1)} copy(bf16[16,96,8,32]{1,3,2,0:T(8,128)(2,1)} %bitcast.108) | data formatting | bytes 1572864 | tf_op jit(solution)/shard_map/reshape | solution.py:25
  55.5 2.9 copy.80
  58.3 57.5 %all-gather.6.cloned.1.call-done = bf16[128,96,256]{2,1,0:T(8,128)(2,1)} async-done(((bf16[16,96,256]{2,1,0:T(8,128)(2,1)}), bf16[128,96,256]{2,1,0:T(8,128)(2,1)}) %all-gather.6.cloned.1.call-update) | async-done | bytes 6291472 | tf_op jit(solution)/shard_map/all_gather | solution.py:82
  115.8 9.2 %copy.83 = bf16[128,96,256]{0,2,1:T(8,128)(2,1)} copy(bf16[128,96,256]{2,1,0:T(8,128)(2,1)} %all-gather.6.cloned.1.call-done) | data formatting | bytes 12582912 | tf_op jit(solution)/shard_map/all_gather | solution.py:82
  124.9 7.6 %convert_reduce_fusion = (f32[96,8,16]{2,1,0:T(8,128)S(1)}, bf16[96,8,16,128]{3,2,1,0:T(8,128)(2,1)}) fusion(bf16[16,96,8,32]{3,0,2,1:T(8,128)(2,1)} %copy.84, bf16[128,96,8,32]{0,3,2,1:T(8,128)(2,1)} %bitcast.95), kind=kOutput, calls=%fused_computation.10 | convolution fusion | flops 106942464 | bytes 10272768 | tf_op jit(solution)/shard_map/srhd,trhd->rhst/dot_general | solution.py:33
  132.5 56.5 %all-gather.4.cloned.1.call-done = bf16[128,96,256]{2,1,0:T(8,128)(2,1)} async-done(((bf16[16,96,256]{2,1,0:T(8,128)(2,1)}), bf16[128,96,256]{2,1,0:T(8,128)(2,1)}) %all-gather.4.cloned.1.call-update) | async-done | bytes 6291472 | tf_op jit(solution)/shard_map/all_gather | solution.py:83
  189.1 9.1 %copy.81 = bf16[128,96,256]{0,2,1:T(8,128)(2,1)} copy(bf16[128,96,256]{2,1,0:T(8,128)(2,1)} %all-gather.4.cloned.1.call-done) | data formatting | bytes 12582912 | tf_op jit(solution)/shard_map/all_gather | solution.py:83
  198.2 9.7 %fusion.24 = f32[96,8,32,16]{2,3,1,0:T(8,128)} fusion(bf16[128,96,8,32]{0,3,2,1:T(8,128)(2,1)} %bitcast.99, bf16[96,8,16,128]{3,2,1,0:T(8,128)(2,1)} %get-tuple-element.66), kind=kOutput, calls=%fused_computation.44 | convolution fusion | flops 100663296 | bytes 11010048 | tf_op jit(solution)/shard_map/rhst,trhd->srhd/dot_general | solution.py:38
  207.9 6.1 %copy.85 = f32[96,8,32,16]{0,2,1,3:T(8,128)} copy(f32[96,8,32,16]{2,3,1,0:T(8,128)} %fusion.24) | data formatting | bytes 3145728 | tf_op jit(solution)/shard_map/rhst,trhd->srhd/dot_general | solution.py:38
  214.1 2.8 fusion.9
  223.0 7.3 %all-to-all-start.1 = ((bf16[16,96,256]{2,1,0:T(8,128)(2,1)}), bf16[16,96,256]{2,1,0:T(8,128)(2,1)S(1)}, u32[]{:S(2)}, u32[]{:S(2)}) async-start(bf16[16,96,256]{2,1,0:T(8,128)(2,1)} %get-tuple-element.68), calls=%async_computation.1 | async-start | bytes 1572864 | tf_op jit(solution)/shard_map/all_to_all | solution.py:86
  230.3 59.8 %all-gather.8.cloned.1.call-done = bf16[16,1536,32]{2,0,1:T(8,128)(2,1)} async-done(((bf16[16,96,32]{2,0,1:T(8,128)(2,1)}), bf16[16,1536,32]{2,0,1:T(8,128)(2,1)}) %all-gather.8.cloned.1.call-update) | async-done | bytes 1572880 | tf_op jit(solution)/shard_map/all_gather | solution.py:89
  290.1 9.5 %reshape.89 = bf16[8,2,49152]{2,1,0:T(2,128)(2,1)} reshape(bf16[1536,16,32]{2,1,0:T(8,128)(2,1)} %bitcast.106) | data formatting | bytes 3145728
  299.6 4.1 all-to-all-start.2
  305.5 39.4 %all_gather.14 = bf16[128,96,32]{1,2,0:T(8,128)(2,1)S(1)} all-gather(bf16[16,96,32]{1,2,0:T(8,128)(2,1)S(1)} %convolution_convert_fusion.5), channel_id=1, replica_groups=mesh['wide'=16,'narrow'=8] {'narrow'}, dimensions={0}, use_global_device_ids=true | all-gather | bytes 884736 | tf_op jit(solution)/shard_map/all_gather | solution.py:88
  344.9 2.1 copy.88
  347.0 5.4 %reshape.90 = bf16[1536,16,32]{2,1,0:T(8,128)(2,1)} reshape(bf16[8,2,49152]{2,1,0:T(2,128)(2,1)S(1)} %all-to-all-done.2) | data formatting | bytes 3145728
  352.4 7.1 %copy.90 = bf16[16,8,192,32]{2,3,0,1:T(8,128)(2,1)} copy(bf16[16,8,192,32]{3,0,2,1:T(8,128)(2,1)} %bitcast.100) | data formatting | bytes 3145728 | tf_op jit(solution)/shard_map/all_to_all | solution.py:90
  359.5 3.5 copy.91
  363.0 81.9 %while.10 = (s32[]{:T(128)}, bf16[12,8,192,128]{3,2,1,0:T(8,128)(2,1)}, bf16[12,128,8,32]{1,3,2,0:T(8,128)(2,1)}, bf16[128,192,32]{0,1,2:T(8,128)(2,1)S(1)}, bf16[1024,128]{1,0:T(8,128)(2,1)S(1)}, /*index=5*/s32[]{:T(128)}) while((s32[]{:T(128)}, bf16[12,8,192,128]{3,2,1,0:T(8,128)(2,1)}, bf16[12,128,8,32]{1,3,2,0:T(8,128)(2,1)}, ...), condition=%wide.region_6.7_spmd, body=%wide.region_5.6_spmd.sunk | while | flops 808648704 | bytes 14877765 | solution.py:72
  363.0 2.1 fusion.45
  365.1 2.6 copy.103
  369.8 2.1 fusion.45
  371.9 2.6 copy.103
  374.5 2.1 fusion.46
  376.6 2.1 fusion.45
  378.7 2.6 copy.103
  383.4 2.1 fusion.45
  385.6 2.6 copy.103
  390.3 2.1 fusion.45
  392.4 2.6 copy.103
  397.1 2.1 fusion.45
  399.2 2.6 copy.103
  403.9 2.1 fusion.45
  406.0 2.6 copy.103
  410.7 2.1 fusion.45
  412.8 2.6 copy.103
  417.5 2.1 fusion.45
  419.7 2.6 copy.103
  424.4 2.1 fusion.45
  426.5 2.6 copy.103
  431.2 2.1 fusion.45
  433.3 2.6 copy.103
  438.0 2.1 fusion.45
  440.1 2.6 copy.103
  (63 shorter events, 41.2 us)
Async XLA Ops:
  7.2 209.8 %copy-start = (bf16[256,256]{1,0:T(8,128)(2,1)S(1)}, bf16[256,256]{1,0:T(8,128)(2,1)}, u32[]{:S(2)}) copy-start(bf16[256,256]{1,0:T(8,128)(2,1)} %param.16) | copy-start | bytes 393220
  7.2 108.6 %all-gather.6.cloned.1.call-start = ((), (), s32[]{:S(2)}) async-start(), calls=%async_computation.4 | async-start | bytes 7077888 | tf_op jit(solution)/shard_map/all_gather | solution.py:82
  43.3 1.2 copy-start.3
  44.0 1.8 copy-start.4
  44.5 2.8 copy-start.5
  45.8 143.3 %all-gather.4.cloned.1.call-start = ((), (), s32[]{:S(2)}) async-start(), calls=%async_computation.3 | async-start | bytes 7077888 | tf_op jit(solution)/shard_map/all_gather | solution.py:83
  47.1 242.9 %all-gather.8.cloned.1.call-start = ((), (), s32[]{:S(2)}) async-start(), calls=%async_computation.5 | async-start | bytes 6684672 | tf_op jit(solution)/shard_map/all_gather | solution.py:89
  49.0 4.7 %copy-start.6 = (bf16[256,256]{1,0:T(8,128)(2,1)S(1)}, bf16[256,256]{1,0:T(8,128)(2,1)}, u32[]{:S(2)}) copy-start(bf16[256,256]{1,0:T(8,128)(2,1)} %param.15) | copy-start | bytes 393220
  217.0 3.2 copy-start.7
  223.0 76.5 %all-to-all-start.1 = ((bf16[16,96,256]{2,1,0:T(8,128)(2,1)}), bf16[16,96,256]{2,1,0:T(8,128)(2,1)S(1)}, u32[]{:S(2)}, u32[]{:S(2)}) async-start(bf16[16,96,256]{2,1,0:T(8,128)(2,1)} %get-tuple-element.68), calls=%async_computation.1 | async-start | bytes 1572864 | tf_op jit(solution)/shard_map/all_to_all | solution.py:86
  299.6 4.2 copy-start.8
  299.6 47.4 %all-to-all-start.2 = ((bf16[8,2,49152]{2,1,0:T(2,128)(2,1)}), bf16[8,2,49152]{2,1,0:T(2,128)(2,1)S(1)}, u32[]{:S(2)}, u32[]{:S(2)}) async-start(bf16[8,2,49152]{2,1,0:T(2,128)(2,1)} %reshape.89), calls=%async_computation.2 | async-start | bytes 3145728 | tf_op jit(solution)/shard_map/all_to_all | solution.py:90
  359.5 3.5 copy-start.2
  444.8 1.0 copy-start.1
Sparse Core Ops, SparseCore 0:
  45.9 69.8 all-gather.5
  118.0 71.0 all-gather.3
  223.1 66.8 all-gather.7
where the time goes:
time: 459 us; the launch traced here: 452 us
  waiting for transfers between devices  174 us (38%)
  local copies, waits for them, and re-layouts  98.7 us (22%)
  matrix products  77.2 us (17%)
  blocking collectives  62.8 us (14%)
  other arithmetic  14 us (3%)
  between operations  14 us (3%)
  starting transfers between devices  11.7 us (3%)
    all_gather x1, waiting for transfers between devices, body(): lax.all_gather(project(normed_two, w_right), 'wide', axis=1, tiled=True)  59.8 us
    all_gather x1, waiting for transfers between devices, body(): lax.all_gather(key_rows, 'narrow', axis=0, tiled=True)  57.5 us
    all_gather x1, waiting for transfers between devices, body(): lax.all_gather(value_rows, 'narrow', axis=0, tiled=True)  56.5 us
    all_gather x1, blocking collectives, body(): lax.all_gather(project(normed_two, w_left), 'narrow', axis=0, tiled=True)  39.4 us
    convert_element_type x12, local copies, waits for them, and re-layouts, pair_block(): outer_prod.astype(jnp.bfloat16).reshape(8, col_count, opm * opm)  31.3 us
    dot_general x12, matrix products, pair_block(): jnp.einsum('sic,sje->ijce', left_block, right_all, preferred_element_type...  25.3 us
    dot_general x12, matrix products, pair_block(): jnp.dot(outer_prod, w_pair, preferred_element_type=jnp.float32)  25.2 us
    all_to_all x1, blocking collectives, body(): lax.all_to_all(alignment, 'wide', split_axis=1, concat_axis=0, tiled=True)  23.4 us
  transfers between devices with their start and end apart: 5, of which 3 were waited for; matrix products, arithmetic and copies ran while one was open for 9% of the time, Pallas kernels for 0%

commit v1 on v0

v1 whole, which is shorter than its diff:
```python
import functools

import jax
import jax.numpy as jnp
from jax import lax
from jax.experimental import pallas as pl
from jax.experimental.pallas import tpu as pltpu
from jax.sharding import Mesh, PartitionSpec as P

HEADS = 8
HEAD_DIM = 32
OPM = 32
SEQS = 128
WIDTH = 256
LANES = 128
AXES = ("x_hi", "z", "core", "x_lo", "y")
SIZES = (2, 4, 2, 2, 4)
BLK = 12
ROWS = 2 * BLK
PEERS = 8
VMEM = pltpu.CompilerParams(vmem_limit_bytes=50 * 1024 * 1024)
F32 = jnp.float32
BF16 = jnp.bfloat16
NT = (((1,), (1,)), ((), ()))


def block_of(device):
    y, rest = device % 4, device // 4
    x_lo, rest = rest % 2, rest // 2
    core, rest = rest % 2, rest // 2
    z, x_hi = rest % 4, rest // 4
    return (x_lo * 4 + y) * 16 + core * 8 + x_hi * 4 + z


BLOCK_OF = [block_of(d) for d in range(SEQS)]
DEVICE_OF = [BLOCK_OF.index(b) for b in range(SEQS)]


def vmem_spec():
    return pl.BlockSpec(memory_space=pltpu.VMEM)


def normalise(values):
    average = jnp.mean(values, axis=-1, keepdims=True)
    centered = values - average
    variance = jnp.mean(centered * centered, axis=-1, keepdims=True)
    return (centered * lax.rsqrt(variance + 1e-05)).astype(BF16)


def pack_kernel(x_ref, out_ref):
    for group in range(SEQS // 4):
        rows = x_ref[group * 48 : group * 48 + 48, :].astype(F32)
        for part in range(4):
            piece = rows[part * BLK : part * BLK + BLK]
            both = jnp.concatenate([piece[:, :LANES], piece[:, LANES:]], axis=0)
            out_ref[DEVICE_OF[group * 4 + part]] = both.astype(BF16)


def unpack_kernel(x_ref, out_ref):
    for group in range(SEQS // 4):
        pieces = [x_ref[DEVICE_OF[group * 4 + part]].astype(F32) for part in range(4)]
        left = jnp.concatenate([piece[:BLK] for piece in pieces], axis=0)
        right = jnp.concatenate([piece[BLK:] for piece in pieces], axis=0)
        out_ref[group * 48 : group * 48 + 48, :] = jnp.concatenate([left, right], axis=1).astype(BF16)


def attention_kernel(
    x_ref, wq_ref, wk_ref, wv_ref, wg_ref, wa_ref, wlr_ref, u_ref, lt_ref, rt_ref,
    flat, normed, query, key, value, gate, attended, update,
):
    flat[...] = x_ref[...].astype(F32).reshape(SEQS * ROWS, LANES)

    def residue(r):
        return jnp.concatenate(
            [flat[pl.ds(r, SEQS, stride=ROWS), :], flat[pl.ds(BLK + r, SEQS, stride=ROWS), :]], axis=1
        )

    def span(r):
        return pl.ds(pl.multiple_of(r * SEQS, SEQS), SEQS)

    for r in range(BLK):
        normed[span(r), :] = normalise(residue(r))
    rows = normed[...]
    query[...] = jnp.dot(rows, wq_ref[...], preferred_element_type=F32).astype(BF16)
    key[...] = jnp.dot(rows, wk_ref[...], preferred_element_type=F32).astype(BF16)
    value[...] = jnp.dot(rows, wv_ref[...], preferred_element_type=F32).astype(BF16)
    gate[...] = jax.nn.sigmoid(jnp.dot(rows, wg_ref[...], preferred_element_type=F32))

    lane = lax.broadcasted_iota(jnp.int32, (SEQS, WIDTH), 1) // HEAD_DIM
    own = [(lane == h) for h in range(HEADS)]
    zero = jnp.zeros((SEQS, WIDTH), BF16)
    ones = jnp.concatenate([jnp.where(m, 1.0, 0.0).astype(BF16) for m in own], axis=0)

    def attend(r, carry):
        at = span(r)
        q, k, v = query[at, :], key[at, :], value[at, :]
        k_heads = jnp.concatenate([jnp.where(m, k, zero) for m in own], axis=0)
        v_heads = jnp.concatenate([jnp.where(m, v, zero) for m in own], axis=0)
        scores = lax.dot_general(q, k_heads, NT, preferred_element_type=F32) * HEAD_DIM ** (-0.5)
        weighted = jnp.exp(scores).astype(BF16)
        numerator = jnp.dot(weighted, v_heads, preferred_element_type=F32)
        denominator = jnp.dot(weighted, ones, preferred_element_type=F32)
        attended[at, :] = (gate[at, :] * numerator / denominator).astype(BF16)
        return carry

    lax.fori_loop(0, BLK, attend, 0)
    update[...] = jnp.dot(attended[...], wa_ref[...], preferred_element_type=F32)
    for r in range(BLK):
        updated = (residue(r) + update[span(r), :]).astype(BF16).astype(F32)
        flat[pl.ds(r, SEQS, stride=ROWS), :] = updated[:, :LANES]
        flat[pl.ds(BLK + r, SEQS, stride=ROWS), :] = updated[:, LANES:]
        normed[span(r), :] = normalise(updated)
    sides = lax.dot_general(wlr_ref[...], normed[...], NT, preferred_element_type=F32).astype(BF16)
    for r in range(BLK):
        lt_ref[r * OPM : (r + 1) * OPM, :] = sides[:OPM, r * SEQS : (r + 1) * SEQS]
        rt_ref[r * OPM : (r + 1) * OPM, :] = sides[OPM:, r * SEQS : (r + 1) * SEQS]
    u_ref[...] = flat[...].reshape(SEQS, ROWS, LANES).astype(BF16)


def attention(x, wq, wk, wv, wg, wa, wlr):
    tall = SEQS * BLK
    return pl.pallas_call(
        attention_kernel,
        out_shape=(
            jax.ShapeDtypeStruct((SEQS, ROWS, LANES), BF16),
            jax.ShapeDtypeStruct((BLK * OPM, SEQS), BF16),
            jax.ShapeDtypeStruct((BLK * OPM, SEQS), BF16),
        ),
        in_specs=[vmem_spec()] * 7,
        out_specs=(vmem_spec(),) * 3,
        scratch_shapes=[
            pltpu.VMEM((SEQS * ROWS, LANES), F32),
            pltpu.VMEM((tall, WIDTH), BF16),
            pltpu.VMEM((tall, WIDTH), BF16),
            pltpu.VMEM((tall, WIDTH), BF16),
            pltpu.VMEM((tall, WIDTH), BF16),
            pltpu.VMEM((tall, WIDTH), F32),
            pltpu.VMEM((tall, WIDTH), BF16),
            pltpu.VMEM((tall, WIDTH), F32),
        ],
        compiler_params=VMEM,
        name="attention",
    )(x, wq, wk, wv, wg, wa, wlr)


def pair_kernel(at_ref, l_ref, own_ref, other_ref, we_ref, wo_ref, out_ref, flat, right, outer):
    cols = 192
    half = PEERS * BLK * OPM

    @pl.when(pl.program_id(0) == 0)
    def _():
        first = pl.multiple_of(at_ref[1] * half, half)
        flat[pl.ds(first, half), :] = own_ref[...].astype(F32)
        flat[pl.ds(pl.multiple_of(half - first, half), half), :] = other_ref[...].astype(F32)
        for p in range(OPM // 2):
            even = flat[pl.ds(2 * p, cols, stride=OPM), :]
            odd = flat[pl.ds(2 * p + 1, cols, stride=OPM), :]
            right[p] = jnp.concatenate([even, odd], axis=0).T.astype(BF16)

    left = l_ref[0]
    for p in range(OPM // 2):
        product = jnp.dot(left, right[p], preferred_element_type=F32).astype(BF16)
        for i in range(BLK):
            outer[i, p * OPM : (p + 1) * OPM, :] = product[i * OPM : (i + 1) * OPM]
    even_w, odd_w = we_ref[...], wo_ref[...]
    for i in range(BLK):
        even = jnp.dot(even_w, outer[i, :, :256], preferred_element_type=F32)
        odd = jnp.dot(odd_w, outer[i, :, 128:], preferred_element_type=F32)
        total = (even[:, :cols] + odd[:, 64:]) * (1.0 / SEQS)
        out_ref[i] = total.T.astype(BF16)


def pair_grid(place, left, own, other, w_even, w_odd):
    half = PEERS * BLK * OPM
    return pl.pallas_call(
        pair_kernel,
        out_shape=jax.ShapeDtypeStruct((PEERS * BLK, 192, 128), BF16),
        grid_spec=pltpu.PrefetchScalarGridSpec(
            num_scalar_prefetch=1,
            grid=(PEERS,),
            in_specs=[
                pl.BlockSpec((1, BLK * OPM, SEQS), lambda k, at: (k, 0, 0)),
                pl.BlockSpec((half, SEQS), lambda k, at: (0, 0)),
                pl.BlockSpec((half, SEQS), lambda k, at: (0, 0)),
                pl.BlockSpec((128, 512), lambda k, at: (0, 0)),
                pl.BlockSpec((128, 512), lambda k, at: (0, 0)),
            ],
            out_specs=pl.BlockSpec((BLK, 192, 128), lambda k, at: (k ^ at[0], 0, 0)),
            scratch_shapes=[
                pltpu.VMEM((2 * half, SEQS), F32),
                pltpu.VMEM((OPM // 2, SEQS, 384), BF16),
                pltpu.VMEM((BLK, 512, 384), BF16),
            ],
        ),
        compiler_params=VMEM,
        name="pair_grid",
    )(place, left, own, other, w_even, w_odd)


def left_route(step):
    pairs = []
    for d in range(SEQS):
        y, x_lo, core, z, x_hi = d % 4, d // 4 % 2, d // 8 % 2, d // 16 % 4, d // 64
        place = (x_hi * 4 + z) ^ step
        pairs.append((d, ((x_lo * 4 + y) * 2 + core) * 8 + place))
    return pairs


def body(alignment, w_query, w_key, w_value, w_gate, w_attend, w_left, w_right, w_pair):
    one = jax.ShapeDtypeStruct((SEQS, ROWS, LANES), BF16)
    packed = pl.pallas_call(
        pack_kernel, out_shape=one, in_specs=[vmem_spec()], out_specs=vmem_spec(),
        compiler_params=VMEM, name="pack",
    )(alignment[0])
    blocks = lax.all_to_all(packed, AXES, split_axis=0, concat_axis=0, tiled=True)
    w_sides = jnp.concatenate([w_left, w_right], axis=1).T
    updated, left, right = attention(blocks, w_query, w_key, w_value, w_gate, w_attend, w_sides)

    copies = jnp.broadcast_to(right[None], (PEERS,) + right.shape)
    own = lax.all_to_all(copies, ("x_hi", "z"), split_axis=0, concat_axis=0, tiled=True)
    own = own.reshape(PEERS * BLK * OPM, SEQS)
    other = lax.ppermute(own, "core", [(0, 1), (1, 0)])
    lefts = jnp.stack([lax.ppermute(left, AXES, left_route(k)) for k in range(PEERS)])

    returned = lax.all_to_all(updated, AXES, split_axis=0, concat_axis=0, tiled=True)
    weights = w_pair.reshape(OPM, OPM // 2, 2, 128).transpose(2, 3, 1, 0).reshape(2, 128, 512)
    place = jnp.stack([lax.axis_index(("x_lo", "y")), lax.axis_index("core")]).astype(jnp.int32)
    pair_update = pair_grid(place, lefts, own, other, weights[0], weights[1])
    alignment_out = pl.pallas_call(
        unpack_kernel, out_shape=jax.ShapeDtypeStruct(alignment.shape[1:], BF16),
        in_specs=[vmem_spec()], out_specs=vmem_spec(), compiler_params=VMEM, name="unpack",
    )(returned)
    return (alignment_out[None], pair_update)


def solution(mesh):
    fine = Mesh(mesh.devices.reshape(SIZES), AXES)
    placed = (P(AXES, None, None),) + (P(),) * 8
    return jax.shard_map(
        body,
        mesh=fine,
        in_specs=placed,
        out_specs=(P(AXES, None, None), P(AXES[:3], AXES[3:], None)),
        check_vma=False,
    )
```

time: 459 us -> 142 us (0.31); the launches traced: 452 us -> 141 us
  waiting for transfers between devices: 174 us -> 49.1 us
  local copies, waits for them, and re-layouts: 98.7 us -> 7.7 us
  matrix products: 77.2 us -> 0 us
  blocking collectives: 62.8 us -> 0 us
  Pallas kernels: 0 us -> 36.8 us
  starting transfers between devices: 11.7 us -> 47 us
  other arithmetic: 14 us -> 0.08 us
  between operations: 14 us -> 0.86 us
    all_gather x3 -> x0, waiting for transfers between devices: 174 us -> none  [the longest x1 59.8 us: body(): lax.all_gather(project(normed_two, w_right), 'wide', axis=1, tiled=True)]
    dot_general x33 -> x0, matrix products: 77.2 us -> none  [the longest x12 25.3 us: pair_block(): jnp.einsum('sic,sje->ijce', left_block, right_all, preferred_element_type...]
    all_gather x1 -> x0, blocking collectives: 39.4 us -> none  [body(): lax.all_gather(project(normed_two, w_left), 'narrow', axis=0, tiled=True)]
    pallas_call x0 -> x4, Pallas kernels: none -> 36.8 us  [the longest x1 25.2 us: pair_grid(): pl.pallas_call(pair_kernel, out_shape=jax.ShapeDtypeStruct((PEERS * BLK,...]
    convert_element_type x14 -> x0, local copies, waits for them, and re-layouts: 33.7 us -> none  [the longest x12 31.3 us: pair_block(): outer_prod.astype(jnp.bfloat16).reshape(8, col_count, opm * opm)]
    all_to_all x2 -> x3, starting transfers between devices: 11.4 us -> 37.8 us  [the longest x1 13.7 us: body(): lax.all_to_all(updated, AXES, split_axis=0, concat_axis=0, tiled=True)]
    all_to_all x2 -> x3, waiting for transfers between devices: 0.01 us -> 25.1 us  [the longest x1 14.1 us: body(): lax.all_to_all(packed, AXES, split_axis=0, concat_axis=0, tiled=True)]
    ppermute x0 -> x9, waiting for transfers between devices: none -> 23.9 us  [the longest x8 23.9 us: body(): lax.ppermute(left, AXES, left_route(k))]
  transfers between devices with their start and end apart: 5 -> 12, of which waited for: 3 -> 5; matrix products, arithmetic and copies ran while one was open for 9% -> 5% of each run, Pallas kernels for 0% -> 1%
where the time goes in v1:
time: 142 us; the launch traced here: 141 us
  waiting for transfers between devices  49.1 us (35%)
  starting transfers between devices  47 us (33%)
  Pallas kernels  36.8 us (26%)
  local copies, waits for them, and re-layouts  7.7 us (5%)
    pallas_call x1, Pallas kernels, pair_grid(): pl.pallas_call(pair_kernel, out_shape=jax.ShapeDtypeStruct((PEERS * BLK,...  25.2 us
    ppermute x8, waiting for transfers between devices, body(): lax.ppermute(left, AXES, left_route(k))  23.9 us
    all_to_all x1, waiting for transfers between devices, body(): lax.all_to_all(packed, AXES, split_axis=0, concat_axis=0, tiled=True)  14.1 us
    all_to_all x1, starting transfers between devices, body(): lax.all_to_all(updated, AXES, split_axis=0, concat_axis=0, tiled=True)  13.7 us
    all_to_all x1, starting transfers between devices, body(): lax.all_to_all(copies, ('x_hi', 'z'), split_axis=0, concat_axis=0, tiled=...  12.6 us
    all_to_all x1, starting transfers between devices, body(): lax.all_to_all(packed, AXES, split_axis=0, concat_axis=0, tiled=True)  11.5 us
    all_to_all x1, waiting for transfers between devices, body(): lax.all_to_all(updated, AXES, split_axis=0, concat_axis=0, tiled=True)  11 us
    pallas_call x1, Pallas kernels, attention(): pl.pallas_call(attention_kernel, out_shape=(jax.ShapeDtypeStruct((SEQS, R...  9.5 us
  transfers between devices with their start and end apart: 12, of which 5 were waited for; matrix products, arithmetic and copies ran while one was open for 5% of the time, Pallas kernels for 1%

profile of v1, /device:TPU:1, one launch (start us, length us, event | category | flops | bytes accessed | tf_op | source)
XLA Modules:
  0.0 141.5 jit_solution(13156895632671699158)
XLA Ops:
  0.6 0.0 copy-start
  0.6 1.1 copy-done
  1.8 0.0 copy-start.3
  1.8 0.0 copy-start.4
  1.8 0.0 copy-start.5
  1.8 1.0 pack.1
  2.8 11.5 %all-to-all-start = ((bf16[128,24,128]{2,1,0:T(8,128)(2,1)}), bf16[128,24,128]{2,1,0:T(8,128)(2,1)S(1)}, u32[]{:S(2)}, u32[]{:S(2)}) async-start(bf16[128,24,128]{2,1,0:T(8,128)(2,1)} %pack.1), calls=%async_computation | async-start | bytes 1572864 | tf_op jit(solution)/shard_map/all_to_all | solution.py:215
  14.3 1.5 %fusion = (bf16[1,128,16,32]{1,0,2,3:T(2,128)(2,1)S(1)}, bf16[1,128,16,32]{1,0,2,3:T(2,128)(2,1)S(1)}) fusion(bf16[2,128,16,32]{1,0,2,3:T(2,128)(2,1)} %bitcast.31), kind=kLoop, calls=%fused_computation.10 | loop fusion | bytes 524288 | tf_op jit(solution)/shard_map/slice | solution.py:228
  15.8 0.1 copy.15
  15.9 0.1 copy.17.wo_ref
  16.0 0.1 copy.14
  16.1 0.1 copy.16.we_ref
  16.3 0.0 copy-done.6
  16.3 0.0 copy-done.7
  16.3 14.1 %all-to-all-done.x_ref = bf16[128,24,128]{2,1,0:T(8,128)(2,1)S(1)} async-done(((bf16[128,24,128]{2,1,0:T(8,128)(2,1)}), bf16[128,24,128]{2,1,0:T(8,128)(2,1)S(1)}, u32[]{:S(2)}, u32[]{:S(2)}) %all-to-all-start) | async-done | bytes 786464 | tf_op jit(solution)/shard_map/all_to_all | solution.py:215
  30.4 0.0 copy-done.1
  30.4 0.0 copy-done.2
  30.4 9.5 %attention.1 = (bf16[128,24,128]{2,1,0:T(8,128)(2,1)}, bf16[384,128]{1,0:T(8,128)(2,1)S(1)}, bf16[384,128]{1,0:T(8,128)(2,1)S(1)}) custom-call(bf16[128,24,128]{2,1,0:T(8,128)(2,1)S(1)} %all-to-all-done.x_ref, bf16[256,256]{1,0:T(8,128)(2,1)S(1)} %copy-done.1, bf16[256,256]{1,0:T(8,128)(2,1)S(1)} %copy-done.2, bf16[256,256]{1,0:T(8,128)(2,1)S(1)} %copy-done.3, ...), custom_call_target="tpu_custom_call" | custom-call | tf_op jit(solution)/shard_map/attention/pallas_call | solution.py:122
  39.9 0.7 collective-permute-start
  40.6 0.1 pad_add_fusion.at_ref
  40.7 4.3 %collective-permute-start.7 = (bf16[384,128]{1,0:T(8,128)(2,1)S(1)}, bf16[384,128]{1,0:T(8,128)(2,1)}, u32[]{:S(2)}, u32[]{:S(2)}) collective-permute-start(bf16[384,128]{1,0:T(8,128)(2,1)S(1)} %get-tuple-element.6), channel_id=1, source_target_pairs={{0,7},{1,23},{2,39},{3,55},{4,71},{5,87},{6,103},{7,119},{8,15},{9... | collective-permute-start | bytes 294920 | tf_op jit(solution)/shard_map/ppermute | solution.py:223
  44.9 1.4 %collective-permute-start.6 = (bf16[384,128]{1,0:T(8,128)(2,1)S(1)}, bf16[384,128]{1,0:T(8,128)(2,1)}, u32[]{:S(2)}, u32[]{:S(2)}) collective-permute-start(bf16[384,128]{1,0:T(8,128)(2,1)S(1)} %get-tuple-element.6), channel_id=1, source_target_pairs={{0,6},{1,22},{2,38},{3,54},{4,70},{5,86},{6,102},{7,118},{8,14},{9... | collective-permute-start | bytes 294920 | tf_op jit(solution)/shard_map/ppermute | solution.py:223
  46.4 0.6 collective-permute-start.5
  47.0 0.8 collective-permute-start.4
  47.8 1.0 broadcast_in_dim.10
  48.8 12.6 %all-to-all-start.2 = ((bf16[8,384,128]{2,1,0:T(8,128)(2,1)}), bf16[8,384,128]{2,1,0:T(8,128)(2,1)S(1)}, u32[]{:S(2)}, u32[]{:S(2)}) async-start(bf16[8,384,128]{2,1,0:T(8,128)(2,1)} %broadcast_in_dim.10), calls=%async_computation.2 | async-start | bytes 1572864 | tf_op jit(solution)/shard_map/all_to_all | solution.py:220
  61.4 0.0 collective-permute-done
  61.4 0.1 collective-permute-start.1
  61.5 13.8 %collective-permute-done.1 = bf16[384,128]{1,0:T(8,128)(2,1)S(1)} collective-permute-done((bf16[384,128]{1,0:T(8,128)(2,1)S(1)}, bf16[384,128]{1,0:T(8,128)(2,1)S(1)}, u32[]{:S(2)}, u32[]{:S(2)}) %collective-permute-start.1) | collective-permute-done | bytes 98336 | tf_op jit(solution)/shard_map/ppermute | solution.py:223
  75.3 0.0 collective-permute-start.2
  75.3 5.5 %collective-permute-done.2 = bf16[384,128]{1,0:T(8,128)(2,1)S(1)} collective-permute-done((bf16[384,128]{1,0:T(8,128)(2,1)S(1)}, bf16[384,128]{1,0:T(8,128)(2,1)S(1)}, u32[]{:S(2)}, u32[]{:S(2)}) %collective-permute-start.2) | collective-permute-done | bytes 98336 | tf_op jit(solution)/shard_map/ppermute | solution.py:223
  80.8 0.0 collective-permute-start.3
  80.8 4.7 %collective-permute-done.3 = bf16[384,128]{1,0:T(8,128)(2,1)S(1)} collective-permute-done((bf16[384,128]{1,0:T(8,128)(2,1)S(1)}, bf16[384,128]{1,0:T(8,128)(2,1)S(1)}, u32[]{:S(2)}, u32[]{:S(2)}) %collective-permute-start.3) | collective-permute-done | bytes 98336 | tf_op jit(solution)/shard_map/ppermute | solution.py:223
  85.4 0.0 all-to-all-done.2
  85.5 13.7 %all-to-all-start.1 = ((bf16[128,24,128]{2,1,0:T(8,128)(2,1)}), bf16[128,24,128]{2,1,0:T(8,128)(2,1)S(1)}, u32[]{:S(2)}, u32[]{:S(2)}) async-start(bf16[128,24,128]{2,1,0:T(8,128)(2,1)} %get-tuple-element.5), calls=%async_computation.1 | async-start | bytes 1572864 | tf_op jit(solution)/shard_map/all_to_all | solution.py:225
  99.2 1.3 collective-permute-start.8
  100.5 0.0 collective-permute-done.4
  100.5 0.9 bitcast_dynamic-update-slice_fusion.3
  101.4 0.0 collective-permute-done.5
  101.4 0.9 bitcast_dynamic-update-slice_fusion.2
  102.3 0.0 collective-permute-done.6
  102.3 0.9 bitcast_dynamic-update-slice_fusion.1
  103.2 0.0 collective-permute-done.7
  103.3 0.9 bitcast_dynamic-update-slice_fusion.l_ref
  104.2 11.0 %all-to-all-done.1.x_ref = bf16[128,24,128]{2,1,0:T(8,128)(2,1)S(1)} async-done(((bf16[128,24,128]{2,1,0:T(8,128)(2,1)}), bf16[128,24,128]{2,1,0:T(8,128)(2,1)S(1)}, u32[]{:S(2)}, u32[]{:S(2)}) %all-to-all-start.1) | async-done | bytes 786464 | tf_op jit(solution)/shard_map/all_to_all | solution.py:225
  115.2 1.0 unpack.1
  116.2 0.0 collective-permute-done.8.other_ref
  116.2 25.2 %pair_grid.1 = bf16[96,192,128]{2,1,0:T(8,128)(2,1)} custom-call(s32[2]{0:T(128)S(1)} %pad_add_fusion.at_ref, bf16[8,384,128]{2,1,0:T(8,128)(2,1)S(1)} %bitcast_dynamic-update-slice_fusion.l_ref, bf16[3072,128]{1,0:T(8,128)(2,1)S(1)} %bitcast.29, bf16[3072,128]{1,0:T(8,128)(2,1)S(1)} %collective-permute-done.8.other_ref, bf16[128,512]{1,0:T(8,128)(2,1)S(1)} %copy.16.we_ref, ...), custom_call_target="tpu_custom_call" | custom-call | tf_op jit(solution)/shard_map/pair_grid/pallas_call | solution.py:175
  (12 shorter events, 0.1 us)
Async XLA Ops:
  0.6 1.1 copy-start
  1.8 14.5 %copy-start.6 = (bf16[256,32]{0,1:T(8,128)(2,1)S(1)}, bf16[256,32]{0,1:T(8,128)(2,1)}, u32[]{:S(2)}) copy-start(bf16[256,32]{0,1:T(8,128)(2,1)} %param.16) | copy-start | bytes 49156
  1.8 14.5 %copy-start.7 = (bf16[256,32]{0,1:T(8,128)(2,1)S(1)}, bf16[256,32]{0,1:T(8,128)(2,1)}, u32[]{:S(2)}) copy-start(bf16[256,32]{0,1:T(8,128)(2,1)} %param.15) | copy-start | bytes 49156
  1.8 28.6 %copy-start.1 = (bf16[256,256]{1,0:T(8,128)(2,1)S(1)}, bf16[256,256]{1,0:T(8,128)(2,1)}, u32[]{:S(2)}) copy-start(bf16[256,256]{1,0:T(8,128)(2,1)} %wq_ref.1) | copy-start | bytes 393220
  1.8 28.6 %copy-start.2 = (bf16[256,256]{1,0:T(8,128)(2,1)S(1)}, bf16[256,256]{1,0:T(8,128)(2,1)}, u32[]{:S(2)}) copy-start(bf16[256,256]{1,0:T(8,128)(2,1)} %wk_ref.1) | copy-start | bytes 393220
  1.8 28.6 %copy-start.3 = (bf16[256,256]{1,0:T(8,128)(2,1)S(1)}, bf16[256,256]{1,0:T(8,128)(2,1)}, u32[]{:S(2)}) copy-start(bf16[256,256]{1,0:T(8,128)(2,1)} %wv_ref.1) | copy-start | bytes 393220
  1.8 28.6 %copy-start.4 = (bf16[256,256]{1,0:T(8,128)(2,1)S(1)}, bf16[256,256]{1,0:T(8,128)(2,1)}, u32[]{:S(2)}) copy-start(bf16[256,256]{1,0:T(8,128)(2,1)} %wg_ref.1) | copy-start | bytes 393220
  1.8 28.6 %copy-start.5 = (bf16[256,256]{1,0:T(8,128)(2,1)S(1)}, bf16[256,256]{1,0:T(8,128)(2,1)}, u32[]{:S(2)}) copy-start(bf16[256,256]{1,0:T(8,128)(2,1)} %wa_ref.1) | copy-start | bytes 393220
  2.8 27.5 %all-to-all-start = ((bf16[128,24,128]{2,1,0:T(8,128)(2,1)}), bf16[128,24,128]{2,1,0:T(8,128)(2,1)S(1)}, u32[]{:S(2)}, u32[]{:S(2)}) async-start(bf16[128,24,128]{2,1,0:T(8,128)(2,1)} %pack.1), calls=%async_computation | async-start | bytes 1572864 | tf_op jit(solution)/shard_map/all_to_all | solution.py:215
  39.9 21.4 %collective-permute-start = (bf16[384,128]{1,0:T(8,128)(2,1)S(1)}, bf16[384,128]{1,0:T(8,128)(2,1)S(1)}, u32[]{:S(2)}, u32[]{:S(2)}) collective-permute-start(bf16[384,128]{1,0:T(8,128)(2,1)S(1)} %get-tuple-element.6), channel_id=1, source_target_pairs={{0,0},{1,16},{2,32},{3,48},{4,64},{5,80},{6,96},{7,112},{8,8},{9,2... | collective-permute-start | bytes 294920 | tf_op jit(solution)/shard_map/ppermute | solution.py:223
  40.7 62.6 %collective-permute-start.7 = (bf16[384,128]{1,0:T(8,128)(2,1)S(1)}, bf16[384,128]{1,0:T(8,128)(2,1)}, u32[]{:S(2)}, u32[]{:S(2)}) collective-permute-start(bf16[384,128]{1,0:T(8,128)(2,1)S(1)} %get-tuple-element.6), channel_id=1, source_target_pairs={{0,7},{1,23},{2,39},{3,55},{4,71},{5,87},{6,103},{7,119},{8,15},{9... | collective-permute-start | bytes 294920 | tf_op jit(solution)/shard_map/ppermute | solution.py:223
  44.9 57.4 %collective-permute-start.6 = (bf16[384,128]{1,0:T(8,128)(2,1)S(1)}, bf16[384,128]{1,0:T(8,128)(2,1)}, u32[]{:S(2)}, u32[]{:S(2)}) collective-permute-start(bf16[384,128]{1,0:T(8,128)(2,1)S(1)} %get-tuple-element.6), channel_id=1, source_target_pairs={{0,6},{1,22},{2,38},{3,54},{4,70},{5,86},{6,102},{7,118},{8,14},{9... | collective-permute-start | bytes 294920 | tf_op jit(solution)/shard_map/ppermute | solution.py:223
  46.4 55.0 %collective-permute-start.5 = (bf16[384,128]{1,0:T(8,128)(2,1)S(1)}, bf16[384,128]{1,0:T(8,128)(2,1)}, u32[]{:S(2)}, u32[]{:S(2)}) collective-permute-start(bf16[384,128]{1,0:T(8,128)(2,1)S(1)} %get-tuple-element.6), channel_id=1, source_target_pairs={{0,5},{1,21},{2,37},{3,53},{4,69},{5,85},{6,101},{7,117},{8,13},{9... | collective-permute-start | bytes 294920 | tf_op jit(solution)/shard_map/ppermute | solution.py:223
  47.0 53.5 %collective-permute-start.4 = (bf16[384,128]{1,0:T(8,128)(2,1)S(1)}, bf16[384,128]{1,0:T(8,128)(2,1)}, u32[]{:S(2)}, u32[]{:S(2)}) collective-permute-start(bf16[384,128]{1,0:T(8,128)(2,1)S(1)} %get-tuple-element.6), channel_id=1, source_target_pairs={{0,4},{1,20},{2,36},{3,52},{4,68},{5,84},{6,100},{7,116},{8,12},{9... | collective-permute-start | bytes 294920 | tf_op jit(solution)/shard_map/ppermute | solution.py:223
  48.8 36.7 %all-to-all-start.2 = ((bf16[8,384,128]{2,1,0:T(8,128)(2,1)}), bf16[8,384,128]{2,1,0:T(8,128)(2,1)S(1)}, u32[]{:S(2)}, u32[]{:S(2)}) async-start(bf16[8,384,128]{2,1,0:T(8,128)(2,1)} %broadcast_in_dim.10), calls=%async_computation.2 | async-start | bytes 1572864 | tf_op jit(solution)/shard_map/all_to_all | solution.py:220
  61.4 13.9 %collective-permute-start.1 = (bf16[384,128]{1,0:T(8,128)(2,1)S(1)}, bf16[384,128]{1,0:T(8,128)(2,1)S(1)}, u32[]{:S(2)}, u32[]{:S(2)}) collective-permute-start(bf16[384,128]{1,0:T(8,128)(2,1)S(1)} %get-tuple-element.6), channel_id=1, source_target_pairs={{0,1},{1,17},{2,33},{3,49},{4,65},{5,81},{6,97},{7,113},{8,9},{9,2... | collective-permute-start | bytes 294920 | tf_op jit(solution)/shard_map/ppermute | solution.py:223
  75.3 5.5 %collective-permute-start.2 = (bf16[384,128]{1,0:T(8,128)(2,1)S(1)}, bf16[384,128]{1,0:T(8,128)(2,1)S(1)}, u32[]{:S(2)}, u32[]{:S(2)}) collective-permute-start(bf16[384,128]{1,0:T(8,128)(2,1)S(1)} %get-tuple-element.6), channel_id=1, source_target_pairs={{0,2},{1,18},{2,34},{3,50},{4,66},{5,82},{6,98},{7,114},{8,10},{9,... | collective-permute-start | bytes 294920 | tf_op jit(solution)/shard_map/ppermute | solution.py:223
  80.8 4.7 %collective-permute-start.3 = (bf16[384,128]{1,0:T(8,128)(2,1)S(1)}, bf16[384,128]{1,0:T(8,128)(2,1)S(1)}, u32[]{:S(2)}, u32[]{:S(2)}) collective-permute-start(bf16[384,128]{1,0:T(8,128)(2,1)S(1)} %get-tuple-element.6), channel_id=1, source_target_pairs={{0,3},{1,19},{2,35},{3,51},{4,67},{5,83},{6,99},{7,115},{8,11},{9,... | collective-permute-start | bytes 294920 | tf_op jit(solution)/shard_map/ppermute | solution.py:223
  85.5 29.7 %all-to-all-start.1 = ((bf16[128,24,128]{2,1,0:T(8,128)(2,1)}), bf16[128,24,128]{2,1,0:T(8,128)(2,1)S(1)}, u32[]{:S(2)}, u32[]{:S(2)}) async-start(bf16[128,24,128]{2,1,0:T(8,128)(2,1)} %get-tuple-element.5), calls=%async_computation.1 | async-start | bytes 1572864 | tf_op jit(solution)/shard_map/all_to_all | solution.py:225
  99.2 17.1 %collective-permute-start.8 = (bf16[3072,128]{1,0:T(8,128)(2,1)S(1)}, bf16[3072,128]{1,0:T(8,128)(2,1)S(1)}, u32[]{:S(2)}, u32[]{:S(2)}) collective-permute-start(bf16[3072,128]{1,0:T(8,128)(2,1)S(1)} %bitcast.28), channel_id=1, source_target_pairs={{0,8},{8,0},{1,9},{9,1},{2,10},{10,2},{3,11},{11,3},{4,12},{12,4},... | collective-permute-start | bytes 2359304 | tf_op jit(solution)/shard_map/ppermute | solution.py:222

commit v2 on v1

v2 whole, which is shorter than its diff:
```python
import functools

import jax
import jax.numpy as jnp
from jax import lax
from jax.experimental import pallas as pl
from jax.experimental.pallas import tpu as pltpu
from jax.sharding import Mesh, PartitionSpec as P

HEADS = 8
HEAD_DIM = 32
OPM = 32
SEQS = 128
WIDTH = 256
LANES = 128
AXES = ("x_hi", "z", "core", "x_lo", "y")
SIZES = (2, 4, 2, 2, 4)
BLK = 12
ROWS = 2 * BLK
PEERS = 8
VMEM = pltpu.CompilerParams(vmem_limit_bytes=24 * 1024 * 1024)
F32 = jnp.float32
BF16 = jnp.bfloat16
NT = (((1,), (1,)), ((), ()))


def block_of(device):
    y, rest = device % 4, device // 4
    x_lo, rest = rest % 2, rest // 2
    core, rest = rest % 2, rest // 2
    z, x_hi = rest % 4, rest // 4
    return (x_lo * 4 + y) * 16 + core * 8 + x_hi * 4 + z


BLOCK_OF = [block_of(d) for d in range(SEQS)]
DEVICE_OF = [BLOCK_OF.index(b) for b in range(SEQS)]


def vmem_spec():
    return pl.BlockSpec(memory_space=pltpu.VMEM)


def normalise(values):
    average = jnp.mean(values, axis=-1, keepdims=True)
    centered = values - average
    variance = jnp.mean(centered * centered, axis=-1, keepdims=True)
    return (centered * lax.rsqrt(variance + 1e-05)).astype(BF16)


def pack_kernel(x_ref, out_ref):
    for group in range(SEQS // 4):
        rows = x_ref[group * 48 : group * 48 + 48, :].astype(F32)
        for part in range(4):
            piece = rows[part * BLK : part * BLK + BLK]
            both = jnp.concatenate([piece[:, :LANES], piece[:, LANES:]], axis=0)
            out_ref[DEVICE_OF[group * 4 + part]] = both.astype(BF16)


def unpack_kernel(x_ref, out_ref):
    for group in range(SEQS // 4):
        pieces = [x_ref[DEVICE_OF[group * 4 + part]].astype(F32) for part in range(4)]
        left = jnp.concatenate([piece[:BLK] for piece in pieces], axis=0)
        right = jnp.concatenate([piece[BLK:] for piece in pieces], axis=0)
        out_ref[group * 48 : group * 48 + 48, :] = jnp.concatenate([left, right], axis=1).astype(BF16)


def attention_kernel(
    x_ref, w_ref, wlr_ref, u_ref, lt_ref, rt_ref,
    flat, normed, query, key, value, gate, attended, update,
):
    flat[...] = x_ref[...].astype(F32).reshape(SEQS * ROWS, LANES)

    def residue(r):
        return jnp.concatenate(
            [flat[pl.ds(r, SEQS, stride=ROWS), :], flat[pl.ds(BLK + r, SEQS, stride=ROWS), :]], axis=1
        )

    def span(r):
        return pl.ds(r * SEQS, SEQS)

    for r in range(BLK):
        normed[span(r), :] = normalise(residue(r))
    rows = normed[...]
    query[...] = jnp.dot(rows, w_ref[0], preferred_element_type=F32).astype(BF16)
    key[...] = jnp.dot(rows, w_ref[1], preferred_element_type=F32).astype(BF16)
    value[...] = jnp.dot(rows, w_ref[2], preferred_element_type=F32).astype(BF16)
    gate[...] = jax.nn.sigmoid(jnp.dot(rows, w_ref[3], preferred_element_type=F32))

    lane = lax.broadcasted_iota(jnp.int32, (SEQS, WIDTH), 1) // HEAD_DIM
    own = [(lane == h) for h in range(HEADS)]
    zero = jnp.zeros((SEQS, WIDTH), BF16)
    ones = jnp.concatenate([jnp.where(m, 1.0, 0.0).astype(BF16) for m in own], axis=0)

    for r in range(BLK):
        at = span(r)
        q, k, v = query[at, :], key[at, :], value[at, :]
        k_heads = jnp.concatenate([jnp.where(m, k, zero) for m in own], axis=0)
        v_heads = jnp.concatenate([jnp.where(m, v, zero) for m in own], axis=0)
        scores = lax.dot_general(q, k_heads, NT, preferred_element_type=F32) * HEAD_DIM ** (-0.5)
        weighted = jnp.exp(scores).astype(BF16)
        numerator = jnp.dot(weighted, v_heads, preferred_element_type=F32)
        denominator = jnp.dot(weighted, ones, preferred_element_type=F32)
        attended[at, :] = (gate[at, :] * numerator / denominator).astype(BF16)

    update[...] = jnp.dot(attended[...], w_ref[4], preferred_element_type=F32)
    for r in range(BLK):
        updated = (residue(r) + update[span(r), :]).astype(BF16).astype(F32)
        flat[pl.ds(r, SEQS, stride=ROWS), :] = updated[:, :LANES]
        flat[pl.ds(BLK + r, SEQS, stride=ROWS), :] = updated[:, LANES:]
        normed[span(r), :] = normalise(updated)
    sides = lax.dot_general(wlr_ref[...], normed[...], NT, preferred_element_type=F32).astype(BF16)
    for r in range(BLK):
        lt_ref[r * OPM : (r + 1) * OPM, :] = sides[:OPM, r * SEQS : (r + 1) * SEQS]
        for copy in range(PEERS):
            rt_ref[copy, r * OPM : (r + 1) * OPM, :] = sides[OPM:, r * SEQS : (r + 1) * SEQS]
    u_ref[...] = flat[...].reshape(SEQS, ROWS, LANES).astype(BF16)


def attention(x, weights, wlr):
    tall = SEQS * BLK
    return pl.pallas_call(
        attention_kernel,
        out_shape=(
            jax.ShapeDtypeStruct((SEQS, ROWS, LANES), BF16),
            jax.ShapeDtypeStruct((BLK * OPM, SEQS), BF16),
            jax.ShapeDtypeStruct((PEERS, BLK * OPM, SEQS), BF16),
        ),
        in_specs=[vmem_spec()] * 3,
        out_specs=(vmem_spec(),) * 3,
        scratch_shapes=[
            pltpu.VMEM((SEQS * ROWS, LANES), F32),
            pltpu.VMEM((tall, WIDTH), BF16),
            pltpu.VMEM((tall, WIDTH), BF16),
            pltpu.VMEM((tall, WIDTH), BF16),
            pltpu.VMEM((tall, WIDTH), BF16),
            pltpu.VMEM((tall, WIDTH), F32),
            pltpu.VMEM((tall, WIDTH), BF16),
            pltpu.VMEM((tall, WIDTH), F32),
        ],
        compiler_params=VMEM,
        name="attention",
    )(x, weights, wlr)


COLS = 192
HALF = PEERS * BLK * OPM


def pair_rows(left, right, we_ref, wo_ref, out_ref, outer):
    for p in range(OPM // 2):
        product = jnp.dot(left, right[p], preferred_element_type=F32).astype(BF16)
        for i in range(BLK):
            outer[i, p * OPM : (p + 1) * OPM, :] = product[i * OPM : (i + 1) * OPM]
    even_w, odd_w = we_ref[...], wo_ref[...]
    for i in range(BLK):
        even = jnp.dot(even_w, outer[i, :, :256], preferred_element_type=F32)
        odd = jnp.dot(odd_w, outer[i, :, 128:], preferred_element_type=F32)
        total = (even.T[:COLS] + odd.T[64:]) * (1.0 / SEQS)
        out_ref[i] = total.astype(BF16)


def first_pair_kernel(at_ref, l_ref, own_ref, other_ref, we_ref, wo_ref, out_ref, right, flat, outer):
    first = pl.multiple_of(at_ref[2] * HALF, HALF)
    flat[pl.ds(first, HALF), :] = own_ref[...].astype(F32)
    flat[pl.ds(pl.multiple_of(HALF - first, HALF), HALF), :] = other_ref[...].astype(F32)
    for p in range(OPM // 2):
        even = flat[pl.ds(2 * p, COLS, stride=OPM), :]
        odd = flat[pl.ds(2 * p + 1, COLS, stride=OPM), :]
        right[p] = jnp.concatenate([even, odd], axis=0).T.astype(BF16)
    pair_rows(l_ref[0], right, we_ref, wo_ref, out_ref, outer)


def next_pair_kernel(at_ref, l_ref, right, we_ref, wo_ref, before_ref, out_ref, outer):
    pair_rows(l_ref[0], right, we_ref, wo_ref, out_ref, outer)


def whole(*shape):
    return pl.BlockSpec(shape, lambda k, at: (0,) * len(shape))


def pair_call(kernel, where, steps, operands, in_specs, extra_shapes, extra_specs, scratch, aliases):
    flops = 2 * steps * BLK * COLS * OPM * OPM * (SEQS + 128)
    return pl.pallas_call(
        kernel,
        out_shape=[jax.ShapeDtypeStruct((PEERS * BLK, COLS, 128), BF16)] + extra_shapes,
        grid_spec=pltpu.PrefetchScalarGridSpec(
            num_scalar_prefetch=1,
            grid=(steps,),
            in_specs=[pl.BlockSpec((1, BLK * OPM, SEQS), lambda k, at: (k, 0, 0))] + in_specs,
            out_specs=[pl.BlockSpec((BLK, COLS, 128), lambda k, at: (where(k, at[0], at[1]), 0, 0))] + extra_specs,
            scratch_shapes=scratch + [pltpu.VMEM((BLK, 512, 384), BF16)],
        ),
        input_output_aliases=aliases,
        cost_estimate=pl.CostEstimate(flops=flops, bytes_accessed=8 * 1024 * 1024, transcendentals=0),
        compiler_params=VMEM,
        name="pair_grid",
    )(*operands)


def pair_first(place, left, own, other, weights):
    right = (OPM // 2, SEQS, 384)
    return pair_call(
        first_pair_kernel, lambda k, x_lo, y: x_lo * 4 + y, 1, (place, left, own, other) + weights,
        [whole(HALF, SEQS)] * 2 + [vmem_spec()] * 2,
        [jax.ShapeDtypeStruct(right, BF16)], [vmem_spec()], [pltpu.VMEM((2 * HALF, SEQS), F32)], {},
    )


def pair_next(place, left, right, weights, before, where):
    return pair_call(
        next_pair_kernel, where, left.shape[0], (place, left, right) + weights + (before,),
        [vmem_spec()] * 3 + [pl.BlockSpec(memory_space=pl.ANY)],
        [], [], [], {5: 0},
    )[0]


def crossed():
    pairs = []
    for d in range(SEQS):
        y, x_lo, core, z, x_hi = d % 4, d // 4 % 2, d // 8 % 2, d // 16 % 4, d // 64
        pairs.append((d, ((x_lo * 4 + y) * 2 + core) * 8 + x_hi * 4 + z))
    return pairs


def flipped(size, bit):
    return [(i, i ^ bit) for i in range(size)]


def body(alignment, w_query, w_key, w_value, w_gate, w_attend, w_left, w_right, w_pair):
    one = jax.ShapeDtypeStruct((SEQS, ROWS, LANES), BF16)
    packed = pl.pallas_call(
        pack_kernel, out_shape=one, in_specs=[vmem_spec()], out_specs=vmem_spec(),
        compiler_params=VMEM, name="pack",
    )(alignment[0])
    blocks = lax.all_to_all(packed, AXES, split_axis=0, concat_axis=0, tiled=True)
    w_sides = jnp.concatenate([w_left, w_right], axis=1).T
    w_pairs = w_pair.reshape(OPM, OPM // 2, 2, 128).transpose(2, 3, 1, 0).reshape(2, 128, 512)
    place = jnp.stack([lax.axis_index(a) for a in ("x_lo", "y", "core")]).astype(jnp.int32)
    blocks, w_even, w_odd, place = lax.optimization_barrier((blocks, w_pairs[0], w_pairs[1], place))
    weights = (w_even, w_odd)
    updated, left, right = attention(blocks, jnp.stack([w_query, w_key, w_value, w_gate, w_attend]), w_sides)

    own = lax.all_to_all(right, ("x_hi", "z"), split_axis=0, concat_axis=0, tiled=True)
    near = lax.ppermute(left, AXES, crossed())[None]
    near, own = lax.optimization_barrier((near, own))
    own = own.reshape(HALF, SEQS)
    other = lax.ppermute(own, "core", flipped(2, 1))
    returned = lax.all_to_all(updated, AXES, split_axis=0, concat_axis=0, tiled=True)
    second = lax.ppermute(near, "y", flipped(4, 2))
    grid, rights = pair_first(place, near, own, other, weights)

    second, grid = lax.optimization_barrier((second, grid))
    two = jnp.concatenate([near, second])
    third = lax.ppermute(two, "y", flipped(4, 1))
    fourth = lax.ppermute(two, "x_lo", flipped(2, 1))
    grid = pair_next(place, second, rights, weights, grid, lambda k, x_lo, y: x_lo * 4 + (y ^ 2))
    last = lax.ppermute(third, "x_lo", flipped(2, 1))
    grid = pair_next(place, third, rights, weights, grid, lambda k, x_lo, y: x_lo * 4 + (y ^ 1 ^ (k << 1)))
    grid = pair_next(place, fourth, rights, weights, grid, lambda k, x_lo, y: (1 - x_lo) * 4 + (y ^ (k << 1)))
    pair_update = pair_next(
        place, last, rights, weights, grid, lambda k, x_lo, y: (1 - x_lo) * 4 + (y ^ 1 ^ (k << 1))
    )
    returned, pair_update = lax.optimization_barrier((returned, pair_update))
    alignment_out = pl.pallas_call(
        unpack_kernel, out_shape=jax.ShapeDtypeStruct(alignment.shape[1:], BF16),
        in_specs=[vmem_spec()], out_specs=vmem_spec(), compiler_params=VMEM, name="unpack",
    )(returned)
    return (alignment_out[None], pair_update)


def solution(mesh):
    fine = Mesh(mesh.devices.reshape(SIZES), AXES)
    placed = (P(AXES, None, None),) + (P(),) * 8
    return jax.shard_map(
        body,
        mesh=fine,
        in_specs=placed,
        out_specs=(P(AXES, None, None), P(AXES[:3], AXES[3:], None)),
        check_vma=False,
    )
```

time: 142 us -> 105 us (0.74)
  waiting for transfers between devices: 49.1 us -> 27.3 us
  starting transfers between devices: 47 us -> 34 us
  local copies, waits for them, and re-layouts: 7.7 us -> 5.12 us
    ppermute x9 -> x6, waiting for transfers between devices: 23.9 us -> 2.89 us  [the longest x1 2.87 us: body(): fourth = lax.ppermute(two, 'x_lo', flipped(2, 1))]
    all_to_all x1, waiting for transfers between devices: 11 us -> 0.01 us  [body(): lax.all_to_all(updated, AXES, split_axis=0, concat_axis=0, tiled=True)]
    all_to_all x1, waiting for transfers between devices: 0.01 us -> 10.3 us  [body(): lax.all_to_all(right, ('x_hi', 'z'), split_axis=0, concat_axis=0, tiled=T...]
    all_to_all x1, starting transfers between devices: 12.6 us -> 3.55 us  [body(): lax.all_to_all(right, ('x_hi', 'z'), split_axis=0, concat_axis=0, tiled=T...]
    all_to_all x1, starting transfers between devices: 13.7 us -> 10.2 us  [body(): lax.all_to_all(updated, AXES, split_axis=0, concat_axis=0, tiled=True)]
    pallas_call x1 -> x5, Pallas kernels: 25.2 us -> 27.2 us  [pair_call(): pl.pallas_call(kernel, out_shape=[jax.ShapeDtypeStruct((PEERS * BLK, COLS...]
    unnamed x23 -> x25, local copies, waits for them, and re-layouts: 3.92 us -> 3.21 us
    ppermute x9 -> x6, starting transfers between devices: 9.2 us -> 8.79 us  [the longest x1 3.29 us: body(): other = lax.ppermute(own, 'core', flipped(2, 1))]
  transfers between devices with their start and end apart: 12 -> 9, of which waited for: 5 -> 3; matrix products, arithmetic and copies ran while one was open for 5% -> 2% of each run, Pallas kernels for 1% -> 26%
where the time goes in v2:
time: 105 us
  Pallas kernels  37.4 us (36%)
  starting transfers between devices  34 us (32%)
  waiting for transfers between devices  27.3 us (26%)
  local copies, waits for them, and re-layouts  5.12 us (5%)
    pallas_call x5, Pallas kernels, pair_call(): pl.pallas_call(kernel, out_shape=[jax.ShapeDtypeStruct((PEERS * BLK, COLS...  27.2 us
    all_to_all x1, waiting for transfers between devices, body(): lax.all_to_all(packed, AXES, split_axis=0, concat_axis=0, tiled=True)  14.1 us
    all_to_all x1, starting transfers between devices, body(): lax.all_to_all(packed, AXES, split_axis=0, concat_axis=0, tiled=True)  11.5 us
    all_to_all x1, waiting for transfers between devices, body(): lax.all_to_all(right, ('x_hi', 'z'), split_axis=0, concat_axis=0, tiled=T...  10.3 us
    all_to_all x1, starting transfers between devices, body(): lax.all_to_all(updated, AXES, split_axis=0, concat_axis=0, tiled=True)  10.2 us
    pallas_call x1, Pallas kernels, attention(): pl.pallas_call(attention_kernel, out_shape=(jax.ShapeDtypeStruct((SEQS, R...  8.17 us
    all_to_all x1, starting transfers between devices, body(): lax.all_to_all(right, ('x_hi', 'z'), split_axis=0, concat_axis=0, tiled=T...  3.55 us
    ppermute x1, starting transfers between devices, body(): other = lax.ppermute(own, 'core', flipped(2, 1))  3.29 us
  transfers between devices with their start and end apart: 9, of which 3 were waited for; matrix products, arithmetic and copies ran while one was open for 2% of the time, Pallas kernels for 26%

profile of v2, /device:TPU:1, one launch (start us, length us, event | category | flops | bytes accessed | tf_op | source)
XLA Modules:
  0.0 104.8 jit_solution(16572565203653232189)
XLA Ops:
  0.6 0.0 copy-start
  0.6 1.1 %copy-done = bf16[1,1536,256]{2,1,0:T(8,128)(2,1)S(1)} copy-done((bf16[1,1536,256]{2,1,0:T(8,128)(2,1)S(1)}, bf16[1,1536,256]{2,1,0:T(8,128)(2,1)}, u32[]{:S(2)}) %copy-start) | copy-done | bytes 786456
  1.8 0.0 copy-start.3
  1.8 0.0 copy-start.5
  1.8 0.0 copy-start.6
  1.8 0.0 copy-start.7
  1.8 1.0 pack.1
  2.8 11.5 %all-to-all-start = ((bf16[128,24,128]{2,1,0:T(8,128)(2,1)}), bf16[128,24,128]{2,1,0:T(8,128)(2,1)S(1)}, u32[]{:S(2)}, u32[]{:S(2)}) async-start(bf16[128,24,128]{2,1,0:T(8,128)(2,1)} %pack.1), calls=%async_computation | async-start | bytes 1572864 | tf_op jit(solution)/shard_map/all_to_all | solution.py:235
  14.3 1.5 %fusion = (bf16[1,128,16,32]{1,0,2,3:T(2,128)(2,1)S(1)}, bf16[1,128,16,32]{1,0,2,3:T(2,128)(2,1)S(1)}) fusion(bf16[2,128,16,32]{1,0,2,3:T(2,128)(2,1)} %bitcast.30), kind=kLoop, calls=%fused_computation.9 | loop fusion | bytes 524288 | tf_op jit(solution)/shard_map/slice | solution.py:239
  15.8 0.1 copy.27
  15.9 0.1 copy.26
  16.0 0.0 copy-done.3
  16.1 0.0 copy-done.8
  16.1 0.0 copy-done.9
  16.1 0.0 copy-done.4
  16.1 0.1 pad_add_fusion.at_ref
  16.2 0.0 copy-done.5
  16.2 0.0 copy-done.6
  16.2 0.0 copy-done.7
  16.3 14.1 %all-to-all-done.x_ref = bf16[128,24,128]{2,1,0:T(8,128)(2,1)S(1)} async-done(((bf16[128,24,128]{2,1,0:T(8,128)(2,1)}), bf16[128,24,128]{2,1,0:T(8,128)(2,1)S(1)}, u32[]{:S(2)}, u32[]{:S(2)}) %all-to-all-start) | async-done | bytes 786464 | tf_op jit(solution)/shard_map/all_to_all | solution.py:235
  30.4 8.2 %attention.1 = (bf16[128,24,128]{2,1,0:T(8,128)(2,1)}, bf16[384,128]{1,0:T(8,128)(2,1)S(1)}, bf16[8,384,128]{2,1,0:T(8,128)(2,1)}) custom-call(bf16[128,24,128]{2,1,0:T(8,128)(2,1)S(1)} %all-to-all-done.x_ref, bf16[5,256,256]{2,1,0:T(8,128)(2,1)S(1)} %bitcast_dynamic-update-slice_fusion.w_ref, bf16[64,256]{1,0:T(8,128)(2,1)S(1)} %maximum_bitcast_fusion.wlr_ref), custom_call_target="tpu_custom_call" | custom-call | tf_op jit(solution)/shard_map/attention/pallas_call | solution.py:121
  38.5 3.5 %all-to-all-start.2 = ((bf16[8,384,128]{2,1,0:T(8,128)(2,1)}), bf16[8,384,128]{2,1,0:T(8,128)(2,1)S(1)}, u32[]{:S(2)}, u32[]{:S(2)}) async-start(bf16[8,384,128]{2,1,0:T(8,128)(2,1)} %get-tuple-element.21), calls=%async_computation.2 | async-start | bytes 1572864 | tf_op jit(solution)/shard_map/all_to_all | solution.py:243
  42.1 0.7 collective-permute-start
  42.8 0.0 collective-permute-done
  42.8 10.3 %all-to-all-done.2 = bf16[8,384,128]{2,1,0:T(8,128)(2,1)S(1)} async-done(((bf16[8,384,128]{2,1,0:T(8,128)(2,1)}), bf16[8,384,128]{2,1,0:T(8,128)(2,1)S(1)}, u32[]{:S(2)}, u32[]{:S(2)}) %all-to-all-start.2) | async-done | bytes 786464 | tf_op jit(solution)/shard_map/all_to_all | solution.py:243
  53.1 3.3 %collective-permute-start.2 = (bf16[3072,128]{1,0:T(8,128)(2,1)S(1)}, bf16[3072,128]{1,0:T(8,128)(2,1)S(1)}, u32[]{:S(2)}, u32[]{:S(2)}) collective-permute-start(bf16[3072,128]{1,0:T(8,128)(2,1)S(1)} %bitcast.25), channel_id=1, source_target_pairs={{0,8},{8,0},{1,9},{9,1},{2,10},{10,2},{3,11},{11,3},{4,12},{12,4},... | collective-permute-start | bytes 2359304 | tf_op jit(solution)/shard_map/ppermute | solution.py:247
  56.4 0.1 copy.28.we_ref
  56.5 0.1 copy.29.wo_ref
  56.6 2.8 %collective-permute-start.1 = (bf16[1,384,128]{2,1,0:T(8,128)(2,1)S(1)}, bf16[1,384,128]{2,1,0:T(8,128)(2,1)S(1)}, u32[]{:S(2)}, u32[]{:S(2)}) collective-permute-start(bf16[1,384,128]{2,1,0:T(8,128)(2,1)S(1)} %bitcast.27), channel_id=1, source_target_pairs={{0,2},{1,3},{2,0},{3,1},{4,6},{5,7},{6,4},{7,5},{8,10},{9,11},{10,... | collective-permute-start | bytes 294920 | tf_op jit(solution)/shard_map/ppermute | solution.py:249
  59.5 0.0 collective-permute-done.2.other_ref
  59.5 0.0 copy-start.1
  59.5 0.9 copy-done.1
  60.3 1.1 %copy-done.2 = bf16[3072,128]{1,0:T(8,128)(2,1)S(1)} copy-done((bf16[3072,128]{1,0:T(8,128)(2,1)S(1)}, bf16[3072,128]{1,0:T(8,128)(2,1)}, u32[]{:S(2)}) %copy-start.2) | copy-done | bytes 786456
  61.5 5.4 %pair_grid.5 = (bf16[96,192,128]{2,1,0:T(8,128)(2,1)}, bf16[16,128,384]{2,1,0:T(8,128)(2,1)S(1)}) custom-call(s32[3]{0:T(128)S(1)} %pad_add_fusion.at_ref, bf16[1,384,128]{2,1,0:T(8,128)(2,1)S(1)} %bitcast.29, bf16[3072,128]{1,0:T(8,128)(2,1)S(1)} %bitcast.26, bf16[3072,128]{1,0:T(8,128)(2,1)S(1)} %copy-done.2, bf16[128,512]{1,0:T(8,128)(2,1)S(1)} %copy.28.we_ref, ...), custom_call_target="tpu_custom_call" | custom-call | flops 1207959552 | bytes 8388608 | tf_op jit(solution)/shard_map/pair_grid/pallas_call | solution.py:183
  66.8 0.0 collective-permute-done.1.l_ref
  66.9 0.5 collective-permute-start.3
  67.3 10.2 %all-to-all-start.1 = ((bf16[128,24,128]{2,1,0:T(8,128)(2,1)}), bf16[128,24,128]{2,1,0:T(8,128)(2,1)S(1)}, u32[]{:S(2)}, u32[]{:S(2)}) async-start(bf16[128,24,128]{2,1,0:T(8,128)(2,1)} %get-tuple-element.18), calls=%async_computation.1 | async-start | bytes 1572864 | tf_op jit(solution)/shard_map/all_to_all | solution.py:248
  77.5 1.5 %collective-permute-start.5 = (bf16[2,384,128]{2,1,0:T(8,128)(2,1)S(1)}, bf16[2,384,128]{2,1,0:T(8,128)(2,1)S(1)}, u32[]{:S(2)}, u32[]{:S(2)}) collective-permute-start(bf16[2,384,128]{2,1,0:T(8,128)(2,1)S(1)} %constant_dynamic-update-slice_fusion), channel_id=1, source_target_pairs={{0,4},{4,0},{1,5},{5,1},{2,6},{6,2},{3,7},{7,3},{8,12},{12,8},{9,1... | collective-permute-start | bytes 589832 | tf_op jit(solution)/shard_map/ppermute | solution.py:255
  79.0 3.7 %pair_grid.6.before_ref = bf16[96,192,128]{2,1,0:T(8,128)(2,1)} custom-call(s32[3]{0:T(128)S(1)} %pad_add_fusion.at_ref, bf16[1,384,128]{2,1,0:T(8,128)(2,1)S(1)} %collective-permute-done.1.l_ref, bf16[16,128,384]{2,1,0:T(8,128)(2,1)S(1)} %get-tuple-element.28.right, bf16[128,512]{1,0:T(8,128)(2,1)S(1)} %copy.28.we_ref, ...), custom_call_target="tpu_custom_call", output_to_operand_aliasing={{}: (5, {})} | custom-call | flops 1207959552 | bytes 8388608 | tf_op jit(solution)/shard_map/pair_grid/pallas_call | solution.py:183
  82.7 0.0 collective-permute-done.3.l_ref
  82.7 0.1 collective-permute-start.4
  82.7 6.0 %pair_grid.7.before_ref = bf16[96,192,128]{2,1,0:T(8,128)(2,1)} custom-call(s32[3]{0:T(128)S(1)} %pad_add_fusion.at_ref, bf16[2,384,128]{2,1,0:T(8,128)(2,1)S(1)} %collective-permute-done.3.l_ref, bf16[16,128,384]{2,1,0:T(8,128)(2,1)S(1)} %get-tuple-element.28.right, bf16[128,512]{1,0:T(8,128)(2,1)S(1)} %copy.28.we_ref, ...), custom_call_target="tpu_custom_call", output_to_operand_aliasing={{}: (5, {})} | custom-call | flops 2415919104 | bytes 8388608 | tf_op jit(solution)/shard_map/pair_grid/pallas_call | solution.py:183
  88.8 2.9 %collective-permute-done.5.l_ref = bf16[2,384,128]{2,1,0:T(8,128)(2,1)S(1)} collective-permute-done((bf16[2,384,128]{2,1,0:T(8,128)(2,1)S(1)}, bf16[2,384,128]{2,1,0:T(8,128)(2,1)S(1)}, u32[]{:S(2)}, u32[]{:S(2)}) %collective-permute-start.5) | collective-permute-done | bytes 196640 | tf_op jit(solution)/shard_map/ppermute | solution.py:255
  91.6 6.1 %pair_grid.8.before_ref = bf16[96,192,128]{2,1,0:T(8,128)(2,1)} custom-call(s32[3]{0:T(128)S(1)} %pad_add_fusion.at_ref, bf16[2,384,128]{2,1,0:T(8,128)(2,1)S(1)} %collective-permute-done.5.l_ref, bf16[16,128,384]{2,1,0:T(8,128)(2,1)S(1)} %get-tuple-element.28.right, bf16[128,512]{1,0:T(8,128)(2,1)S(1)} %copy.28.we_ref, ...), custom_call_target="tpu_custom_call", output_to_operand_aliasing={{}: (5, {})} | custom-call | flops 2415919104 | bytes 8388608 | tf_op jit(solution)/shard_map/pair_grid/pallas_call | solution.py:183
  97.7 0.0 collective-permute-done.4.l_ref
  97.7 6.1 %pair_grid.9 = bf16[96,192,128]{2,1,0:T(8,128)(2,1)} custom-call(s32[3]{0:T(128)S(1)} %pad_add_fusion.at_ref, bf16[2,384,128]{2,1,0:T(8,128)(2,1)S(1)} %collective-permute-done.4.l_ref, bf16[16,128,384]{2,1,0:T(8,128)(2,1)S(1)} %get-tuple-element.28.right, bf16[128,512]{1,0:T(8,128)(2,1)S(1)} %copy.28.we_ref, ...), custom_call_target="tpu_custom_call", output_to_operand_aliasing={{}: (5, {})} | custom-call | flops 2415919104 | bytes 8388608 | tf_op jit(solution)/shard_map/pair_grid/pallas_call | solution.py:183
  103.7 0.0 all-to-all-done.1.x_ref
  103.8 1.0 unpack.1
  (12 shorter events, 0.1 us)
Async XLA Ops:
  0.6 1.1 %copy-start = (bf16[1,1536,256]{2,1,0:T(8,128)(2,1)S(1)}, bf16[1,1536,256]{2,1,0:T(8,128)(2,1)}, u32[]{:S(2)}) copy-start(bf16[1,1536,256]{2,1,0:T(8,128)(2,1)} %param.9) | copy-start | bytes 2359300
  1.8 14.3 %copy-start.3 = (bf16[256,256]{1,0:T(8,128)(2,1)S(1)}, bf16[256,256]{1,0:T(8,128)(2,1)}, u32[]{:S(2)}) copy-start(bf16[256,256]{1,0:T(8,128)(2,1)} %param.10) | copy-start | bytes 393220
  1.8 14.3 %copy-start.8 = (bf16[256,32]{0,1:T(8,128)(2,1)S(1)}, bf16[256,32]{0,1:T(8,128)(2,1)}, u32[]{:S(2)}) copy-start(bf16[256,32]{0,1:T(8,128)(2,1)} %param.16) | copy-start | bytes 49156
  1.8 14.3 %copy-start.9 = (bf16[256,32]{0,1:T(8,128)(2,1)S(1)}, bf16[256,32]{0,1:T(8,128)(2,1)}, u32[]{:S(2)}) copy-start(bf16[256,32]{0,1:T(8,128)(2,1)} %param.15) | copy-start | bytes 49156
  1.8 14.3 %copy-start.4 = (bf16[256,256]{1,0:T(8,128)(2,1)S(1)}, bf16[256,256]{1,0:T(8,128)(2,1)}, u32[]{:S(2)}) copy-start(bf16[256,256]{1,0:T(8,128)(2,1)} %param.11) | copy-start | bytes 393220
  1.8 14.4 %copy-start.5 = (bf16[256,256]{1,0:T(8,128)(2,1)S(1)}, bf16[256,256]{1,0:T(8,128)(2,1)}, u32[]{:S(2)}) copy-start(bf16[256,256]{1,0:T(8,128)(2,1)} %param.12) | copy-start | bytes 393220
  1.8 14.4 %copy-start.6 = (bf16[256,256]{1,0:T(8,128)(2,1)S(1)}, bf16[256,256]{1,0:T(8,128)(2,1)}, u32[]{:S(2)}) copy-start(bf16[256,256]{1,0:T(8,128)(2,1)} %param.13) | copy-start | bytes 393220
  1.8 14.4 %copy-start.7 = (bf16[256,256]{1,0:T(8,128)(2,1)S(1)}, bf16[256,256]{1,0:T(8,128)(2,1)}, u32[]{:S(2)}) copy-start(bf16[256,256]{1,0:T(8,128)(2,1)} %param.14) | copy-start | bytes 393220
  2.8 27.5 %all-to-all-start = ((bf16[128,24,128]{2,1,0:T(8,128)(2,1)}), bf16[128,24,128]{2,1,0:T(8,128)(2,1)S(1)}, u32[]{:S(2)}, u32[]{:S(2)}) async-start(bf16[128,24,128]{2,1,0:T(8,128)(2,1)} %pack.1), calls=%async_computation | async-start | bytes 1572864 | tf_op jit(solution)/shard_map/all_to_all | solution.py:235
  38.5 14.5 %all-to-all-start.2 = ((bf16[8,384,128]{2,1,0:T(8,128)(2,1)}), bf16[8,384,128]{2,1,0:T(8,128)(2,1)S(1)}, u32[]{:S(2)}, u32[]{:S(2)}) async-start(bf16[8,384,128]{2,1,0:T(8,128)(2,1)} %get-tuple-element.21), calls=%async_computation.2 | async-start | bytes 1572864 | tf_op jit(solution)/shard_map/all_to_all | solution.py:243
  42.1 0.7 collective-permute-start
  53.1 6.4 %collective-permute-start.2 = (bf16[3072,128]{1,0:T(8,128)(2,1)S(1)}, bf16[3072,128]{1,0:T(8,128)(2,1)S(1)}, u32[]{:S(2)}, u32[]{:S(2)}) collective-permute-start(bf16[3072,128]{1,0:T(8,128)(2,1)S(1)} %bitcast.25), channel_id=1, source_target_pairs={{0,8},{8,0},{1,9},{9,1},{2,10},{10,2},{3,11},{11,3},{4,12},{12,4},... | collective-permute-start | bytes 2359304 | tf_op jit(solution)/shard_map/ppermute | solution.py:247
  56.6 10.2 %collective-permute-start.1 = (bf16[1,384,128]{2,1,0:T(8,128)(2,1)S(1)}, bf16[1,384,128]{2,1,0:T(8,128)(2,1)S(1)}, u32[]{:S(2)}, u32[]{:S(2)}) collective-permute-start(bf16[1,384,128]{2,1,0:T(8,128)(2,1)S(1)} %bitcast.27), channel_id=1, source_target_pairs={{0,2},{1,3},{2,0},{3,1},{4,6},{5,7},{6,4},{7,5},{8,10},{9,11},{10,... | collective-permute-start | bytes 294920 | tf_op jit(solution)/shard_map/ppermute | solution.py:249
  59.5 0.9 copy-start.1
  60.3 1.1 %copy-start.2 = (bf16[3072,128]{1,0:T(8,128)(2,1)S(1)}, bf16[3072,128]{1,0:T(8,128)(2,1)}, u32[]{:S(2)}) copy-start(bf16[3072,128]{1,0:T(8,128)(2,1)} %copy-done.1) | copy-start | bytes 2359300
  66.9 15.8 %collective-permute-start.3 = (bf16[2,384,128]{2,1,0:T(8,128)(2,1)S(1)}, bf16[2,384,128]{2,1,0:T(8,128)(2,1)S(1)}, u32[]{:S(2)}, u32[]{:S(2)}) collective-permute-start(bf16[2,384,128]{2,1,0:T(8,128)(2,1)S(1)} %constant_dynamic-update-slice_fusion), channel_id=1, source_target_pairs={{0,1},{1,0},{2,3},{3,2},{4,5},{5,4},{6,7},{7,6},{8,9},{9,8},{10,11... | collective-permute-start | bytes 589832 | tf_op jit(solution)/shard_map/ppermute | solution.py:254
  67.3 36.4 %all-to-all-start.1 = ((bf16[128,24,128]{2,1,0:T(8,128)(2,1)}), bf16[128,24,128]{2,1,0:T(8,128)(2,1)S(1)}, u32[]{:S(2)}, u32[]{:S(2)}) async-start(bf16[128,24,128]{2,1,0:T(8,128)(2,1)} %get-tuple-element.18), calls=%async_computation.1 | async-start | bytes 1572864 | tf_op jit(solution)/shard_map/all_to_all | solution.py:248
  77.5 14.1 %collective-permute-start.5 = (bf16[2,384,128]{2,1,0:T(8,128)(2,1)S(1)}, bf16[2,384,128]{2,1,0:T(8,128)(2,1)S(1)}, u32[]{:S(2)}, u32[]{:S(2)}) collective-permute-start(bf16[2,384,128]{2,1,0:T(8,128)(2,1)S(1)} %constant_dynamic-update-slice_fusion), channel_id=1, source_target_pairs={{0,4},{4,0},{1,5},{5,1},{2,6},{6,2},{3,7},{7,3},{8,12},{12,8},{9,1... | collective-permute-start | bytes 589832 | tf_op jit(solution)/shard_map/ppermute | solution.py:255
  82.7 15.0 %collective-permute-start.4 = (bf16[2,384,128]{2,1,0:T(8,128)(2,1)S(1)}, bf16[2,384,128]{2,1,0:T(8,128)(2,1)S(1)}, u32[]{:S(2)}, u32[]{:S(2)}) collective-permute-start(bf16[2,384,128]{2,1,0:T(8,128)(2,1)S(1)} %collective-permute-done.3.l_ref), channel_id=1, source_target_pairs={{0,4},{4,0},{1,5},{5,1},{2,6},{6,2},{3,7},{7,3},{8,12},{12,8},{9,1... | collective-permute-start | bytes 589832 | tf_op jit(solution)/shard_map/ppermute | solution.py:257

commit v3 on v2

--- a/solution.py
+++ b/solution.py
@@ -111,8 +111,7 @@
     sides = lax.dot_general(wlr_ref[...], normed[...], NT, preferred_element_type=F32).astype(BF16)
     for r in range(BLK):
         lt_ref[r * OPM : (r + 1) * OPM, :] = sides[:OPM, r * SEQS : (r + 1) * SEQS]
-        for copy in range(PEERS):
-            rt_ref[copy, r * OPM : (r + 1) * OPM, :] = sides[OPM:, r * SEQS : (r + 1) * SEQS]
+        rt_ref[r * OPM : (r + 1) * OPM, :] = sides[OPM:, r * SEQS : (r + 1) * SEQS]
     u_ref[...] = flat[...].reshape(SEQS, ROWS, LANES).astype(BF16)
 
 
@@ -123,7 +122,7 @@
         out_shape=(
             jax.ShapeDtypeStruct((SEQS, ROWS, LANES), BF16),
             jax.ShapeDtypeStruct((BLK * OPM, SEQS), BF16),
-            jax.ShapeDtypeStruct((PEERS, BLK * OPM, SEQS), BF16),
+            jax.ShapeDtypeStruct((BLK * OPM, SEQS), BF16),
         ),
         in_specs=[vmem_spec()] * 3,
         out_specs=(vmem_spec(),) * 3,
@@ -159,14 +158,23 @@
         out_ref[i] = total.astype(BF16)
 
 
-def first_pair_kernel(at_ref, l_ref, own_ref, other_ref, we_ref, wo_ref, out_ref, right, flat, outer):
-    first = pl.multiple_of(at_ref[2] * HALF, HALF)
-    flat[pl.ds(first, HALF), :] = own_ref[...].astype(F32)
-    flat[pl.ds(pl.multiple_of(HALF - first, HALF), HALF), :] = other_ref[...].astype(F32)
-    for p in range(OPM // 2):
-        even = flat[pl.ds(2 * p, COLS, stride=OPM), :]
-        odd = flat[pl.ds(2 * p + 1, COLS, stride=OPM), :]
-        right[p] = jnp.concatenate([even, odd], axis=0).T.astype(BF16)
+def first_pair_kernel(at_ref, l_ref, *refs):
+    pieces, (we_ref, wo_ref, out_ref, right, flat, outer) = refs[:8], refs[8:]
+    step = BLK * OPM
+
+    @pl.when(pl.program_id(0) == 0)
+    def _():
+        for n, piece in enumerate(pieces):
+            core = at_ref[2] ^ (n // 4)
+            z = (at_ref[4] + (0, 3, 1, 2)[n % 4]) & 3
+            for b in range(2):
+                block = core * 8 + (at_ref[3] ^ b) * 4 + z
+                flat[pl.ds(pl.multiple_of(block * step, step), step), :] = piece[b].astype(F32)
+        for p in range(OPM // 2):
+            even = flat[pl.ds(2 * p, COLS, stride=OPM), :]
+            odd = flat[pl.ds(2 * p + 1, COLS, stride=OPM), :]
+            right[p] = jnp.concatenate([even, odd], axis=0).T.astype(BF16)
+
     pair_rows(l_ref[0], right, we_ref, wo_ref, out_ref, outer)
 
 
@@ -179,7 +187,6 @@
 
 
 def pair_call(kernel, where, steps, operands, in_specs, extra_shapes, extra_specs, scratch, aliases):
-    flops = 2 * steps * BLK * COLS * OPM * OPM * (SEQS + 128)
     return pl.pallas_call(
         kernel,
         out_shape=[jax.ShapeDtypeStruct((PEERS * BLK, COLS, 128), BF16)] + extra_shapes,
@@ -191,17 +198,17 @@
             scratch_shapes=scratch + [pltpu.VMEM((BLK, 512, 384), BF16)],
         ),
         input_output_aliases=aliases,
-        cost_estimate=pl.CostEstimate(flops=flops, bytes_accessed=8 * 1024 * 1024, transcendentals=0),
+        cost_estimate=pl.CostEstimate(flops=1000, bytes_accessed=1000, transcendentals=0),
         compiler_params=VMEM,
         name="pair_grid",
     )(*operands)
 
 
-def pair_first(place, left, own, other, weights):
+def pair_first(place, left, pieces, weights):
     right = (OPM // 2, SEQS, 384)
     return pair_call(
-        first_pair_kernel, lambda k, x_lo, y: x_lo * 4 + y, 1, (place, left, own, other) + weights,
-        [whole(HALF, SEQS)] * 2 + [vmem_spec()] * 2,
+        first_pair_kernel, lambda k, x_lo, y: x_lo * 4 + (y ^ (k << 1)), 2, (place, left) + pieces + weights,
+        [whole(*piece.shape) for piece in pieces] + [vmem_spec()] * 2,
         [jax.ShapeDtypeStruct(right, BF16)], [vmem_spec()], [pltpu.VMEM((2 * HALF, SEQS), F32)], {},
     )
 
@@ -220,6 +227,10 @@
         y, x_lo, core, z, x_hi = d % 4, d // 4 % 2, d // 8 % 2, d // 16 % 4, d // 64
         pairs.append((d, ((x_lo * 4 + y) * 2 + core) * 8 + x_hi * 4 + z))
     return pairs
+
+
+def shifted(step):
+    return [(i, (i + step) % 4) for i in range(4)]
 
 
 def flipped(size, bit):
@@ -235,25 +246,25 @@
     blocks = lax.all_to_all(packed, AXES, split_axis=0, concat_axis=0, tiled=True)
     w_sides = jnp.concatenate([w_left, w_right], axis=1).T
     w_pairs = w_pair.reshape(OPM, OPM // 2, 2, 128).transpose(2, 3, 1, 0).reshape(2, 128, 512)
-    place = jnp.stack([lax.axis_index(a) for a in ("x_lo", "y", "core")]).astype(jnp.int32)
+    place = jnp.stack([lax.axis_index(a) for a in ("x_lo", "y", "core", "x_hi", "z")]).astype(jnp.int32)
     blocks, w_even, w_odd, place = lax.optimization_barrier((blocks, w_pairs[0], w_pairs[1], place))
     weights = (w_even, w_odd)
     updated, left, right = attention(blocks, jnp.stack([w_query, w_key, w_value, w_gate, w_attend]), w_sides)
 
-    own = lax.all_to_all(right, ("x_hi", "z"), split_axis=0, concat_axis=0, tiled=True)
     near = lax.ppermute(left, AXES, crossed())[None]
-    near, own = lax.optimization_barrier((near, own))
-    own = own.reshape(HALF, SEQS)
-    other = lax.ppermute(own, "core", flipped(2, 1))
+    mine = right[None]
+    mine = jnp.concatenate([mine, lax.ppermute(mine, "x_hi", flipped(2, 1))])
+    second = lax.ppermute(near, "y", flipped(4, 2))
+    pieces = (mine, lax.ppermute(mine, "z", shifted(1)), lax.ppermute(mine, "z", shifted(3)), lax.ppermute(mine, "z", flipped(4, 2)))
+    pieces, second, updated = lax.optimization_barrier((pieces, second, updated))
+    pieces += tuple(lax.ppermute(piece, "core", flipped(2, 1)) for piece in pieces)
     returned = lax.all_to_all(updated, AXES, split_axis=0, concat_axis=0, tiled=True)
-    second = lax.ppermute(near, "y", flipped(4, 2))
-    grid, rights = pair_first(place, near, own, other, weights)
-
-    second, grid = lax.optimization_barrier((second, grid))
+
     two = jnp.concatenate([near, second])
     third = lax.ppermute(two, "y", flipped(4, 1))
     fourth = lax.ppermute(two, "x_lo", flipped(2, 1))
-    grid = pair_next(place, second, rights, weights, grid, lambda k, x_lo, y: x_lo * 4 + (y ^ 2))
+    grid, rights = pair_first(place, two, pieces, weights)
+    third, grid = lax.optimization_barrier((third, grid))
     last = lax.ppermute(third, "x_lo", flipped(2, 1))
     grid = pair_next(place, third, rights, weights, grid, lambda k, x_lo, y: x_lo * 4 + (y ^ 1 ^ (k << 1)))
     grid = pair_next(place, fourth, rights, weights, grid, lambda k, x_lo, y: (1 - x_lo) * 4 + (y ^ (k << 1)))

time: 105 us -> 98.6 us (0.939)
  starting transfers between devices: 34 us -> 32 us
  local copies, waits for them, and re-layouts: 5.12 us -> 3.18 us
  Pallas kernels: 37.4 us -> 35.9 us
    all_to_all x1 -> x0, waiting for transfers between devices: 10.3 us -> none  [body(): lax.all_to_all(right, ('x_hi', 'z'), split_axis=0, concat_axis=0, tiled=T...]
    ppermute x1 -> x8, waiting for transfers between devices: 0.01 us -> 6.83 us  [the longest x1 4 us: body(): mine = jnp.concatenate([mine, lax.ppermute(mine, 'x_hi', flipped(2, 1))])]
    all_to_all x1 -> x0, starting transfers between devices: 3.55 us -> none  [body(): lax.all_to_all(right, ('x_hi', 'z'), split_axis=0, concat_axis=0, tiled=T...]
    ppermute x1, waiting for transfers between devices: 0.01 us -> 3.26 us  [body(): second = lax.ppermute(near, 'y', flipped(4, 2))]
    ppermute x1, waiting for transfers between devices: 2.87 us -> 0.01 us  [body(): fourth = lax.ppermute(two, 'x_lo', flipped(2, 1))]
    ppermute x1 -> x8, starting transfers between devices: 3.29 us -> 6.13 us  [the longest x1 2.61 us: body(): lax.ppermute(mine, 'z', flipped(4, 2))]
    ppermute x1, waiting for transfers between devices: 0.01 us -> 2.19 us  [body(): third = lax.ppermute(two, 'y', flipped(4, 1))]
    unnamed x25 -> x20, local copies, waits for them, and re-layouts: 3.21 us -> 1.2 us
  transfers between devices with their start and end apart: 9 -> 15, of which waited for: 3 -> 6; matrix products, arithmetic and copies ran while one was open for 2% -> 2% of each run, Pallas kernels for 26% -> 27%
where the time goes in v3:
time: 98.6 us; the launch traced here: 98.3 us
  Pallas kernels  35.9 us (36%)
  starting transfers between devices  32 us (32%)
  waiting for transfers between devices  26.4 us (27%)
  local copies, waits for them, and re-layouts  3.18 us (3%)
    pallas_call x4, Pallas kernels, pair_call(): pl.pallas_call(kernel, out_shape=[jax.ShapeDtypeStruct((PEERS * BLK, COLS...  26.2 us
    all_to_all x1, waiting for transfers between devices, body(): lax.all_to_all(packed, AXES, split_axis=0, concat_axis=0, tiled=True)  14.1 us
    all_to_all x1, starting transfers between devices, body(): lax.all_to_all(packed, AXES, split_axis=0, concat_axis=0, tiled=True)  11.5 us
    all_to_all x1, starting transfers between devices, body(): lax.all_to_all(updated, AXES, split_axis=0, concat_axis=0, tiled=True)  8.52 us
    pallas_call x1, Pallas kernels, attention(): pl.pallas_call(attention_kernel, out_shape=(jax.ShapeDtypeStruct((SEQS, R...  7.6 us
    ppermute x1, waiting for transfers between devices, body(): mine = jnp.concatenate([mine, lax.ppermute(mine, 'x_hi', flipped(2, 1))])  4 us
    ppermute x1, waiting for transfers between devices, body(): second = lax.ppermute(near, 'y', flipped(4, 2))  3.26 us
    ppermute x1, starting transfers between devices, body(): lax.ppermute(mine, 'z', flipped(4, 2))  2.61 us
  transfers between devices with their start and end apart: 15, of which 6 were waited for; matrix products, arithmetic and copies ran while one was open for 2% of the time, Pallas kernels for 27%

profile of v3, /device:TPU:1, one launch (start us, length us, event | category | flops | bytes accessed | tf_op | source)
XLA Modules:
  0.0 98.3 jit_solution(6522980159567951184)
XLA Ops:
  0.6 0.0 copy-start
  0.6 1.1 %copy-done = bf16[1,1536,256]{2,1,0:T(8,128)(2,1)S(1)} copy-done((bf16[1,1536,256]{2,1,0:T(8,128)(2,1)S(1)}, bf16[1,1536,256]{2,1,0:T(8,128)(2,1)}, u32[]{:S(2)}) %copy-start) | copy-done | bytes 786456
  1.8 0.0 copy-start.3
  1.8 1.0 %pack.1 = bf16[128,24,128]{2,1,0:T(8,128)(2,1)} custom-call(bf16[1536,256]{1,0:T(8,128)(2,1)S(1)} %bitcast.26), custom_call_target="tpu_custom_call" | custom-call | tf_op jit(solution)/shard_map/pack/pallas_call | solution.py:242
  2.8 11.5 %all-to-all-start = ((bf16[128,24,128]{2,1,0:T(8,128)(2,1)}), bf16[128,24,128]{2,1,0:T(8,128)(2,1)S(1)}, u32[]{:S(2)}, u32[]{:S(2)}) async-start(bf16[128,24,128]{2,1,0:T(8,128)(2,1)} %pack.1), calls=%async_computation | async-start | bytes 1572864 | tf_op jit(solution)/shard_map/all_to_all | solution.py:246
  14.3 1.5 %fusion = (bf16[1,128,16,32]{1,0,2,3:T(2,128)(2,1)S(1)}, bf16[1,128,16,32]{1,0,2,3:T(2,128)(2,1)S(1)}) fusion(bf16[2,128,16,32]{1,0,2,3:T(2,128)(2,1)} %bitcast.29), kind=kLoop, calls=%fused_computation.8 | loop fusion | bytes 524288 | tf_op jit(solution)/shard_map/slice | solution.py:250
  15.8 0.1 copy.24
  15.9 0.1 copy.23
  16.1 0.1 stack.41.at_ref
  16.2 0.0 copy-done.6
  16.2 0.0 copy-done.4
  16.3 14.1 %all-to-all-done.x_ref = bf16[128,24,128]{2,1,0:T(8,128)(2,1)S(1)} async-done(((bf16[128,24,128]{2,1,0:T(8,128)(2,1)}), bf16[128,24,128]{2,1,0:T(8,128)(2,1)S(1)}, u32[]{:S(2)}, u32[]{:S(2)}) %all-to-all-start) | async-done | bytes 786464 | tf_op jit(solution)/shard_map/all_to_all | solution.py:246
  30.4 7.6 %attention.1 = (bf16[128,24,128]{2,1,0:T(8,128)(2,1)}, bf16[384,128]{1,0:T(8,128)(2,1)S(1)}, bf16[384,128]{1,0:T(8,128)(2,1)S(1)}) custom-call(bf16[128,24,128]{2,1,0:T(8,128)(2,1)S(1)} %all-to-all-done.x_ref, bf16[5,256,256]{2,1,0:T(8,128)(2,1)S(1)} %bitcast_dynamic-update-slice_fusion.w_ref, bf16[64,256]{1,0:T(8,128)(2,1)S(1)} %maximum_bitcast_fusion.wlr_ref), custom_call_target="tpu_custom_call" | custom-call | tf_op jit(solution)/shard_map/attention/pallas_call | solution.py:120
  38.0 0.3 collective-permute-start
  38.3 0.7 collective-permute-start.4
  38.9 4.0 %collective-permute-done = bf16[1,384,128]{2,1,0:T(8,128)(2,1)S(1)} collective-permute-done((bf16[1,384,128]{2,1,0:T(8,128)(2,1)S(1)}, bf16[1,384,128]{2,1,0:T(8,128)(2,1)S(1)}, u32[]{:S(2)}, u32[]{:S(2)}) %collective-permute-start) | collective-permute-done | bytes 98336 | tf_op jit(solution)/shard_map/ppermute | solution.py:256
  43.0 2.6 %collective-permute-start.3 = (bf16[2,384,128]{2,1,0:T(8,128)(2,1)S(1)}, bf16[2,384,128]{2,1,0:T(8,128)(2,1)S(1)}, u32[]{:S(2)}, u32[]{:S(2)}) collective-permute-start(bf16[2,384,128]{2,1,0:T(8,128)(2,1)S(1)} %pad_maximum_fusion.refs_0_), channel_id=1, source_target_pairs={{0,32},{16,48},{32,0},{48,16},{1,33},{17,49},{33,1},{49,17},{2,34}... | collective-permute-start | bytes 589832 | tf_op jit(solution)/shard_map/ppermute | solution.py:258
  45.6 0.5 collective-permute-start.2
  46.1 0.9 collective-permute-start.1
  47.1 0.0 collective-permute-done.4
  47.1 2.0 %collective-permute-start.5 = (bf16[1,384,128]{2,1,0:T(8,128)(2,1)S(1)}, bf16[1,384,128]{2,1,0:T(8,128)(2,1)S(1)}, u32[]{:S(2)}, u32[]{:S(2)}) collective-permute-start(bf16[1,384,128]{2,1,0:T(8,128)(2,1)S(1)} %bitcast.33), channel_id=1, source_target_pairs={{0,2},{1,3},{2,0},{3,1},{4,6},{5,7},{6,4},{7,5},{8,10},{9,11},{10,... | collective-permute-start | bytes 294920 | tf_op jit(solution)/shard_map/ppermute | solution.py:257
  49.1 3.3 %collective-permute-done.5 = bf16[1,384,128]{2,1,0:T(8,128)(2,1)S(1)} collective-permute-done((bf16[1,384,128]{2,1,0:T(8,128)(2,1)S(1)}, bf16[1,384,128]{2,1,0:T(8,128)(2,1)S(1)}, u32[]{:S(2)}, u32[]{:S(2)}) %collective-permute-start.5) | collective-permute-done | bytes 98336 | tf_op jit(solution)/shard_map/ppermute | solution.py:257
  52.3 0.0 collective-permute-done.3.refs_3_
  52.3 2.1 %collective-permute-done.2.refs_2_ = bf16[2,384,128]{2,1,0:T(8,128)(2,1)S(1)} collective-permute-done((bf16[2,384,128]{2,1,0:T(8,128)(2,1)S(1)}, bf16[2,384,128]{2,1,0:T(8,128)(2,1)S(1)}, u32[]{:S(2)}, u32[]{:S(2)}) %collective-permute-start.2) | collective-permute-done | bytes 196640 | tf_op jit(solution)/shard_map/ppermute | solution.py:258
  54.4 0.7 collective-permute-done.1.refs_1_
  55.1 8.5 %all-to-all-start.1 = ((bf16[128,24,128]{2,1,0:T(8,128)(2,1)}), bf16[128,24,128]{2,1,0:T(8,128)(2,1)S(1)}, u32[]{:S(2)}, u32[]{:S(2)}) async-start(bf16[128,24,128]{2,1,0:T(8,128)(2,1)} %get-tuple-element.25), calls=%async_computation.1 | async-start | bytes 1572864 | tf_op jit(solution)/shard_map/all_to_all | solution.py:261
  63.7 1.1 %collective-permute-start.7 = (bf16[2,384,128]{2,1,0:T(8,128)(2,1)S(1)}, bf16[2,384,128]{2,1,0:T(8,128)(2,1)S(1)}, u32[]{:S(2)}, u32[]{:S(2)}) collective-permute-start(bf16[2,384,128]{2,1,0:T(8,128)(2,1)S(1)} %pad_maximum_fusion.refs_0_), channel_id=1, source_target_pairs={{0,8},{8,0},{1,9},{9,1},{2,10},{10,2},{3,11},{11,3},{4,12},{12,4},... | collective-permute-start | bytes 589832 | tf_op jit(solution)/shard_map/ppermute | solution.py:260
  64.8 0.1 collective-permute-start.8
  64.9 0.4 collective-permute-start.9
  65.3 0.1 collective-permute-start.10
  65.5 0.8 collective-permute-start.6
  66.3 0.1 copy.25.refs_8_.we_ref
  66.4 0.1 copy.26.refs_9_.wo_ref
  66.5 0.0 collective-permute-done.7.refs_4_
  66.5 1.4 %collective-permute-start.12 = (bf16[2,384,128]{2,1,0:T(8,128)(2,1)S(1)}, bf16[2,384,128]{2,1,0:T(8,128)(2,1)S(1)}, u32[]{:S(2)}, u32[]{:S(2)}) collective-permute-start(bf16[2,384,128]{2,1,0:T(8,128)(2,1)S(1)} %pad_maximum_fusion.1.l_ref), channel_id=1, source_target_pairs={{0,4},{4,0},{1,5},{5,1},{2,6},{6,2},{3,7},{7,3},{8,12},{12,8},{9,1... | collective-permute-start | bytes 589832 | tf_op jit(solution)/shard_map/ppermute | solution.py:265
  68.0 0.0 collective-permute-done.8.refs_5_
  68.0 0.0 collective-permute-done.9.refs_6_
  68.0 0.0 collective-permute-done.10.refs_7_
  68.0 8.1 %pair_grid.4 = (bf16[96,192,128]{2,1,0:T(8,128)(2,1)}, bf16[16,128,384]{2,1,0:T(8,128)(2,1)S(1)}) custom-call(s32[5]{0:T(128)S(1)} %stack.41.at_ref, bf16[2,384,128]{2,1,0:T(8,128)(2,1)S(1)} %pad_maximum_fusion.1.l_ref, bf16[2,384,128]{2,1,0:T(8,128)(2,1)S(1)} %pad_maximum_fusion.refs_0_, bf16[2,384,128]{2,1,0:T(8,128)(2,1)S(1)} %collective-permute-done.1.refs_1_, ...), custom_call_target="tpu_custom_call" | custom-call | flops 1000 | bytes 1000 | tf_op jit(solution)/shard_map/pair_grid/pallas_call | solution.py:190
  76.0 2.2 %collective-permute-done.6.l_ref = bf16[2,384,128]{2,1,0:T(8,128)(2,1)S(1)} collective-permute-done((bf16[2,384,128]{2,1,0:T(8,128)(2,1)S(1)}, bf16[2,384,128]{2,1,0:T(8,128)(2,1)S(1)}, u32[]{:S(2)}, u32[]{:S(2)}) %collective-permute-start.6) | collective-permute-done | bytes 196640 | tf_op jit(solution)/shard_map/ppermute | solution.py:264
  78.2 0.9 collective-permute-start.11
  79.1 6.0 %pair_grid.5.before_ref = bf16[96,192,128]{2,1,0:T(8,128)(2,1)} custom-call(s32[5]{0:T(128)S(1)} %stack.41.at_ref, bf16[2,384,128]{2,1,0:T(8,128)(2,1)S(1)} %collective-permute-done.6.l_ref, bf16[16,128,384]{2,1,0:T(8,128)(2,1)S(1)} %get-tuple-element.36.right, bf16[128,512]{1,0:T(8,128)(2,1)S(1)} %copy.25.refs_8_.we_ref, ...), custom_call_target="tpu_custom_call", output_to_operand_aliasing={{}: (5, {})} | custom-call | flops 1000 | bytes 1000 | tf_op jit(solution)/shard_map/pair_grid/pallas_call | solution.py:190
  85.2 0.0 collective-permute-done.12.l_ref
  85.2 6.0 %pair_grid.6.before_ref = bf16[96,192,128]{2,1,0:T(8,128)(2,1)} custom-call(s32[5]{0:T(128)S(1)} %stack.41.at_ref, bf16[2,384,128]{2,1,0:T(8,128)(2,1)S(1)} %collective-permute-done.12.l_ref, bf16[16,128,384]{2,1,0:T(8,128)(2,1)S(1)} %get-tuple-element.36.right, bf16[128,512]{1,0:T(8,128)(2,1)S(1)} %copy.25.refs_8_.we_ref, ...), custom_call_target="tpu_custom_call", output_to_operand_aliasing={{}: (5, {})} | custom-call | flops 1000 | bytes 1000 | tf_op jit(solution)/shard_map/pair_grid/pallas_call | solution.py:190
  91.2 0.0 collective-permute-done.11.l_ref
  91.2 6.1 %pair_grid.7 = bf16[96,192,128]{2,1,0:T(8,128)(2,1)} custom-call(s32[5]{0:T(128)S(1)} %stack.41.at_ref, bf16[2,384,128]{2,1,0:T(8,128)(2,1)S(1)} %collective-permute-done.11.l_ref, bf16[16,128,384]{2,1,0:T(8,128)(2,1)S(1)} %get-tuple-element.36.right, bf16[128,512]{1,0:T(8,128)(2,1)S(1)} %copy.25.refs_8_.we_ref, ...), custom_call_target="tpu_custom_call", output_to_operand_aliasing={{}: (5, {})} | custom-call | flops 1000 | bytes 1000 | tf_op jit(solution)/shard_map/pair_grid/pallas_call | solution.py:190
  97.3 0.0 all-to-all-done.1.x_ref
  97.3 1.0 %unpack.1 = bf16[1536,256]{1,0:T(8,128)(2,1)} custom-call(bf16[128,24,128]{2,1,0:T(8,128)(2,1)S(1)} %all-to-all-done.1.x_ref), custom_call_target="tpu_custom_call" | custom-call | tf_op jit(solution)/shard_map/unpack/pallas_call | solution.py:275
  (19 shorter events, 0.1 us)
Async XLA Ops:
  0.6 1.1 %copy-start = (bf16[1,1536,256]{2,1,0:T(8,128)(2,1)S(1)}, bf16[1,1536,256]{2,1,0:T(8,128)(2,1)}, u32[]{:S(2)}) copy-start(bf16[1,1536,256]{2,1,0:T(8,128)(2,1)} %param.9) | copy-start | bytes 2359300
  1.8 14.3 %copy-start.1 = (bf16[256,256]{1,0:T(8,128)(2,1)S(1)}, bf16[256,256]{1,0:T(8,128)(2,1)}, u32[]{:S(2)}) copy-start(bf16[256,256]{1,0:T(8,128)(2,1)} %param.10) | copy-start | bytes 393220
  1.8 14.3 %copy-start.2 = (bf16[256,256]{1,0:T(8,128)(2,1)S(1)}, bf16[256,256]{1,0:T(8,128)(2,1)}, u32[]{:S(2)}) copy-start(bf16[256,256]{1,0:T(8,128)(2,1)} %param.11) | copy-start | bytes 393220
  1.8 14.4 %copy-start.6 = (bf16[256,32]{0,1:T(8,128)(2,1)S(1)}, bf16[256,32]{0,1:T(8,128)(2,1)}, u32[]{:S(2)}) copy-start(bf16[256,32]{0,1:T(8,128)(2,1)} %param.16) | copy-start | bytes 49156
  1.8 14.4 %copy-start.7 = (bf16[256,32]{0,1:T(8,128)(2,1)S(1)}, bf16[256,32]{0,1:T(8,128)(2,1)}, u32[]{:S(2)}) copy-start(bf16[256,32]{0,1:T(8,128)(2,1)} %param.15) | copy-start | bytes 49156
  1.8 14.4 %copy-start.3 = (bf16[256,256]{1,0:T(8,128)(2,1)S(1)}, bf16[256,256]{1,0:T(8,128)(2,1)}, u32[]{:S(2)}) copy-start(bf16[256,256]{1,0:T(8,128)(2,1)} %param.12) | copy-start | bytes 393220
  1.8 14.4 %copy-start.4 = (bf16[256,256]{1,0:T(8,128)(2,1)S(1)}, bf16[256,256]{1,0:T(8,128)(2,1)}, u32[]{:S(2)}) copy-start(bf16[256,256]{1,0:T(8,128)(2,1)} %param.13) | copy-start | bytes 393220
  1.8 14.4 %copy-start.5 = (bf16[256,256]{1,0:T(8,128)(2,1)S(1)}, bf16[256,256]{1,0:T(8,128)(2,1)}, u32[]{:S(2)}) copy-start(bf16[256,256]{1,0:T(8,128)(2,1)} %param.14) | copy-start | bytes 393220
  2.8 27.5 %all-to-all-start = ((bf16[128,24,128]{2,1,0:T(8,128)(2,1)}), bf16[128,24,128]{2,1,0:T(8,128)(2,1)S(1)}, u32[]{:S(2)}, u32[]{:S(2)}) async-start(bf16[128,24,128]{2,1,0:T(8,128)(2,1)} %pack.1), calls=%async_computation | async-start | bytes 1572864 | tf_op jit(solution)/shard_map/all_to_all | solution.py:246
  38.0 5.0 %collective-permute-start = (bf16[1,384,128]{2,1,0:T(8,128)(2,1)S(1)}, bf16[1,384,128]{2,1,0:T(8,128)(2,1)S(1)}, u32[]{:S(2)}, u32[]{:S(2)}) collective-permute-start(bf16[1,384,128]{2,1,0:T(8,128)(2,1)S(1)} %bitcast.27), channel_id=1, source_target_pairs={{0,64},{64,0},{1,65},{65,1},{2,66},{66,2},{3,67},{67,3},{4,68},{68... | collective-permute-start | bytes 294920 | tf_op jit(solution)/shard_map/ppermute | solution.py:256
  38.3 8.8 %collective-permute-start.4 = (bf16[384,128]{1,0:T(8,128)(2,1)S(1)}, bf16[384,128]{1,0:T(8,128)(2,1)S(1)}, u32[]{:S(2)}, u32[]{:S(2)}) collective-permute-start(bf16[384,128]{1,0:T(8,128)(2,1)S(1)} %get-tuple-element.23), channel_id=1, source_target_pairs={{0,0},{1,16},{2,32},{3,48},{4,64},{5,80},{6,96},{7,112},{8,8},{9,2... | collective-permute-start | bytes 294920 | tf_op jit(solution)/shard_map/ppermute | solution.py:254
  43.0 9.3 %collective-permute-start.3 = (bf16[2,384,128]{2,1,0:T(8,128)(2,1)S(1)}, bf16[2,384,128]{2,1,0:T(8,128)(2,1)S(1)}, u32[]{:S(2)}, u32[]{:S(2)}) collective-permute-start(bf16[2,384,128]{2,1,0:T(8,128)(2,1)S(1)} %pad_maximum_fusion.refs_0_), channel_id=1, source_target_pairs={{0,32},{16,48},{32,0},{48,16},{1,33},{17,49},{33,1},{49,17},{2,34}... | collective-permute-start | bytes 589832 | tf_op jit(solution)/shard_map/ppermute | solution.py:258
  45.6 8.8 %collective-permute-start.2 = (bf16[2,384,128]{2,1,0:T(8,128)(2,1)S(1)}, bf16[2,384,128]{2,1,0:T(8,128)(2,1)S(1)}, u32[]{:S(2)}, u32[]{:S(2)}) collective-permute-start(bf16[2,384,128]{2,1,0:T(8,128)(2,1)S(1)} %pad_maximum_fusion.refs_0_), channel_id=1, source_target_pairs={{0,48},{16,0},{32,16},{48,32},{1,49},{17,1},{33,17},{49,33},{2,50}... | collective-permute-start | bytes 589832 | tf_op jit(solution)/shard_map/ppermute | solution.py:258
  46.1 9.0 %collective-permute-start.1 = (bf16[2,384,128]{2,1,0:T(8,128)(2,1)S(1)}, bf16[2,384,128]{2,1,0:T(8,128)(2,1)S(1)}, u32[]{:S(2)}, u32[]{:S(2)}) collective-permute-start(bf16[2,384,128]{2,1,0:T(8,128)(2,1)S(1)} %pad_maximum_fusion.refs_0_), channel_id=1, source_target_pairs={{0,16},{16,32},{32,48},{48,0},{1,17},{17,33},{33,49},{49,1},{2,18}... | collective-permute-start | bytes 589832 | tf_op jit(solution)/shard_map/ppermute | solution.py:258
  47.1 5.3 %collective-permute-start.5 = (bf16[1,384,128]{2,1,0:T(8,128)(2,1)S(1)}, bf16[1,384,128]{2,1,0:T(8,128)(2,1)S(1)}, u32[]{:S(2)}, u32[]{:S(2)}) collective-permute-start(bf16[1,384,128]{2,1,0:T(8,128)(2,1)S(1)} %bitcast.33), channel_id=1, source_target_pairs={{0,2},{1,3},{2,0},{3,1},{4,6},{5,7},{6,4},{7,5},{8,10},{9,11},{10,... | collective-permute-start | bytes 294920 | tf_op jit(solution)/shard_map/ppermute | solution.py:257
  55.1 42.1 %all-to-all-start.1 = ((bf16[128,24,128]{2,1,0:T(8,128)(2,1)}), bf16[128,24,128]{2,1,0:T(8,128)(2,1)S(1)}, u32[]{:S(2)}, u32[]{:S(2)}) async-start(bf16[128,24,128]{2,1,0:T(8,128)(2,1)} %get-tuple-element.25), calls=%async_computation.1 | async-start | bytes 1572864 | tf_op jit(solution)/shard_map/all_to_all | solution.py:261
  63.7 2.8 %collective-permute-start.7 = (bf16[2,384,128]{2,1,0:T(8,128)(2,1)S(1)}, bf16[2,384,128]{2,1,0:T(8,128)(2,1)S(1)}, u32[]{:S(2)}, u32[]{:S(2)}) collective-permute-start(bf16[2,384,128]{2,1,0:T(8,128)(2,1)S(1)} %pad_maximum_fusion.refs_0_), channel_id=1, source_target_pairs={{0,8},{8,0},{1,9},{9,1},{2,10},{10,2},{3,11},{11,3},{4,12},{12,4},... | collective-permute-start | bytes 589832 | tf_op jit(solution)/shard_map/ppermute | solution.py:260
  64.8 3.1 %collective-permute-start.8 = (bf16[2,384,128]{2,1,0:T(8,128)(2,1)S(1)}, bf16[2,384,128]{2,1,0:T(8,128)(2,1)S(1)}, u32[]{:S(2)}, u32[]{:S(2)}) collective-permute-start(bf16[2,384,128]{2,1,0:T(8,128)(2,1)S(1)} %collective-permute-done.1.refs_1_), channel_id=1, source_target_pairs={{0,8},{8,0},{1,9},{9,1},{2,10},{10,2},{3,11},{11,3},{4,12},{12,4},... | collective-permute-start | bytes 589832 | tf_op jit(solution)/shard_map/ppermute | solution.py:260
  64.9 3.1 %collective-permute-start.9 = (bf16[2,384,128]{2,1,0:T(8,128)(2,1)S(1)}, bf16[2,384,128]{2,1,0:T(8,128)(2,1)S(1)}, u32[]{:S(2)}, u32[]{:S(2)}) collective-permute-start(bf16[2,384,128]{2,1,0:T(8,128)(2,1)S(1)} %collective-permute-done.2.refs_2_), channel_id=1, source_target_pairs={{0,8},{8,0},{1,9},{9,1},{2,10},{10,2},{3,11},{11,3},{4,12},{12,4},... | collective-permute-start | bytes 589832 | tf_op jit(solution)/shard_map/ppermute | solution.py:260
  65.3 2.6 %collective-permute-start.10 = (bf16[2,384,128]{2,1,0:T(8,128)(2,1)S(1)}, bf16[2,384,128]{2,1,0:T(8,128)(2,1)S(1)}, u32[]{:S(2)}, u32[]{:S(2)}) collective-permute-start(bf16[2,384,128]{2,1,0:T(8,128)(2,1)S(1)} %collective-permute-done.3.refs_3_), channel_id=1, source_target_pairs={{0,8},{8,0},{1,9},{9,1},{2,10},{10,2},{3,11},{11,3},{4,12},{12,4},... | collective-permute-start | bytes 589832 | tf_op jit(solution)/shard_map/ppermute | solution.py:260
  65.5 12.8 %collective-permute-start.6 = (bf16[2,384,128]{2,1,0:T(8,128)(2,1)S(1)}, bf16[2,384,128]{2,1,0:T(8,128)(2,1)S(1)}, u32[]{:S(2)}, u32[]{:S(2)}) collective-permute-start(bf16[2,384,128]{2,1,0:T(8,128)(2,1)S(1)} %pad_maximum_fusion.1.l_ref), channel_id=1, source_target_pairs={{0,1},{1,0},{2,3},{3,2},{4,5},{5,4},{6,7},{7,6},{8,9},{9,8},{10,11... | collective-permute-start | bytes 589832 | tf_op jit(solution)/shard_map/ppermute | solution.py:264
  66.5 18.7 %collective-permute-start.12 = (bf16[2,384,128]{2,1,0:T(8,128)(2,1)S(1)}, bf16[2,384,128]{2,1,0:T(8,128)(2,1)S(1)}, u32[]{:S(2)}, u32[]{:S(2)}) collective-permute-start(bf16[2,384,128]{2,1,0:T(8,128)(2,1)S(1)} %pad_maximum_fusion.1.l_ref), channel_id=1, source_target_pairs={{0,4},{4,0},{1,5},{5,1},{2,6},{6,2},{3,7},{7,3},{8,12},{12,8},{9,1... | collective-permute-start | bytes 589832 | tf_op jit(solution)/shard_map/ppermute | solution.py:265
  78.2 13.0 %collective-permute-start.11 = (bf16[2,384,128]{2,1,0:T(8,128)(2,1)S(1)}, bf16[2,384,128]{2,1,0:T(8,128)(2,1)S(1)}, u32[]{:S(2)}, u32[]{:S(2)}) collective-permute-start(bf16[2,384,128]{2,1,0:T(8,128)(2,1)S(1)} %collective-permute-done.6.l_ref), channel_id=1, source_target_pairs={{0,4},{4,0},{1,5},{5,1},{2,6},{6,2},{3,7},{7,3},{8,12},{12,8},{9,1... | collective-permute-start | bytes 589832 | tf_op jit(solution)/shard_map/ppermute | solution.py:268

commit v4 on v2

--- a/solution.py
+++ b/solution.py
@@ -64,6 +64,17 @@
         out_ref[group * 48 : group * 48 + 48, :] = jnp.concatenate([left, right], axis=1).astype(BF16)
 
 
+def head_sums(weighted, own):
+    sides = []
+    for first in (0, HEADS // 2):
+        side = jnp.zeros((SEQS, LANES), F32)
+        for h in range(first, first + HEADS // 2):
+            total = jnp.sum(weighted[:, h * SEQS : (h + 1) * SEQS], axis=-1, keepdims=True)
+            side = jnp.where(own[h - first][:, :LANES], total, side)
+        sides.append(side)
+    return jnp.concatenate(sides, axis=1)
+
+
 def attention_kernel(
     x_ref, w_ref, wlr_ref, u_ref, lt_ref, rt_ref,
     flat, normed, query, key, value, gate, attended, update,
@@ -89,8 +100,6 @@
     lane = lax.broadcasted_iota(jnp.int32, (SEQS, WIDTH), 1) // HEAD_DIM
     own = [(lane == h) for h in range(HEADS)]
     zero = jnp.zeros((SEQS, WIDTH), BF16)
-    ones = jnp.concatenate([jnp.where(m, 1.0, 0.0).astype(BF16) for m in own], axis=0)
-
     for r in range(BLK):
         at = span(r)
         q, k, v = query[at, :], key[at, :], value[at, :]
@@ -99,7 +108,7 @@
         scores = lax.dot_general(q, k_heads, NT, preferred_element_type=F32) * HEAD_DIM ** (-0.5)
         weighted = jnp.exp(scores).astype(BF16)
         numerator = jnp.dot(weighted, v_heads, preferred_element_type=F32)
-        denominator = jnp.dot(weighted, ones, preferred_element_type=F32)
+        denominator = head_sums(weighted.astype(F32), own)
         attended[at, :] = (gate[at, :] * numerator / denominator).astype(BF16)
 
     update[...] = jnp.dot(attended[...], w_ref[4], preferred_element_type=F32)
@@ -111,8 +120,7 @@
     sides = lax.dot_general(wlr_ref[...], normed[...], NT, preferred_element_type=F32).astype(BF16)
     for r in range(BLK):
         lt_ref[r * OPM : (r + 1) * OPM, :] = sides[:OPM, r * SEQS : (r + 1) * SEQS]
-        for copy in range(PEERS):
-            rt_ref[copy, r * OPM : (r + 1) * OPM, :] = sides[OPM:, r * SEQS : (r + 1) * SEQS]
+        rt_ref[r * OPM : (r + 1) * OPM, :] = sides[OPM:, r * SEQS : (r + 1) * SEQS]
     u_ref[...] = flat[...].reshape(SEQS, ROWS, LANES).astype(BF16)
 
 
@@ -123,7 +131,7 @@
         out_shape=(
             jax.ShapeDtypeStruct((SEQS, ROWS, LANES), BF16),
             jax.ShapeDtypeStruct((BLK * OPM, SEQS), BF16),
-            jax.ShapeDtypeStruct((PEERS, BLK * OPM, SEQS), BF16),
+            jax.ShapeDtypeStruct((BLK * OPM, SEQS), BF16),
         ),
         in_specs=[vmem_spec()] * 3,
         out_specs=(vmem_spec(),) * 3,
@@ -143,74 +151,85 @@
 
 
 COLS = 192
+PART = 4
 HALF = PEERS * BLK * OPM
 
 
-def pair_rows(left, right, we_ref, wo_ref, out_ref, outer):
-    for p in range(OPM // 2):
-        product = jnp.dot(left, right[p], preferred_element_type=F32).astype(BF16)
-        for i in range(BLK):
-            outer[i, p * OPM : (p + 1) * OPM, :] = product[i * OPM : (i + 1) * OPM]
+def pair_rows(at_ref, places, l_refs, right, we_ref, wo_ref, out_ref, outer, rows, sems):
     even_w, odd_w = we_ref[...], wo_ref[...]
-    for i in range(BLK):
-        even = jnp.dot(even_w, outer[i, :, :256], preferred_element_type=F32)
-        odd = jnp.dot(odd_w, outer[i, :, 128:], preferred_element_type=F32)
-        total = (even.T[:COLS] + odd.T[64:]) * (1.0 / SEQS)
-        out_ref[i] = total.astype(BF16)
-
-
-def first_pair_kernel(at_ref, l_ref, own_ref, other_ref, we_ref, wo_ref, out_ref, right, flat, outer):
-    first = pl.multiple_of(at_ref[2] * HALF, HALF)
-    flat[pl.ds(first, HALF), :] = own_ref[...].astype(F32)
-    flat[pl.ds(pl.multiple_of(HALF - first, HALF), HALF), :] = other_ref[...].astype(F32)
+    copies = []
+    for turn, l_ref in enumerate(l_refs):
+        left = l_ref[...].reshape(2 * BLK * OPM, SEQS)
+        for p in range(OPM // 2):
+            product = jnp.dot(left, right[p], preferred_element_type=F32).astype(BF16)
+            for i in range(2 * BLK):
+                outer[i, p * OPM : (p + 1) * OPM, :] = product[i * OPM : (i + 1) * OPM]
+        for part in range(2 * BLK // PART):
+            first = turn * 2 * BLK + part * PART
+            for i in range(part * PART, part * PART + PART):
+                even = jnp.dot(even_w, outer[i, :, :256], preferred_element_type=F32)
+                odd = jnp.dot(odd_w, outer[i, :, 128:], preferred_element_type=F32)
+                rows[turn * 2 * BLK + i] = ((even.T[:COLS] + odd.T[64:]) * (1.0 / SEQS)).astype(BF16)
+            x_lo, y = places[first // BLK]
+            target = ((at_ref[0] ^ x_lo) * 4 + (at_ref[1] ^ y)) * BLK + first % BLK
+            copy = pltpu.make_async_copy(
+                rows.at[pl.ds(first, PART)], out_ref.at[pl.ds(target, PART)], sems.at[first // PART]
+            )
+            copy.start()
+            copies.append(copy)
+    for copy in copies:
+        copy.wait()
+
+
+def first_pair_kernel(places, at_ref, l0_ref, l1_ref, *refs):
+    pieces, (we_ref, wo_ref, out_ref, right, flat, outer, rows, sems) = refs[:8], refs[8:]
+    step = BLK * OPM
+    for n, piece in enumerate(pieces):
+        for x in range(2):
+            block = (at_ref[2] ^ (n // 4)) * 8 + (at_ref[3] ^ x) * 4 + (at_ref[4] ^ (n % 4))
+            flat[pl.ds(pl.multiple_of(block * step, step), step), :] = piece[x].astype(F32)
     for p in range(OPM // 2):
         even = flat[pl.ds(2 * p, COLS, stride=OPM), :]
         odd = flat[pl.ds(2 * p + 1, COLS, stride=OPM), :]
         right[p] = jnp.concatenate([even, odd], axis=0).T.astype(BF16)
-    pair_rows(l_ref[0], right, we_ref, wo_ref, out_ref, outer)
-
-
-def next_pair_kernel(at_ref, l_ref, right, we_ref, wo_ref, before_ref, out_ref, outer):
-    pair_rows(l_ref[0], right, we_ref, wo_ref, out_ref, outer)
-
-
-def whole(*shape):
-    return pl.BlockSpec(shape, lambda k, at: (0,) * len(shape))
-
-
-def pair_call(kernel, where, steps, operands, in_specs, extra_shapes, extra_specs, scratch, aliases):
-    flops = 2 * steps * BLK * COLS * OPM * OPM * (SEQS + 128)
+    pair_rows(at_ref, places, (l0_ref, l1_ref), right, we_ref, wo_ref, out_ref, outer, rows, sems)
+
+
+def next_pair_kernel(places, at_ref, l0_ref, l1_ref, right, we_ref, wo_ref, before_ref, out_ref, outer, rows, sems):
+    pair_rows(at_ref, places, (l0_ref, l1_ref), right, we_ref, wo_ref, out_ref, outer, rows, sems)
+
+
+def pair_call(kernel, places, operands, in_specs, extra_shapes, scratch, aliases, flops):
+    anywhere = pl.BlockSpec(memory_space=pl.ANY)
     return pl.pallas_call(
-        kernel,
+        functools.partial(kernel, places),
         out_shape=[jax.ShapeDtypeStruct((PEERS * BLK, COLS, 128), BF16)] + extra_shapes,
-        grid_spec=pltpu.PrefetchScalarGridSpec(
-            num_scalar_prefetch=1,
-            grid=(steps,),
-            in_specs=[pl.BlockSpec((1, BLK * OPM, SEQS), lambda k, at: (k, 0, 0))] + in_specs,
-            out_specs=[pl.BlockSpec((BLK, COLS, 128), lambda k, at: (where(k, at[0], at[1]), 0, 0))] + extra_specs,
-            scratch_shapes=scratch + [pltpu.VMEM((BLK, 512, 384), BF16)],
-        ),
+        in_specs=[pl.BlockSpec(memory_space=pltpu.SMEM)] + in_specs,
+        out_specs=[anywhere] + [vmem_spec()] * len(extra_shapes),
+        scratch_shapes=scratch
+        + [
+            pltpu.VMEM((2 * BLK, 512, 384), BF16),
+            pltpu.VMEM((4 * BLK, COLS, 128), BF16),
+            pltpu.SemaphoreType.DMA((4 * BLK // PART,)),
+        ],
         input_output_aliases=aliases,
-        cost_estimate=pl.CostEstimate(flops=flops, bytes_accessed=8 * 1024 * 1024, transcendentals=0),
+        cost_estimate=pl.CostEstimate(flops=flops, bytes_accessed=1000, transcendentals=0),
         compiler_params=VMEM,
         name="pair_grid",
     )(*operands)
 
 
-def pair_first(place, left, own, other, weights):
-    right = (OPM // 2, SEQS, 384)
+def pair_first(place, lefts, pieces, weights, places):
     return pair_call(
-        first_pair_kernel, lambda k, x_lo, y: x_lo * 4 + y, 1, (place, left, own, other) + weights,
-        [whole(HALF, SEQS)] * 2 + [vmem_spec()] * 2,
-        [jax.ShapeDtypeStruct(right, BF16)], [vmem_spec()], [pltpu.VMEM((2 * HALF, SEQS), F32)], {},
+        first_pair_kernel, places, (place,) + lefts + pieces + weights, [vmem_spec()] * 12,
+        [jax.ShapeDtypeStruct((OPM // 2, SEQS, 384), BF16)], [pltpu.VMEM((2 * HALF, SEQS), F32)], {}, 40_000_000_000,
     )
 
 
-def pair_next(place, left, right, weights, before, where):
+def pair_next(place, lefts, right, weights, before, places):
     return pair_call(
-        next_pair_kernel, where, left.shape[0], (place, left, right) + weights + (before,),
-        [vmem_spec()] * 3 + [pl.BlockSpec(memory_space=pl.ANY)],
-        [], [], [], {5: 0},
+        next_pair_kernel, places, (place,) + lefts + (right,) + weights + (before,),
+        [vmem_spec()] * 5 + [pl.BlockSpec(memory_space=pl.ANY)], [], [], {6: 0}, 1000,
     )[0]
 
 
@@ -235,31 +254,25 @@
     blocks = lax.all_to_all(packed, AXES, split_axis=0, concat_axis=0, tiled=True)
     w_sides = jnp.concatenate([w_left, w_right], axis=1).T
     w_pairs = w_pair.reshape(OPM, OPM // 2, 2, 128).transpose(2, 3, 1, 0).reshape(2, 128, 512)
-    place = jnp.stack([lax.axis_index(a) for a in ("x_lo", "y", "core")]).astype(jnp.int32)
+    place = jnp.stack([lax.axis_index(a) for a in ("x_lo", "y", "core", "x_hi", "z")]).astype(jnp.int32)
     blocks, w_even, w_odd, place = lax.optimization_barrier((blocks, w_pairs[0], w_pairs[1], place))
     weights = (w_even, w_odd)
     updated, left, right = attention(blocks, jnp.stack([w_query, w_key, w_value, w_gate, w_attend]), w_sides)
 
-    own = lax.all_to_all(right, ("x_hi", "z"), split_axis=0, concat_axis=0, tiled=True)
     near = lax.ppermute(left, AXES, crossed())[None]
-    near, own = lax.optimization_barrier((near, own))
-    own = own.reshape(HALF, SEQS)
-    other = lax.ppermute(own, "core", flipped(2, 1))
+    two = jnp.concatenate([near, lax.ppermute(near, "y", flipped(4, 1))])
+    more = lax.ppermute(two, "y", flipped(4, 3))
+    mine = right[None]
+    mine = jnp.concatenate([mine, lax.ppermute(mine, "x_hi", flipped(2, 1))])
+    pieces = (mine, lax.ppermute(mine, "z", flipped(4, 1)), lax.ppermute(mine, "z", flipped(4, 2)), lax.ppermute(mine, "z", flipped(4, 3)))
+    pieces, more, updated = lax.optimization_barrier((pieces, more, updated))
+    others = tuple(lax.ppermute(piece, "core", flipped(2, 1)) for piece in pieces)
+    updated, _ = lax.optimization_barrier((updated, others[0]))
     returned = lax.all_to_all(updated, AXES, split_axis=0, concat_axis=0, tiled=True)
-    second = lax.ppermute(near, "y", flipped(4, 2))
-    grid, rights = pair_first(place, near, own, other, weights)
-
-    second, grid = lax.optimization_barrier((second, grid))
-    two = jnp.concatenate([near, second])
-    third = lax.ppermute(two, "y", flipped(4, 1))
-    fourth = lax.ppermute(two, "x_lo", flipped(2, 1))
-    grid = pair_next(place, second, rights, weights, grid, lambda k, x_lo, y: x_lo * 4 + (y ^ 2))
-    last = lax.ppermute(third, "x_lo", flipped(2, 1))
-    grid = pair_next(place, third, rights, weights, grid, lambda k, x_lo, y: x_lo * 4 + (y ^ 1 ^ (k << 1)))
-    grid = pair_next(place, fourth, rights, weights, grid, lambda k, x_lo, y: (1 - x_lo) * 4 + (y ^ (k << 1)))
-    pair_update = pair_next(
-        place, last, rights, weights, grid, lambda k, x_lo, y: (1 - x_lo) * 4 + (y ^ 1 ^ (k << 1))
-    )
+
+    far = tuple(lax.ppermute(blocks, "x_lo", flipped(2, 1)) for blocks in (two, more))
+    grid, rights = pair_first(place, (two, more), pieces + others, weights, ((0, 0), (0, 1), (0, 3), (0, 2)))
+    pair_update = pair_next(place, far, rights, weights, grid, ((1, 0), (1, 1), (1, 3), (1, 2)))
     returned, pair_update = lax.optimization_barrier((returned, pair_update))
     alignment_out = pl.pallas_call(
         unpack_kernel, out_shape=jax.ShapeDtypeStruct(alignment.shape[1:], BF16),

time: 105 us -> 93.8 us (0.89)
  waiting for transfers between devices: 27.3 us -> 18 us
  starting transfers between devices: 34 us -> 42.3 us
  Pallas kernels: 37.4 us -> 29.2 us
  local copies, waits for them, and re-layouts: 5.12 us -> 3.18 us
    ppermute x5 -> x12, starting transfers between devices: 8.13 us -> 20.5 us  [the longest x1 5.97 us: body(): lax.ppermute(mine, 'z', flipped(4, 3))]
    all_to_all x1 -> x0, waiting for transfers between devices: 10.3 us -> none  [body(): lax.all_to_all(right, ('x_hi', 'z'), split_axis=0, concat_axis=0, tiled=T...]
    pallas_call x5 -> x2, Pallas kernels: 27.2 us -> 20.8 us  [pair_call(): pl.pallas_call(functools.partial(kernel, places), out_shape=[jax.ShapeDty...]
    all_to_all x1 -> x0, starting transfers between devices: 3.55 us -> none  [body(): lax.all_to_all(right, ('x_hi', 'z'), split_axis=0, concat_axis=0, tiled=T...]
    unnamed x25 -> x20, local copies, waits for them, and re-layouts: 3.21 us -> 1.2 us
    pallas_call x1, Pallas kernels: 8.17 us -> 6.32 us  [attention(): pl.pallas_call(attention_kernel, out_shape=(jax.ShapeDtypeStruct((SEQS, R...]
    ppermute x5 -> x12, waiting for transfers between devices: 2.88 us -> 3.87 us  [the longest x1 3.28 us: body(): lax.ppermute(mine, 'z', flipped(4, 3))]
  transfers between devices with their start and end apart: 9 -> 15, of which waited for: 3 -> 4; matrix products, arithmetic and copies ran while one was open for 2% -> 2% of each run, Pallas kernels for 26% -> 22%
where the time goes in v4:
time: 93.8 us; the launch traced here: 93.5 us
  starting transfers between devices  42.3 us (45%)
  Pallas kernels  29.2 us (31%)
  waiting for transfers between devices  18 us (19%)
  local copies, waits for them, and re-layouts  3.18 us (3%)
    pallas_call x2, Pallas kernels, pair_call(): pl.pallas_call(functools.partial(kernel, places), out_shape=[jax.ShapeDty...  20.8 us
    all_to_all x1, waiting for transfers between devices, body(): lax.all_to_all(packed, AXES, split_axis=0, concat_axis=0, tiled=True)  14.1 us
    all_to_all x1, starting transfers between devices, body(): lax.all_to_all(packed, AXES, split_axis=0, concat_axis=0, tiled=True)  11.5 us
    all_to_all x1, starting transfers between devices, body(): lax.all_to_all(updated, AXES, split_axis=0, concat_axis=0, tiled=True)  9.63 us
    pallas_call x1, Pallas kernels, attention(): pl.pallas_call(attention_kernel, out_shape=(jax.ShapeDtypeStruct((SEQS, R...  6.32 us
    ppermute x1, starting transfers between devices, body(): lax.ppermute(mine, 'z', flipped(4, 3))  5.97 us
    ppermute x1, starting transfers between devices, body(): more = lax.ppermute(two, 'y', flipped(4, 3))  4.41 us
    ppermute x1, starting transfers between devices, body(): mine = jnp.concatenate([mine, lax.ppermute(mine, 'x_hi', flipped(2, 1))])  3.37 us
  transfers between devices with their start and end apart: 15, of which 4 were waited for; matrix products, arithmetic and copies ran while one was open for 2% of the time, Pallas kernels for 22%

profile of v4, /device:TPU:1, one launch (start us, length us, event | category | flops | bytes accessed | tf_op | source)
XLA Modules:
  0.0 93.5 jit_solution(11129570876450215833)
XLA Ops:
  0.6 0.0 copy-start
  0.6 1.1 %copy-done = bf16[1,1536,256]{2,1,0:T(8,128)(2,1)S(1)} copy-done((bf16[1,1536,256]{2,1,0:T(8,128)(2,1)S(1)}, bf16[1,1536,256]{2,1,0:T(8,128)(2,1)}, u32[]{:S(2)}) %copy-start) | copy-done | bytes 786456
  1.8 0.0 copy-start.3
  1.8 0.0 copy-start.4
  1.8 1.0 %pack.1 = bf16[128,24,128]{2,1,0:T(8,128)(2,1)} custom-call(bf16[1536,256]{1,0:T(8,128)(2,1)S(1)} %bitcast.26), custom_call_target="tpu_custom_call" | custom-call | tf_op jit(solution)/shard_map/pack/pallas_call | solution.py:250
  2.8 11.5 %all-to-all-start = ((bf16[128,24,128]{2,1,0:T(8,128)(2,1)}), bf16[128,24,128]{2,1,0:T(8,128)(2,1)S(1)}, u32[]{:S(2)}, u32[]{:S(2)}) async-start(bf16[128,24,128]{2,1,0:T(8,128)(2,1)} %pack.1), calls=%async_computation | async-start | bytes 1572864 | tf_op jit(solution)/shard_map/all_to_all | solution.py:254
  14.3 1.5 %fusion = (bf16[1,128,16,32]{1,0,2,3:T(2,128)(2,1)S(1)}, bf16[1,128,16,32]{1,0,2,3:T(2,128)(2,1)S(1)}) fusion(bf16[2,128,16,32]{1,0,2,3:T(2,128)(2,1)} %bitcast.29), kind=kLoop, calls=%fused_computation.8 | loop fusion | bytes 524288 | tf_op jit(solution)/shard_map/slice | solution.py:258
  15.8 0.1 copy.18
  15.9 0.1 copy.17
  16.0 0.0 copy-done.1
  16.1 0.0 copy-done.2
  16.1 0.1 stack.41.at_ref
  16.2 0.0 copy-done.5
  16.3 14.1 %all-to-all-done.x_ref = bf16[128,24,128]{2,1,0:T(8,128)(2,1)S(1)} async-done(((bf16[128,24,128]{2,1,0:T(8,128)(2,1)}), bf16[128,24,128]{2,1,0:T(8,128)(2,1)S(1)}, u32[]{:S(2)}, u32[]{:S(2)}) %all-to-all-start) | async-done | bytes 786464 | tf_op jit(solution)/shard_map/all_to_all | solution.py:254
  30.4 6.3 %attention.1 = (bf16[128,24,128]{2,1,0:T(8,128)(2,1)}, bf16[384,128]{1,0:T(8,128)(2,1)S(1)}, bf16[384,128]{1,0:T(8,128)(2,1)S(1)}) custom-call(bf16[128,24,128]{2,1,0:T(8,128)(2,1)S(1)} %all-to-all-done.x_ref, bf16[5,256,256]{2,1,0:T(8,128)(2,1)S(1)} %bitcast_dynamic-update-slice_fusion.w_ref, bf16[64,256]{1,0:T(8,128)(2,1)S(1)} %maximum_bitcast_fusion.wlr_ref), custom_call_target="tpu_custom_call" | custom-call | tf_op jit(solution)/shard_map/attention/pallas_call | solution.py:129
  36.7 0.7 collective-permute-start.4
  37.4 3.4 %collective-permute-start = (bf16[1,384,128]{2,1,0:T(8,128)(2,1)S(1)}, bf16[1,384,128]{2,1,0:T(8,128)(2,1)S(1)}, u32[]{:S(2)}, u32[]{:S(2)}) collective-permute-start(bf16[1,384,128]{2,1,0:T(8,128)(2,1)S(1)} %bitcast.27), channel_id=1, source_target_pairs={{0,64},{64,0},{1,65},{65,1},{2,66},{66,2},{3,67},{67,3},{4,68},{68... | collective-permute-start | bytes 294920 | tf_op jit(solution)/shard_map/ppermute | solution.py:266
  40.7 0.0 collective-permute-done.4
  40.7 1.8 %collective-permute-start.5 = (bf16[1,384,128]{2,1,0:T(8,128)(2,1)S(1)}, bf16[1,384,128]{2,1,0:T(8,128)(2,1)S(1)}, u32[]{:S(2)}, u32[]{:S(2)}) collective-permute-start(bf16[1,384,128]{2,1,0:T(8,128)(2,1)S(1)} %bitcast.33), channel_id=1, source_target_pairs={{0,1},{1,0},{2,3},{3,2},{4,5},{5,4},{6,7},{7,6},{8,9},{9,8},{10,11... | collective-permute-start | bytes 294920 | tf_op jit(solution)/shard_map/ppermute | solution.py:263
  42.6 0.2 collective-permute-done
  42.8 6.0 %collective-permute-start.3 = (bf16[2,384,128]{2,1,0:T(8,128)(2,1)S(1)}, bf16[2,384,128]{2,1,0:T(8,128)(2,1)S(1)}, u32[]{:S(2)}, u32[]{:S(2)}) collective-permute-start(bf16[2,384,128]{2,1,0:T(8,128)(2,1)S(1)} %pad_maximum_fusion.refs_0_), channel_id=1, source_target_pairs={{0,48},{16,32},{32,16},{48,0},{1,49},{17,33},{33,17},{49,1},{2,50}... | collective-permute-start | bytes 589832 | tf_op jit(solution)/shard_map/ppermute | solution.py:267
  48.7 0.0 collective-permute-start.2
  48.8 0.6 collective-permute-start.1
  49.4 0.0 collective-permute-done.5
  49.4 4.4 %collective-permute-start.6 = (bf16[2,384,128]{2,1,0:T(8,128)(2,1)S(1)}, bf16[2,384,128]{2,1,0:T(8,128)(2,1)S(1)}, u32[]{:S(2)}, u32[]{:S(2)}) collective-permute-start(bf16[2,384,128]{2,1,0:T(8,128)(2,1)S(1)} %pad_maximum_fusion.1.l0_ref), channel_id=1, source_target_pairs={{0,3},{1,2},{2,1},{3,0},{4,7},{5,6},{6,5},{7,4},{8,11},{9,10},{10,... | collective-permute-start | bytes 589832 | tf_op jit(solution)/shard_map/ppermute | solution.py:264
  53.8 3.3 %collective-permute-done.3.refs_3_ = bf16[2,384,128]{2,1,0:T(8,128)(2,1)S(1)} collective-permute-done((bf16[2,384,128]{2,1,0:T(8,128)(2,1)S(1)}, bf16[2,384,128]{2,1,0:T(8,128)(2,1)S(1)}, u32[]{:S(2)}, u32[]{:S(2)}) %collective-permute-start.3) | collective-permute-done | bytes 196640 | tf_op jit(solution)/shard_map/ppermute | solution.py:267
  57.1 0.0 collective-permute-done.2.refs_2_
  57.1 0.4 collective-permute-done.1.refs_1_
  57.5 0.0 collective-permute-done.6.l1_ref
  57.5 2.2 %collective-permute-start.7 = (bf16[2,384,128]{2,1,0:T(8,128)(2,1)S(1)}, bf16[2,384,128]{2,1,0:T(8,128)(2,1)S(1)}, u32[]{:S(2)}, u32[]{:S(2)}) collective-permute-start(bf16[2,384,128]{2,1,0:T(8,128)(2,1)S(1)} %pad_maximum_fusion.refs_0_), channel_id=1, source_target_pairs={{0,8},{8,0},{1,9},{9,1},{2,10},{10,2},{3,11},{11,3},{4,12},{12,4},... | collective-permute-start | bytes 589832 | tf_op jit(solution)/shard_map/ppermute | solution.py:269
  59.7 0.0 collective-permute-start.10
  59.7 0.5 collective-permute-start.11
  60.2 0.0 collective-permute-start.12
  60.2 0.1 copy.19.refs_8_.we_ref
  60.3 0.1 copy.20.refs_9_.wo_ref
  60.5 1.3 %collective-permute-start.8 = (bf16[2,384,128]{2,1,0:T(8,128)(2,1)S(1)}, bf16[2,384,128]{2,1,0:T(8,128)(2,1)S(1)}, u32[]{:S(2)}, u32[]{:S(2)}) collective-permute-start(bf16[2,384,128]{2,1,0:T(8,128)(2,1)S(1)} %pad_maximum_fusion.1.l0_ref), channel_id=1, source_target_pairs={{0,4},{4,0},{1,5},{5,1},{2,6},{6,2},{3,7},{7,3},{8,12},{12,8},{9,1... | collective-permute-start | bytes 589832 | tf_op jit(solution)/shard_map/ppermute | solution.py:273
  61.8 0.0 collective-permute-done.7.refs_4_
  61.8 0.2 collective-permute-start.9
  62.0 9.6 %all-to-all-start.1 = ((bf16[128,24,128]{2,1,0:T(8,128)(2,1)}), bf16[128,24,128]{2,1,0:T(8,128)(2,1)S(1)}, u32[]{:S(2)}, u32[]{:S(2)}) async-start(bf16[128,24,128]{2,1,0:T(8,128)(2,1)} %get-tuple-element.26), calls=%async_computation.1 | async-start | bytes 1572864 | tf_op jit(solution)/shard_map/all_to_all | solution.py:271
  71.6 0.0 collective-permute-done.10.refs_5_
  71.7 0.0 collective-permute-done.11.refs_6_
  71.7 0.0 collective-permute-done.12.refs_7_
  71.7 10.7 %pair_grid.2 = (bf16[96,192,128]{2,1,0:T(8,128)(2,1)}, bf16[16,128,384]{2,1,0:T(8,128)(2,1)S(1)}) custom-call(s32[5]{0:T(128)S(1)} %stack.41.at_ref, bf16[2,384,128]{2,1,0:T(8,128)(2,1)S(1)} %pad_maximum_fusion.1.l0_ref, bf16[2,384,128]{2,1,0:T(8,128)(2,1)S(1)} %collective-permute-done.6.l1_ref, bf16[2,384,128]{2,1,0:T(8,128)(2,1)S(1)} %pad_maximum_fusion.refs_0_, ...), custom_call_target="tpu_custom_call" | custom-call | flops 40000000000 | bytes 1000 | tf_op jit(solution)/shard_map/pair_grid/pallas_call | solution.py:204
  82.4 0.0 collective-permute-done.8.l0_ref
  82.4 0.0 collective-permute-done.9.l1_ref
  82.4 10.0 %pair_grid.3 = bf16[96,192,128]{2,1,0:T(8,128)(2,1)} custom-call(s32[5]{0:T(128)S(1)} %stack.41.at_ref, bf16[2,384,128]{2,1,0:T(8,128)(2,1)S(1)} %collective-permute-done.8.l0_ref, bf16[2,384,128]{2,1,0:T(8,128)(2,1)S(1)} %collective-permute-done.9.l1_ref, bf16[16,128,384]{2,1,0:T(8,128)(2,1)S(1)} %get-tuple-element.34.right, ...), custom_call_target="tpu_custom_call", output_to_operand_aliasing={{}: (6, {})} | custom-call | flops 1000 | bytes 1000 | tf_op jit(solution)/shard_map/pair_grid/pallas_call | solution.py:204
  92.5 0.0 all-to-all-done.1.x_ref
  92.5 1.0 %unpack.1 = bf16[1536,256]{1,0:T(8,128)(2,1)} custom-call(bf16[128,24,128]{2,1,0:T(8,128)(2,1)S(1)} %all-to-all-done.1.x_ref), custom_call_target="tpu_custom_call" | custom-call | tf_op jit(solution)/shard_map/unpack/pallas_call | solution.py:277
  (17 shorter events, 0.1 us)
Async XLA Ops:
  0.6 1.1 %copy-start = (bf16[1,1536,256]{2,1,0:T(8,128)(2,1)S(1)}, bf16[1,1536,256]{2,1,0:T(8,128)(2,1)}, u32[]{:S(2)}) copy-start(bf16[1,1536,256]{2,1,0:T(8,128)(2,1)} %param.9) | copy-start | bytes 2359300
  1.8 14.3 %copy-start.1 = (bf16[256,256]{1,0:T(8,128)(2,1)S(1)}, bf16[256,256]{1,0:T(8,128)(2,1)}, u32[]{:S(2)}) copy-start(bf16[256,256]{1,0:T(8,128)(2,1)} %param.10) | copy-start | bytes 393220
  1.8 14.3 %copy-start.2 = (bf16[256,256]{1,0:T(8,128)(2,1)S(1)}, bf16[256,256]{1,0:T(8,128)(2,1)}, u32[]{:S(2)}) copy-start(bf16[256,256]{1,0:T(8,128)(2,1)} %param.11) | copy-start | bytes 393220
  1.8 14.4 %copy-start.6 = (bf16[256,32]{0,1:T(8,128)(2,1)S(1)}, bf16[256,32]{0,1:T(8,128)(2,1)}, u32[]{:S(2)}) copy-start(bf16[256,32]{0,1:T(8,128)(2,1)} %param.16) | copy-start | bytes 49156
  1.8 14.4 %copy-start.7 = (bf16[256,32]{0,1:T(8,128)(2,1)S(1)}, bf16[256,32]{0,1:T(8,128)(2,1)}, u32[]{:S(2)}) copy-start(bf16[256,32]{0,1:T(8,128)(2,1)} %param.15) | copy-start | bytes 49156
  1.8 14.4 %copy-start.3 = (bf16[256,256]{1,0:T(8,128)(2,1)S(1)}, bf16[256,256]{1,0:T(8,128)(2,1)}, u32[]{:S(2)}) copy-start(bf16[256,256]{1,0:T(8,128)(2,1)} %param.12) | copy-start | bytes 393220
  1.8 14.4 %copy-start.4 = (bf16[256,256]{1,0:T(8,128)(2,1)S(1)}, bf16[256,256]{1,0:T(8,128)(2,1)}, u32[]{:S(2)}) copy-start(bf16[256,256]{1,0:T(8,128)(2,1)} %param.13) | copy-start | bytes 393220
  1.8 14.4 %copy-start.5 = (bf16[256,256]{1,0:T(8,128)(2,1)S(1)}, bf16[256,256]{1,0:T(8,128)(2,1)}, u32[]{:S(2)}) copy-start(bf16[256,256]{1,0:T(8,128)(2,1)} %param.14) | copy-start | bytes 393220
  2.8 27.5 %all-to-all-start = ((bf16[128,24,128]{2,1,0:T(8,128)(2,1)}), bf16[128,24,128]{2,1,0:T(8,128)(2,1)S(1)}, u32[]{:S(2)}, u32[]{:S(2)}) async-start(bf16[128,24,128]{2,1,0:T(8,128)(2,1)} %pack.1), calls=%async_computation | async-start | bytes 1572864 | tf_op jit(solution)/shard_map/all_to_all | solution.py:254
  36.7 4.0 %collective-permute-start.4 = (bf16[384,128]{1,0:T(8,128)(2,1)S(1)}, bf16[384,128]{1,0:T(8,128)(2,1)S(1)}, u32[]{:S(2)}, u32[]{:S(2)}) collective-permute-start(bf16[384,128]{1,0:T(8,128)(2,1)S(1)} %get-tuple-element.22), channel_id=1, source_target_pairs={{0,0},{1,16},{2,32},{3,48},{4,64},{5,80},{6,96},{7,112},{8,8},{9,2... | collective-permute-start | bytes 294920 | tf_op jit(solution)/shard_map/ppermute | solution.py:262
  37.4 5.4 %collective-permute-start = (bf16[1,384,128]{2,1,0:T(8,128)(2,1)S(1)}, bf16[1,384,128]{2,1,0:T(8,128)(2,1)S(1)}, u32[]{:S(2)}, u32[]{:S(2)}) collective-permute-start(bf16[1,384,128]{2,1,0:T(8,128)(2,1)S(1)} %bitcast.27), channel_id=1, source_target_pairs={{0,64},{64,0},{1,65},{65,1},{2,66},{66,2},{3,67},{67,3},{4,68},{68... | collective-permute-start | bytes 294920 | tf_op jit(solution)/shard_map/ppermute | solution.py:266
  40.7 8.7 %collective-permute-start.5 = (bf16[1,384,128]{2,1,0:T(8,128)(2,1)S(1)}, bf16[1,384,128]{2,1,0:T(8,128)(2,1)S(1)}, u32[]{:S(2)}, u32[]{:S(2)}) collective-permute-start(bf16[1,384,128]{2,1,0:T(8,128)(2,1)S(1)} %bitcast.33), channel_id=1, source_target_pairs={{0,1},{1,0},{2,3},{3,2},{4,5},{5,4},{6,7},{7,6},{8,9},{9,8},{10,11... | collective-permute-start | bytes 294920 | tf_op jit(solution)/shard_map/ppermute | solution.py:263
  42.8 14.4 %collective-permute-start.3 = (bf16[2,384,128]{2,1,0:T(8,128)(2,1)S(1)}, bf16[2,384,128]{2,1,0:T(8,128)(2,1)S(1)}, u32[]{:S(2)}, u32[]{:S(2)}) collective-permute-start(bf16[2,384,128]{2,1,0:T(8,128)(2,1)S(1)} %pad_maximum_fusion.refs_0_), channel_id=1, source_target_pairs={{0,48},{16,32},{32,16},{48,0},{1,49},{17,33},{33,17},{49,1},{2,50}... | collective-permute-start | bytes 589832 | tf_op jit(solution)/shard_map/ppermute | solution.py:267
  48.7 8.4 %collective-permute-start.2 = (bf16[2,384,128]{2,1,0:T(8,128)(2,1)S(1)}, bf16[2,384,128]{2,1,0:T(8,128)(2,1)S(1)}, u32[]{:S(2)}, u32[]{:S(2)}) collective-permute-start(bf16[2,384,128]{2,1,0:T(8,128)(2,1)S(1)} %pad_maximum_fusion.refs_0_), channel_id=1, source_target_pairs={{0,32},{16,48},{32,0},{48,16},{1,33},{17,49},{33,1},{49,17},{2,34}... | collective-permute-start | bytes 589832 | tf_op jit(solution)/shard_map/ppermute | solution.py:267
  48.8 8.7 %collective-permute-start.1 = (bf16[2,384,128]{2,1,0:T(8,128)(2,1)S(1)}, bf16[2,384,128]{2,1,0:T(8,128)(2,1)S(1)}, u32[]{:S(2)}, u32[]{:S(2)}) collective-permute-start(bf16[2,384,128]{2,1,0:T(8,128)(2,1)S(1)} %pad_maximum_fusion.refs_0_), channel_id=1, source_target_pairs={{0,16},{16,0},{32,48},{48,32},{1,17},{17,1},{33,49},{49,33},{2,18}... | collective-permute-start | bytes 589832 | tf_op jit(solution)/shard_map/ppermute | solution.py:267
  49.4 8.1 %collective-permute-start.6 = (bf16[2,384,128]{2,1,0:T(8,128)(2,1)S(1)}, bf16[2,384,128]{2,1,0:T(8,128)(2,1)S(1)}, u32[]{:S(2)}, u32[]{:S(2)}) collective-permute-start(bf16[2,384,128]{2,1,0:T(8,128)(2,1)S(1)} %pad_maximum_fusion.1.l0_ref), channel_id=1, source_target_pairs={{0,3},{1,2},{2,1},{3,0},{4,7},{5,6},{6,5},{7,4},{8,11},{9,10},{10,... | collective-permute-start | bytes 589832 | tf_op jit(solution)/shard_map/ppermute | solution.py:264
  57.5 4.3 %collective-permute-start.7 = (bf16[2,384,128]{2,1,0:T(8,128)(2,1)S(1)}, bf16[2,384,128]{2,1,0:T(8,128)(2,1)S(1)}, u32[]{:S(2)}, u32[]{:S(2)}) collective-permute-start(bf16[2,384,128]{2,1,0:T(8,128)(2,1)S(1)} %pad_maximum_fusion.refs_0_), channel_id=1, source_target_pairs={{0,8},{8,0},{1,9},{9,1},{2,10},{10,2},{3,11},{11,3},{4,12},{12,4},... | collective-permute-start | bytes 589832 | tf_op jit(solution)/shard_map/ppermute | solution.py:269
  59.7 11.9 %collective-permute-start.10 = (bf16[2,384,128]{2,1,0:T(8,128)(2,1)S(1)}, bf16[2,384,128]{2,1,0:T(8,128)(2,1)S(1)}, u32[]{:S(2)}, u32[]{:S(2)}) collective-permute-start(bf16[2,384,128]{2,1,0:T(8,128)(2,1)S(1)} %collective-permute-done.1.refs_1_), channel_id=1, source_target_pairs={{0,8},{8,0},{1,9},{9,1},{2,10},{10,2},{3,11},{11,3},{4,12},{12,4},... | collective-permute-start | bytes 589832 | tf_op jit(solution)/shard_map/ppermute | solution.py:269
  59.7 12.0 %collective-permute-start.11 = (bf16[2,384,128]{2,1,0:T(8,128)(2,1)S(1)}, bf16[2,384,128]{2,1,0:T(8,128)(2,1)S(1)}, u32[]{:S(2)}, u32[]{:S(2)}) collective-permute-start(bf16[2,384,128]{2,1,0:T(8,128)(2,1)S(1)} %collective-permute-done.2.refs_2_), channel_id=1, source_target_pairs={{0,8},{8,0},{1,9},{9,1},{2,10},{10,2},{3,11},{11,3},{4,12},{12,4},... | collective-permute-start | bytes 589832 | tf_op jit(solution)/shard_map/ppermute | solution.py:269
  60.2 11.5 %collective-permute-start.12 = (bf16[2,384,128]{2,1,0:T(8,128)(2,1)S(1)}, bf16[2,384,128]{2,1,0:T(8,128)(2,1)S(1)}, u32[]{:S(2)}, u32[]{:S(2)}) collective-permute-start(bf16[2,384,128]{2,1,0:T(8,128)(2,1)S(1)} %collective-permute-done.3.refs_3_), channel_id=1, source_target_pairs={{0,8},{8,0},{1,9},{9,1},{2,10},{10,2},{3,11},{11,3},{4,12},{12,4},... | collective-permute-start | bytes 589832 | tf_op jit(solution)/shard_map/ppermute | solution.py:269
  60.5 22.0 %collective-permute-start.8 = (bf16[2,384,128]{2,1,0:T(8,128)(2,1)S(1)}, bf16[2,384,128]{2,1,0:T(8,128)(2,1)S(1)}, u32[]{:S(2)}, u32[]{:S(2)}) collective-permute-start(bf16[2,384,128]{2,1,0:T(8,128)(2,1)S(1)} %pad_maximum_fusion.1.l0_ref), channel_id=1, source_target_pairs={{0,4},{4,0},{1,5},{5,1},{2,6},{6,2},{3,7},{7,3},{8,12},{12,8},{9,1... | collective-permute-start | bytes 589832 | tf_op jit(solution)/shard_map/ppermute | solution.py:273
  61.8 20.7 %collective-permute-start.9 = (bf16[2,384,128]{2,1,0:T(8,128)(2,1)S(1)}, bf16[2,384,128]{2,1,0:T(8,128)(2,1)S(1)}, u32[]{:S(2)}, u32[]{:S(2)}) collective-permute-start(bf16[2,384,128]{2,1,0:T(8,128)(2,1)S(1)} %collective-permute-done.6.l1_ref), channel_id=1, source_target_pairs={{0,4},{4,0},{1,5},{5,1},{2,6},{6,2},{3,7},{7,3},{8,12},{12,8},{9,1... | collective-permute-start | bytes 589832 | tf_op jit(solution)/shard_map/ppermute | solution.py:273
  62.0 30.5 %all-to-all-start.1 = ((bf16[128,24,128]{2,1,0:T(8,128)(2,1)}), bf16[128,24,128]{2,1,0:T(8,128)(2,1)S(1)}, u32[]{:S(2)}, u32[]{:S(2)}) async-start(bf16[128,24,128]{2,1,0:T(8,128)(2,1)} %get-tuple-element.26), calls=%async_computation.1 | async-start | bytes 1572864 | tf_op jit(solution)/shard_map/all_to_all | solution.py:271

commit v5 on v4

--- a/solution.py
+++ b/solution.py
@@ -181,7 +181,7 @@
         copy.wait()
 
 
-def first_pair_kernel(places, at_ref, l0_ref, l1_ref, *refs):
+def first_pair_kernel(places, at_ref, l_ref, *refs):
     pieces, (we_ref, wo_ref, out_ref, right, flat, outer, rows, sems) = refs[:8], refs[8:]
     step = BLK * OPM
     for n, piece in enumerate(pieces):
@@ -192,11 +192,12 @@
         even = flat[pl.ds(2 * p, COLS, stride=OPM), :]
         odd = flat[pl.ds(2 * p + 1, COLS, stride=OPM), :]
         right[p] = jnp.concatenate([even, odd], axis=0).T.astype(BF16)
-    pair_rows(at_ref, places, (l0_ref, l1_ref), right, we_ref, wo_ref, out_ref, outer, rows, sems)
-
-
-def next_pair_kernel(places, at_ref, l0_ref, l1_ref, right, we_ref, wo_ref, before_ref, out_ref, outer, rows, sems):
-    pair_rows(at_ref, places, (l0_ref, l1_ref), right, we_ref, wo_ref, out_ref, outer, rows, sems)
+    pair_rows(at_ref, places, (l_ref,), right, we_ref, wo_ref, out_ref, outer, rows, sems)
+
+
+def next_pair_kernel(places, at_ref, *refs):
+    l_refs, (right, we_ref, wo_ref, before_ref, out_ref, outer, rows, sems) = refs[:-8], refs[-8:]
+    pair_rows(at_ref, places, l_refs, right, we_ref, wo_ref, out_ref, outer, rows, sems)
 
 
 def pair_call(kernel, places, operands, in_specs, extra_shapes, scratch, aliases, flops):
@@ -221,7 +222,7 @@
 
 def pair_first(place, lefts, pieces, weights, places):
     return pair_call(
-        first_pair_kernel, places, (place,) + lefts + pieces + weights, [vmem_spec()] * 12,
+        first_pair_kernel, places, (place, lefts) + pieces + weights, [vmem_spec()] * 11,
         [jax.ShapeDtypeStruct((OPM // 2, SEQS, 384), BF16)], [pltpu.VMEM((2 * HALF, SEQS), F32)], {}, 40_000_000_000,
     )
 
@@ -229,7 +230,7 @@
 def pair_next(place, lefts, right, weights, before, places):
     return pair_call(
         next_pair_kernel, places, (place,) + lefts + (right,) + weights + (before,),
-        [vmem_spec()] * 5 + [pl.BlockSpec(memory_space=pl.ANY)], [], [], {6: 0}, 1000,
+        [vmem_spec()] * (3 + len(lefts)) + [pl.BlockSpec(memory_space=pl.ANY)], [], [], {4 + len(lefts): 0}, 1000,
     )[0]
 
 
@@ -260,19 +261,23 @@
     updated, left, right = attention(blocks, jnp.stack([w_query, w_key, w_value, w_gate, w_attend]), w_sides)
 
     near = lax.ppermute(left, AXES, crossed())[None]
-    two = jnp.concatenate([near, lax.ppermute(near, "y", flipped(4, 1))])
-    more = lax.ppermute(two, "y", flipped(4, 3))
+    second = lax.ppermute(near, "y", flipped(4, 1))
     mine = right[None]
     mine = jnp.concatenate([mine, lax.ppermute(mine, "x_hi", flipped(2, 1))])
     pieces = (mine, lax.ppermute(mine, "z", flipped(4, 1)), lax.ppermute(mine, "z", flipped(4, 2)), lax.ppermute(mine, "z", flipped(4, 3)))
-    pieces, more, updated = lax.optimization_barrier((pieces, more, updated))
+    pieces, second, updated = lax.optimization_barrier((pieces, second, updated))
     others = tuple(lax.ppermute(piece, "core", flipped(2, 1)) for piece in pieces)
     updated, _ = lax.optimization_barrier((updated, others[0]))
     returned = lax.all_to_all(updated, AXES, split_axis=0, concat_axis=0, tiled=True)
 
-    far = tuple(lax.ppermute(blocks, "x_lo", flipped(2, 1)) for blocks in (two, more))
-    grid, rights = pair_first(place, (two, more), pieces + others, weights, ((0, 0), (0, 1), (0, 3), (0, 2)))
-    pair_update = pair_next(place, far, rights, weights, grid, ((1, 0), (1, 1), (1, 3), (1, 2)))
+    two = jnp.concatenate([near, second])
+    more = lax.ppermute(two, "y", flipped(4, 3))
+    far = lax.ppermute(two, "x_lo", flipped(2, 1))
+    grid, rights = pair_first(place, two, pieces + others, weights, ((0, 0), (0, 1)))
+    more, grid = lax.optimization_barrier((more, grid))
+    last = lax.ppermute(more, "x_lo", flipped(2, 1))
+    grid = pair_next(place, (more, far), rights, weights, grid, ((0, 3), (0, 2), (1, 0), (1, 1)))
+    pair_update = pair_next(place, (last,), rights, weights, grid, ((1, 3), (1, 2)))
     returned, pair_update = lax.optimization_barrier((returned, pair_update))
     alignment_out = pl.pallas_call(
         unpack_kernel, out_shape=jax.ShapeDtypeStruct(alignment.shape[1:], BF16),

time: 93.8 us -> 90.9 us (0.969)
  starting transfers between devices: 42.3 us -> 30.1 us
  waiting for transfers between devices: 18 us -> 25.9 us
  Pallas kernels: 29.2 us -> 30.5 us
    ppermute x1, starting transfers between devices: 5.97 us -> 1.4 us  [body(): lax.ppermute(mine, 'z', flipped(4, 3))]
    all_to_all x1, starting transfers between devices: 9.63 us -> 5.4 us  [body(): lax.all_to_all(updated, AXES, split_axis=0, concat_axis=0, tiled=True)]
    ppermute x1, waiting for transfers between devices: 0.19 us -> 4 us  [body(): mine = jnp.concatenate([mine, lax.ppermute(mine, 'x_hi', flipped(2, 1))])]
    ppermute x3, waiting for transfers between devices: 0.01 us -> 3.47 us  [the longest x1 3.46 us: body(): second = lax.ppermute(near, 'y', flipped(4, 1))]
    ppermute x1, starting transfers between devices: 3.37 us -> 0.31 us  [body(): mine = jnp.concatenate([mine, lax.ppermute(mine, 'x_hi', flipped(2, 1))])]
    ppermute x1, starting transfers between devices: 4.41 us -> 2.73 us  [body(): more = lax.ppermute(two, 'y', flipped(4, 3))]
    pallas_call x2 -> x3, Pallas kernels: 20.8 us -> 22.1 us  [pair_call(): pl.pallas_call(functools.partial(kernel, places), out_shape=[jax.ShapeDty...]
    ppermute x1, starting transfers between devices: 0.02 us -> 1.32 us  [body(): lax.ppermute(mine, 'z', flipped(4, 2))]
  transfers between devices with their start and end apart: 15 -> 15, of which waited for: 4 -> 5; matrix products, arithmetic and copies ran while one was open for 2% -> 2% of each run, Pallas kernels for 22% -> 24%
where the time goes in v5:
time: 90.9 us; the launch traced here: 90.6 us
  Pallas kernels  30.5 us (34%)
  starting transfers between devices  30.1 us (33%)
  waiting for transfers between devices  25.9 us (28%)
  local copies, waits for them, and re-layouts  3.18 us (3%)
  between operations  0.91 us (1%)
    pallas_call x3, Pallas kernels, pair_call(): pl.pallas_call(functools.partial(kernel, places), out_shape=[jax.ShapeDty...  22.1 us
    all_to_all x1, waiting for transfers between devices, body(): lax.all_to_all(packed, AXES, split_axis=0, concat_axis=0, tiled=True)  14.1 us
    all_to_all x1, starting transfers between devices, body(): lax.all_to_all(packed, AXES, split_axis=0, concat_axis=0, tiled=True)  11.5 us
    pallas_call x1, Pallas kernels, attention(): pl.pallas_call(attention_kernel, out_shape=(jax.ShapeDtypeStruct((SEQS, R...  6.32 us
    all_to_all x1, starting transfers between devices, body(): lax.all_to_all(updated, AXES, split_axis=0, concat_axis=0, tiled=True)  5.4 us
    ppermute x1, waiting for transfers between devices, body(): mine = jnp.concatenate([mine, lax.ppermute(mine, 'x_hi', flipped(2, 1))])  4 us
    ppermute x1, waiting for transfers between devices, body(): second = lax.ppermute(near, 'y', flipped(4, 1))  3.46 us
    ppermute x4, starting transfers between devices, body(): lax.ppermute(piece, 'core', flipped(2, 1))  3.1 us
  transfers between devices with their start and end apart: 15, of which 5 were waited for; matrix products, arithmetic and copies ran while one was open for 2% of the time, Pallas kernels for 24%

profile of v5, /device:TPU:1, one launch (start us, length us, event | category | flops | bytes accessed | tf_op | source)
XLA Modules:
  0.0 90.6 jit_solution(6332929662215211215)
XLA Ops:
  0.6 0.0 copy-start
  0.6 1.1 %copy-done = bf16[1,1536,256]{2,1,0:T(8,128)(2,1)S(1)} copy-done((bf16[1,1536,256]{2,1,0:T(8,128)(2,1)S(1)}, bf16[1,1536,256]{2,1,0:T(8,128)(2,1)}, u32[]{:S(2)}) %copy-start) | copy-done | bytes 786456
  1.8 0.0 copy-start.3
  1.8 0.0 copy-start.4
  1.8 1.0 %pack.1 = bf16[128,24,128]{2,1,0:T(8,128)(2,1)} custom-call(bf16[1536,256]{1,0:T(8,128)(2,1)S(1)} %bitcast.26), custom_call_target="tpu_custom_call" | custom-call | tf_op jit(solution)/shard_map/pack/pallas_call | solution.py:251
  2.8 11.5 %all-to-all-start = ((bf16[128,24,128]{2,1,0:T(8,128)(2,1)}), bf16[128,24,128]{2,1,0:T(8,128)(2,1)S(1)}, u32[]{:S(2)}, u32[]{:S(2)}) async-start(bf16[128,24,128]{2,1,0:T(8,128)(2,1)} %pack.1), calls=%async_computation | async-start | bytes 1572864 | tf_op jit(solution)/shard_map/all_to_all | solution.py:255
  14.3 1.5 %fusion = (bf16[1,128,16,32]{1,0,2,3:T(2,128)(2,1)S(1)}, bf16[1,128,16,32]{1,0,2,3:T(2,128)(2,1)S(1)}) fusion(bf16[2,128,16,32]{1,0,2,3:T(2,128)(2,1)} %bitcast.29), kind=kLoop, calls=%fused_computation.8 | loop fusion | bytes 524288 | tf_op jit(solution)/shard_map/slice | solution.py:259
  15.8 0.1 copy.21
  15.9 0.1 copy.20
  16.1 0.1 stack.41.at_ref
  16.2 0.0 copy-done.7
  16.2 0.0 copy-done.3
  16.3 14.1 %all-to-all-done.x_ref = bf16[128,24,128]{2,1,0:T(8,128)(2,1)S(1)} async-done(((bf16[128,24,128]{2,1,0:T(8,128)(2,1)}), bf16[128,24,128]{2,1,0:T(8,128)(2,1)S(1)}, u32[]{:S(2)}, u32[]{:S(2)}) %all-to-all-start) | async-done | bytes 786464 | tf_op jit(solution)/shard_map/all_to_all | solution.py:255
  30.4 6.3 %attention.1 = (bf16[128,24,128]{2,1,0:T(8,128)(2,1)}, bf16[384,128]{1,0:T(8,128)(2,1)S(1)}, bf16[384,128]{1,0:T(8,128)(2,1)S(1)}) custom-call(bf16[128,24,128]{2,1,0:T(8,128)(2,1)S(1)} %all-to-all-done.x_ref, bf16[5,256,256]{2,1,0:T(8,128)(2,1)S(1)} %bitcast_dynamic-update-slice_fusion.w_ref, bf16[64,256]{1,0:T(8,128)(2,1)S(1)} %maximum_bitcast_fusion.wlr_ref), custom_call_target="tpu_custom_call" | custom-call | tf_op jit(solution)/shard_map/attention/pallas_call | solution.py:129
  36.7 0.3 collective-permute-start
  37.0 0.7 collective-permute-start.4
  37.7 4.0 %collective-permute-done = bf16[1,384,128]{2,1,0:T(8,128)(2,1)S(1)} collective-permute-done((bf16[1,384,128]{2,1,0:T(8,128)(2,1)S(1)}, bf16[1,384,128]{2,1,0:T(8,128)(2,1)S(1)}, u32[]{:S(2)}, u32[]{:S(2)}) %collective-permute-start) | collective-permute-done | bytes 98336 | tf_op jit(solution)/shard_map/ppermute | solution.py:266
  41.7 1.4 %collective-permute-start.3 = (bf16[2,384,128]{2,1,0:T(8,128)(2,1)S(1)}, bf16[2,384,128]{2,1,0:T(8,128)(2,1)S(1)}, u32[]{:S(2)}, u32[]{:S(2)}) collective-permute-start(bf16[2,384,128]{2,1,0:T(8,128)(2,1)S(1)} %pad_maximum_fusion.refs_0_), channel_id=1, source_target_pairs={{0,48},{16,32},{32,16},{48,0},{1,49},{17,33},{33,17},{49,1},{2,50}... | collective-permute-start | bytes 589832 | tf_op jit(solution)/shard_map/ppermute | solution.py:267
  43.1 1.3 %collective-permute-start.2 = (bf16[2,384,128]{2,1,0:T(8,128)(2,1)S(1)}, bf16[2,384,128]{2,1,0:T(8,128)(2,1)S(1)}, u32[]{:S(2)}, u32[]{:S(2)}) collective-permute-start(bf16[2,384,128]{2,1,0:T(8,128)(2,1)S(1)} %pad_maximum_fusion.refs_0_), channel_id=1, source_target_pairs={{0,32},{16,48},{32,0},{48,16},{1,33},{17,49},{33,1},{49,17},{2,34}... | collective-permute-start | bytes 589832 | tf_op jit(solution)/shard_map/ppermute | solution.py:267
  44.4 0.6 collective-permute-start.1
  45.0 0.0 collective-permute-done.4
  45.0 0.0 collective-permute-start.5
  45.0 3.5 %collective-permute-done.5 = bf16[1,384,128]{2,1,0:T(8,128)(2,1)S(1)} collective-permute-done((bf16[1,384,128]{2,1,0:T(8,128)(2,1)S(1)}, bf16[1,384,128]{2,1,0:T(8,128)(2,1)S(1)}, u32[]{:S(2)}, u32[]{:S(2)}) %collective-permute-start.5) | collective-permute-done | bytes 98336 | tf_op jit(solution)/shard_map/ppermute | solution.py:264
  48.5 2.9 %collective-permute-done.3.refs_3_ = bf16[2,384,128]{2,1,0:T(8,128)(2,1)S(1)} collective-permute-done((bf16[2,384,128]{2,1,0:T(8,128)(2,1)S(1)}, bf16[2,384,128]{2,1,0:T(8,128)(2,1)S(1)}, u32[]{:S(2)}, u32[]{:S(2)}) %collective-permute-start.3) | collective-permute-done | bytes 196640 | tf_op jit(solution)/shard_map/ppermute | solution.py:267
  51.4 0.0 collective-permute-done.2.refs_2_
  51.4 1.4 %collective-permute-done.1.refs_1_ = bf16[2,384,128]{2,1,0:T(8,128)(2,1)S(1)} collective-permute-done((bf16[2,384,128]{2,1,0:T(8,128)(2,1)S(1)}, bf16[2,384,128]{2,1,0:T(8,128)(2,1)S(1)}, u32[]{:S(2)}, u32[]{:S(2)}) %collective-permute-start.1) | collective-permute-done | bytes 196640 | tf_op jit(solution)/shard_map/ppermute | solution.py:267
  52.8 2.6 %collective-permute-start.6 = (bf16[2,384,128]{2,1,0:T(8,128)(2,1)S(1)}, bf16[2,384,128]{2,1,0:T(8,128)(2,1)S(1)}, u32[]{:S(2)}, u32[]{:S(2)}) collective-permute-start(bf16[2,384,128]{2,1,0:T(8,128)(2,1)S(1)} %pad_maximum_fusion.refs_0_), channel_id=1, source_target_pairs={{0,8},{8,0},{1,9},{9,1},{2,10},{10,2},{3,11},{11,3},{4,12},{12,4},... | collective-permute-start | bytes 589832 | tf_op jit(solution)/shard_map/ppermute | solution.py:269
  55.4 0.0 collective-permute-start.8
  55.4 0.5 collective-permute-start.9
  55.9 0.0 collective-permute-start.10
  55.9 0.1 copy.22.refs_8_.refs_3_.refs_2_
  56.0 0.1 copy.23.refs_9_.refs_4_.refs_3_
  56.2 1.6 %collective-permute-start.12 = (bf16[2,384,128]{2,1,0:T(8,128)(2,1)S(1)}, bf16[2,384,128]{2,1,0:T(8,128)(2,1)S(1)}, u32[]{:S(2)}, u32[]{:S(2)}) collective-permute-start(bf16[2,384,128]{2,1,0:T(8,128)(2,1)S(1)} %pad_maximum_fusion.1.l_ref), channel_id=1, source_target_pairs={{0,4},{4,0},{1,5},{5,1},{2,6},{6,2},{3,7},{7,3},{8,12},{12,8},{9,1... | collective-permute-start | bytes 589832 | tf_op jit(solution)/shard_map/ppermute | solution.py:275
  57.8 0.0 collective-permute-done.6.refs_4_
  57.8 2.7 %collective-permute-start.7 = (bf16[2,384,128]{2,1,0:T(8,128)(2,1)S(1)}, bf16[2,384,128]{2,1,0:T(8,128)(2,1)S(1)}, u32[]{:S(2)}, u32[]{:S(2)}) collective-permute-start(bf16[2,384,128]{2,1,0:T(8,128)(2,1)S(1)} %pad_maximum_fusion.1.l_ref), channel_id=1, source_target_pairs={{0,3},{1,2},{2,1},{3,0},{4,7},{5,6},{6,5},{7,4},{8,11},{9,10},{10,... | collective-permute-start | bytes 589832 | tf_op jit(solution)/shard_map/ppermute | solution.py:274
  60.5 5.4 %all-to-all-start.1 = ((bf16[128,24,128]{2,1,0:T(8,128)(2,1)}), bf16[128,24,128]{2,1,0:T(8,128)(2,1)S(1)}, u32[]{:S(2)}, u32[]{:S(2)}) async-start(bf16[128,24,128]{2,1,0:T(8,128)(2,1)} %get-tuple-element.28), calls=%async_computation.1 | async-start | bytes 1572864 | tf_op jit(solution)/shard_map/all_to_all | solution.py:271
  65.9 0.0 collective-permute-done.8.refs_5_
  66.0 0.0 collective-permute-done.9.refs_6_
  66.0 0.0 collective-permute-done.10.refs_7_
  66.0 6.6 %pair_grid.3 = (bf16[96,192,128]{2,1,0:T(8,128)(2,1)}, bf16[16,128,384]{2,1,0:T(8,128)(2,1)S(1)}) custom-call(s32[5]{0:T(128)S(1)} %stack.41.at_ref, bf16[2,384,128]{2,1,0:T(8,128)(2,1)S(1)} %pad_maximum_fusion.1.l_ref, bf16[2,384,128]{2,1,0:T(8,128)(2,1)S(1)} %pad_maximum_fusion.refs_0_, bf16[2,384,128]{2,1,0:T(8,128)(2,1)S(1)} %collective-permute-done.1.refs_1_, ...), custom_call_target="tpu_custom_call" | custom-call | flops 40000000000 | bytes 1000 | tf_op jit(solution)/shard_map/pair_grid/pallas_call | solution.py:205
  72.6 0.0 collective-permute-done.7.refs_0_
  72.6 1.5 %collective-permute-start.11 = (bf16[2,384,128]{2,1,0:T(8,128)(2,1)S(1)}, bf16[2,384,128]{2,1,0:T(8,128)(2,1)S(1)}, u32[]{:S(2)}, u32[]{:S(2)}) collective-permute-start(bf16[2,384,128]{2,1,0:T(8,128)(2,1)S(1)} %collective-permute-done.7.refs_0_), channel_id=1, source_target_pairs={{0,4},{4,0},{1,5},{5,1},{2,6},{6,2},{3,7},{7,3},{8,12},{12,8},{9,1... | collective-permute-start | bytes 589832 | tf_op jit(solution)/shard_map/ppermute | solution.py:278
  74.1 0.0 collective-permute-done.12.refs_1_
  74.1 9.8 %pair_grid.4.refs_4_ = bf16[96,192,128]{2,1,0:T(8,128)(2,1)} custom-call(s32[5]{0:T(128)S(1)} %stack.41.at_ref, bf16[2,384,128]{2,1,0:T(8,128)(2,1)S(1)} %collective-permute-done.7.refs_0_, bf16[2,384,128]{2,1,0:T(8,128)(2,1)S(1)} %collective-permute-done.12.refs_1_, ...), custom_call_target="tpu_custom_call", output_to_operand_aliasing={{}: (6, {})} | custom-call | flops 1000 | bytes 1000 | tf_op jit(solution)/shard_map/pair_grid/pallas_call | solution.py:205
  83.9 0.0 collective-permute-done.11.refs_0_
  83.9 5.7 %pair_grid.5 = bf16[96,192,128]{2,1,0:T(8,128)(2,1)} custom-call(s32[5]{0:T(128)S(1)} %stack.41.at_ref, bf16[2,384,128]{2,1,0:T(8,128)(2,1)S(1)} %collective-permute-done.11.refs_0_, bf16[16,128,384]{2,1,0:T(8,128)(2,1)S(1)} %get-tuple-element.38.refs_2_.refs_1_, bf16[128,512]{1,0:T(8,128)(2,1)S(1)} %copy.22.refs_8_.refs_3_.refs_2_, ...), custom_call_target="tpu_custom_call", output_to_operand_aliasing={{}: (5, {})} | custom-call | flops 1000 | bytes 1000 | tf_op jit(solution)/shard_map/pair_grid/pallas_call | solution.py:205
  89.6 0.0 all-to-all-done.1.x_ref
  89.6 1.0 %unpack.1 = bf16[1536,256]{1,0:T(8,128)(2,1)} custom-call(bf16[128,24,128]{2,1,0:T(8,128)(2,1)S(1)} %all-to-all-done.1.x_ref), custom_call_target="tpu_custom_call" | custom-call | tf_op jit(solution)/shard_map/unpack/pallas_call | solution.py:282
  (18 shorter events, 0.1 us)
Async XLA Ops:
  0.6 1.1 %copy-start = (bf16[1,1536,256]{2,1,0:T(8,128)(2,1)S(1)}, bf16[1,1536,256]{2,1,0:T(8,128)(2,1)}, u32[]{:S(2)}) copy-start(bf16[1,1536,256]{2,1,0:T(8,128)(2,1)} %param.9) | copy-start | bytes 2359300
  1.8 14.3 %copy-start.1 = (bf16[256,256]{1,0:T(8,128)(2,1)S(1)}, bf16[256,256]{1,0:T(8,128)(2,1)}, u32[]{:S(2)}) copy-start(bf16[256,256]{1,0:T(8,128)(2,1)} %param.10) | copy-start | bytes 393220
  1.8 14.3 %copy-start.2 = (bf16[256,256]{1,0:T(8,128)(2,1)S(1)}, bf16[256,256]{1,0:T(8,128)(2,1)}, u32[]{:S(2)}) copy-start(bf16[256,256]{1,0:T(8,128)(2,1)} %param.11) | copy-start | bytes 393220
  1.8 14.4 %copy-start.6 = (bf16[256,32]{0,1:T(8,128)(2,1)S(1)}, bf16[256,32]{0,1:T(8,128)(2,1)}, u32[]{:S(2)}) copy-start(bf16[256,32]{0,1:T(8,128)(2,1)} %param.16) | copy-start | bytes 49156
  1.8 14.4 %copy-start.7 = (bf16[256,32]{0,1:T(8,128)(2,1)S(1)}, bf16[256,32]{0,1:T(8,128)(2,1)}, u32[]{:S(2)}) copy-start(bf16[256,32]{0,1:T(8,128)(2,1)} %param.15) | copy-start | bytes 49156
  1.8 14.4 %copy-start.3 = (bf16[256,256]{1,0:T(8,128)(2,1)S(1)}, bf16[256,256]{1,0:T(8,128)(2,1)}, u32[]{:S(2)}) copy-start(bf16[256,256]{1,0:T(8,128)(2,1)} %param.12) | copy-start | bytes 393220
  1.8 14.4 %copy-start.4 = (bf16[256,256]{1,0:T(8,128)(2,1)S(1)}, bf16[256,256]{1,0:T(8,128)(2,1)}, u32[]{:S(2)}) copy-start(bf16[256,256]{1,0:T(8,128)(2,1)} %param.13) | copy-start | bytes 393220
  1.8 14.4 %copy-start.5 = (bf16[256,256]{1,0:T(8,128)(2,1)S(1)}, bf16[256,256]{1,0:T(8,128)(2,1)}, u32[]{:S(2)}) copy-start(bf16[256,256]{1,0:T(8,128)(2,1)} %param.14) | copy-start | bytes 393220
  2.8 27.5 %all-to-all-start = ((bf16[128,24,128]{2,1,0:T(8,128)(2,1)}), bf16[128,24,128]{2,1,0:T(8,128)(2,1)S(1)}, u32[]{:S(2)}, u32[]{:S(2)}) async-start(bf16[128,24,128]{2,1,0:T(8,128)(2,1)} %pack.1), calls=%async_computation | async-start | bytes 1572864 | tf_op jit(solution)/shard_map/all_to_all | solution.py:255
  36.7 5.0 %collective-permute-start = (bf16[1,384,128]{2,1,0:T(8,128)(2,1)S(1)}, bf16[1,384,128]{2,1,0:T(8,128)(2,1)S(1)}, u32[]{:S(2)}, u32[]{:S(2)}) collective-permute-start(bf16[1,384,128]{2,1,0:T(8,128)(2,1)S(1)} %bitcast.27), channel_id=1, source_target_pairs={{0,64},{64,0},{1,65},{65,1},{2,66},{66,2},{3,67},{67,3},{4,68},{68... | collective-permute-start | bytes 294920 | tf_op jit(solution)/shard_map/ppermute | solution.py:266
  37.0 8.0 %collective-permute-start.4 = (bf16[384,128]{1,0:T(8,128)(2,1)S(1)}, bf16[384,128]{1,0:T(8,128)(2,1)S(1)}, u32[]{:S(2)}, u32[]{:S(2)}) collective-permute-start(bf16[384,128]{1,0:T(8,128)(2,1)S(1)} %get-tuple-element.24), channel_id=1, source_target_pairs={{0,0},{1,16},{2,32},{3,48},{4,64},{5,80},{6,96},{7,112},{8,8},{9,2... | collective-permute-start | bytes 294920 | tf_op jit(solution)/shard_map/ppermute | solution.py:263
  41.7 9.7 %collective-permute-start.3 = (bf16[2,384,128]{2,1,0:T(8,128)(2,1)S(1)}, bf16[2,384,128]{2,1,0:T(8,128)(2,1)S(1)}, u32[]{:S(2)}, u32[]{:S(2)}) collective-permute-start(bf16[2,384,128]{2,1,0:T(8,128)(2,1)S(1)} %pad_maximum_fusion.refs_0_), channel_id=1, source_target_pairs={{0,48},{16,32},{32,16},{48,0},{1,49},{17,33},{33,17},{49,1},{2,50}... | collective-permute-start | bytes 589832 | tf_op jit(solution)/shard_map/ppermute | solution.py:267
  43.1 8.3 %collective-permute-start.2 = (bf16[2,384,128]{2,1,0:T(8,128)(2,1)S(1)}, bf16[2,384,128]{2,1,0:T(8,128)(2,1)S(1)}, u32[]{:S(2)}, u32[]{:S(2)}) collective-permute-start(bf16[2,384,128]{2,1,0:T(8,128)(2,1)S(1)} %pad_maximum_fusion.refs_0_), channel_id=1, source_target_pairs={{0,32},{16,48},{32,0},{48,16},{1,33},{17,49},{33,1},{49,17},{2,34}... | collective-permute-start | bytes 589832 | tf_op jit(solution)/shard_map/ppermute | solution.py:267
  44.4 8.4 %collective-permute-start.1 = (bf16[2,384,128]{2,1,0:T(8,128)(2,1)S(1)}, bf16[2,384,128]{2,1,0:T(8,128)(2,1)S(1)}, u32[]{:S(2)}, u32[]{:S(2)}) collective-permute-start(bf16[2,384,128]{2,1,0:T(8,128)(2,1)S(1)} %pad_maximum_fusion.refs_0_), channel_id=1, source_target_pairs={{0,16},{16,0},{32,48},{48,32},{1,17},{17,1},{33,49},{49,33},{2,18}... | collective-permute-start | bytes 589832 | tf_op jit(solution)/shard_map/ppermute | solution.py:267
  45.0 3.5 %collective-permute-start.5 = (bf16[1,384,128]{2,1,0:T(8,128)(2,1)S(1)}, bf16[1,384,128]{2,1,0:T(8,128)(2,1)S(1)}, u32[]{:S(2)}, u32[]{:S(2)}) collective-permute-start(bf16[1,384,128]{2,1,0:T(8,128)(2,1)S(1)} %bitcast.33), channel_id=1, source_target_pairs={{0,1},{1,0},{2,3},{3,2},{4,5},{5,4},{6,7},{7,6},{8,9},{9,8},{10,11... | collective-permute-start | bytes 294920 | tf_op jit(solution)/shard_map/ppermute | solution.py:264
  52.8 5.0 %collective-permute-start.6 = (bf16[2,384,128]{2,1,0:T(8,128)(2,1)S(1)}, bf16[2,384,128]{2,1,0:T(8,128)(2,1)S(1)}, u32[]{:S(2)}, u32[]{:S(2)}) collective-permute-start(bf16[2,384,128]{2,1,0:T(8,128)(2,1)S(1)} %pad_maximum_fusion.refs_0_), channel_id=1, source_target_pairs={{0,8},{8,0},{1,9},{9,1},{2,10},{10,2},{3,11},{11,3},{4,12},{12,4},... | collective-permute-start | bytes 589832 | tf_op jit(solution)/shard_map/ppermute | solution.py:269
  55.4 10.6 %collective-permute-start.8 = (bf16[2,384,128]{2,1,0:T(8,128)(2,1)S(1)}, bf16[2,384,128]{2,1,0:T(8,128)(2,1)S(1)}, u32[]{:S(2)}, u32[]{:S(2)}) collective-permute-start(bf16[2,384,128]{2,1,0:T(8,128)(2,1)S(1)} %collective-permute-done.1.refs_1_), channel_id=1, source_target_pairs={{0,8},{8,0},{1,9},{9,1},{2,10},{10,2},{3,11},{11,3},{4,12},{12,4},... | collective-permute-start | bytes 589832 | tf_op jit(solution)/shard_map/ppermute | solution.py:269
  55.4 10.6 %collective-permute-start.9 = (bf16[2,384,128]{2,1,0:T(8,128)(2,1)S(1)}, bf16[2,384,128]{2,1,0:T(8,128)(2,1)S(1)}, u32[]{:S(2)}, u32[]{:S(2)}) collective-permute-start(bf16[2,384,128]{2,1,0:T(8,128)(2,1)S(1)} %collective-permute-done.2.refs_2_), channel_id=1, source_target_pairs={{0,8},{8,0},{1,9},{9,1},{2,10},{10,2},{3,11},{11,3},{4,12},{12,4},... | collective-permute-start | bytes 589832 | tf_op jit(solution)/shard_map/ppermute | solution.py:269
  55.9 10.1 %collective-permute-start.10 = (bf16[2,384,128]{2,1,0:T(8,128)(2,1)S(1)}, bf16[2,384,128]{2,1,0:T(8,128)(2,1)S(1)}, u32[]{:S(2)}, u32[]{:S(2)}) collective-permute-start(bf16[2,384,128]{2,1,0:T(8,128)(2,1)S(1)} %collective-permute-done.3.refs_3_), channel_id=1, source_target_pairs={{0,8},{8,0},{1,9},{9,1},{2,10},{10,2},{3,11},{11,3},{4,12},{12,4},... | collective-permute-start | bytes 589832 | tf_op jit(solution)/shard_map/ppermute | solution.py:269
  56.2 17.9 %collective-permute-start.12 = (bf16[2,384,128]{2,1,0:T(8,128)(2,1)S(1)}, bf16[2,384,128]{2,1,0:T(8,128)(2,1)S(1)}, u32[]{:S(2)}, u32[]{:S(2)}) collective-permute-start(bf16[2,384,128]{2,1,0:T(8,128)(2,1)S(1)} %pad_maximum_fusion.1.l_ref), channel_id=1, source_target_pairs={{0,4},{4,0},{1,5},{5,1},{2,6},{6,2},{3,7},{7,3},{8,12},{12,8},{9,1... | collective-permute-start | bytes 589832 | tf_op jit(solution)/shard_map/ppermute | solution.py:275
  57.8 14.8 %collective-permute-start.7 = (bf16[2,384,128]{2,1,0:T(8,128)(2,1)S(1)}, bf16[2,384,128]{2,1,0:T(8,128)(2,1)S(1)}, u32[]{:S(2)}, u32[]{:S(2)}) collective-permute-start(bf16[2,384,128]{2,1,0:T(8,128)(2,1)S(1)} %pad_maximum_fusion.1.l_ref), channel_id=1, source_target_pairs={{0,3},{1,2},{2,1},{3,0},{4,7},{5,6},{6,5},{7,4},{8,11},{9,10},{10,... | collective-permute-start | bytes 589832 | tf_op jit(solution)/shard_map/ppermute | solution.py:274
  60.5 29.0 %all-to-all-start.1 = ((bf16[128,24,128]{2,1,0:T(8,128)(2,1)}), bf16[128,24,128]{2,1,0:T(8,128)(2,1)S(1)}, u32[]{:S(2)}, u32[]{:S(2)}) async-start(bf16[128,24,128]{2,1,0:T(8,128)(2,1)} %get-tuple-element.28), calls=%async_computation.1 | async-start | bytes 1572864 | tf_op jit(solution)/shard_map/all_to_all | solution.py:271
  72.6 11.3 %collective-permute-start.11 = (bf16[2,384,128]{2,1,0:T(8,128)(2,1)S(1)}, bf16[2,384,128]{2,1,0:T(8,128)(2,1)S(1)}, u32[]{:S(2)}, u32[]{:S(2)}) collective-permute-start(bf16[2,384,128]{2,1,0:T(8,128)(2,1)S(1)} %collective-permute-done.7.refs_0_), channel_id=1, source_target_pairs={{0,4},{4,0},{1,5},{5,1},{2,6},{6,2},{3,7},{7,3},{8,12},{12,8},{9,1... | collective-permute-start | bytes 589832 | tf_op jit(solution)/shard_map/ppermute | solution.py:278

commit v6 on v5

--- a/solution.py
+++ b/solution.py
@@ -264,8 +264,10 @@
     second = lax.ppermute(near, "y", flipped(4, 1))
     mine = right[None]
     mine = jnp.concatenate([mine, lax.ppermute(mine, "x_hi", flipped(2, 1))])
-    pieces = (mine, lax.ppermute(mine, "z", flipped(4, 1)), lax.ppermute(mine, "z", flipped(4, 2)), lax.ppermute(mine, "z", flipped(4, 3)))
-    pieces, second, updated = lax.optimization_barrier((pieces, second, updated))
+    z_1, z_3 = lax.ppermute(mine, "z", flipped(4, 1)), lax.ppermute(mine, "z", flipped(4, 3))
+    z_2 = lax.ppermute(mine, "z", flipped(4, 2))
+    (mine, z_1, z_3, z_2), second, updated = lax.optimization_barrier(((mine, z_1, z_3, z_2), second, updated))
+    pieces = (mine, z_1, z_2, z_3)
     others = tuple(lax.ppermute(piece, "core", flipped(2, 1)) for piece in pieces)
     updated, _ = lax.optimization_barrier((updated, others[0]))
     returned = lax.all_to_all(updated, AXES, split_axis=0, concat_axis=0, tiled=True)

time: 90.9 us -> 91.4 us (level)
    ppermute x4, starting transfers between devices: 3.1 us -> 1.56 us  [body(): lax.ppermute(piece, 'core', flipped(2, 1))]
    ppermute x1, waiting for transfers between devices: 0.01 us -> 1.39 us  [body(): z_2 = lax.ppermute(mine, 'z', flipped(4, 2))]
    ppermute x1, starting transfers between devices: 1.32 us -> 2.63 us  [body(): z_2 = lax.ppermute(mine, 'z', flipped(4, 2))]
    ppermute x1, waiting for transfers between devices: 1.41 us -> 0.42 us  [body(): lax.ppermute(mine, 'z', flipped(4, 1))]
    ppermute x1, waiting for transfers between devices: 2.87 us -> 3.79 us  [body(): lax.ppermute(mine, 'z', flipped(4, 3))]
  transfers between devices with their start and end apart: 15 -> 15, of which waited for: 5 -> 6; matrix products, arithmetic and copies ran while one was open for 2% -> 2% of each run, Pallas kernels for 24% -> 24%
where the time goes in v6:
time: 91.4 us; the launch traced here: 91.1 us
  Pallas kernels  30.5 us (33%)
  starting transfers between devices  29.8 us (33%)
  waiting for transfers between devices  26.7 us (29%)
  local copies, waits for them, and re-layouts  3.18 us (3%)
    pallas_call x3, Pallas kernels, pair_call(): pl.pallas_call(functools.partial(kernel, places), out_shape=[jax.ShapeDty...  22.1 us
    all_to_all x1, waiting for transfers between devices, body(): lax.all_to_all(packed, AXES, split_axis=0, concat_axis=0, tiled=True)  14.1 us
    all_to_all x1, starting transfers between devices, body(): lax.all_to_all(packed, AXES, split_axis=0, concat_axis=0, tiled=True)  11.5 us
    pallas_call x1, Pallas kernels, attention(): pl.pallas_call(attention_kernel, out_shape=(jax.ShapeDtypeStruct((SEQS, R...  6.32 us
    all_to_all x1, starting transfers between devices, body(): lax.all_to_all(updated, AXES, split_axis=0, concat_axis=0, tiled=True)  5.96 us
    ppermute x1, waiting for transfers between devices, body(): mine = jnp.concatenate([mine, lax.ppermute(mine, 'x_hi', flipped(2, 1))])  4 us
    ppermute x1, waiting for transfers between devices, body(): lax.ppermute(mine, 'z', flipped(4, 3))  3.79 us
    ppermute x1, waiting for transfers between devices, body(): second = lax.ppermute(near, 'y', flipped(4, 1))  2.94 us
  transfers between devices with their start and end apart: 15, of which 6 were waited for; matrix products, arithmetic and copies ran while one was open for 2% of the time, Pallas kernels for 24%

profile of v6, /device:TPU:1, one launch (start us, length us, event | category | flops | bytes accessed | tf_op | source)
XLA Modules:
  0.0 91.1 jit_solution(4829446189257920102)
XLA Ops:
  0.6 0.0 copy-start
  0.6 1.1 %copy-done = bf16[1,1536,256]{2,1,0:T(8,128)(2,1)S(1)} copy-done((bf16[1,1536,256]{2,1,0:T(8,128)(2,1)S(1)}, bf16[1,1536,256]{2,1,0:T(8,128)(2,1)}, u32[]{:S(2)}) %copy-start) | copy-done | bytes 786456
  1.8 0.0 copy-start.3
  1.8 0.0 copy-start.4
  1.8 0.0 copy-start.5
  1.8 1.0 %pack.1 = bf16[128,24,128]{2,1,0:T(8,128)(2,1)} custom-call(bf16[1536,256]{1,0:T(8,128)(2,1)S(1)} %bitcast.26), custom_call_target="tpu_custom_call" | custom-call | tf_op jit(solution)/shard_map/pack/pallas_call | solution.py:251
  2.8 11.5 %all-to-all-start = ((bf16[128,24,128]{2,1,0:T(8,128)(2,1)}), bf16[128,24,128]{2,1,0:T(8,128)(2,1)S(1)}, u32[]{:S(2)}, u32[]{:S(2)}) async-start(bf16[128,24,128]{2,1,0:T(8,128)(2,1)} %pack.1), calls=%async_computation | async-start | bytes 1572864 | tf_op jit(solution)/shard_map/all_to_all | solution.py:255
  14.3 1.5 %fusion = (bf16[1,128,16,32]{1,0,2,3:T(2,128)(2,1)S(1)}, bf16[1,128,16,32]{1,0,2,3:T(2,128)(2,1)S(1)}) fusion(bf16[2,128,16,32]{1,0,2,3:T(2,128)(2,1)} %bitcast.29), kind=kLoop, calls=%fused_computation.8 | loop fusion | bytes 524288 | tf_op jit(solution)/shard_map/slice | solution.py:259
  15.8 0.1 copy.21
  15.9 0.1 copy.20
  16.0 0.0 copy-done.1
  16.1 0.1 stack.41.at_ref
  16.3 14.1 %all-to-all-done.x_ref = bf16[128,24,128]{2,1,0:T(8,128)(2,1)S(1)} async-done(((bf16[128,24,128]{2,1,0:T(8,128)(2,1)}), bf16[128,24,128]{2,1,0:T(8,128)(2,1)S(1)}, u32[]{:S(2)}, u32[]{:S(2)}) %all-to-all-start) | async-done | bytes 786464 | tf_op jit(solution)/shard_map/all_to_all | solution.py:255
  30.4 6.3 %attention.1 = (bf16[128,24,128]{2,1,0:T(8,128)(2,1)}, bf16[384,128]{1,0:T(8,128)(2,1)S(1)}, bf16[384,128]{1,0:T(8,128)(2,1)S(1)}) custom-call(bf16[128,24,128]{2,1,0:T(8,128)(2,1)S(1)} %all-to-all-done.x_ref, bf16[5,256,256]{2,1,0:T(8,128)(2,1)S(1)} %bitcast_dynamic-update-slice_fusion.w_ref, bf16[64,256]{1,0:T(8,128)(2,1)S(1)} %maximum_bitcast_fusion.wlr_ref), custom_call_target="tpu_custom_call" | custom-call | tf_op jit(solution)/shard_map/attention/pallas_call | solution.py:129
  36.7 0.3 collective-permute-start
  37.0 0.7 collective-permute-start.4
  37.7 4.0 %collective-permute-done = bf16[1,384,128]{2,1,0:T(8,128)(2,1)S(1)} collective-permute-done((bf16[1,384,128]{2,1,0:T(8,128)(2,1)S(1)}, bf16[1,384,128]{2,1,0:T(8,128)(2,1)S(1)}, u32[]{:S(2)}, u32[]{:S(2)}) %collective-permute-start) | collective-permute-done | bytes 98336 | tf_op jit(solution)/shard_map/ppermute | solution.py:266
  41.7 2.6 %collective-permute-start.3 = (bf16[2,384,128]{2,1,0:T(8,128)(2,1)S(1)}, bf16[2,384,128]{2,1,0:T(8,128)(2,1)S(1)}, u32[]{:S(2)}, u32[]{:S(2)}) collective-permute-start(bf16[2,384,128]{2,1,0:T(8,128)(2,1)S(1)} %pad_maximum_fusion.refs_0_), channel_id=1, source_target_pairs={{0,32},{16,48},{32,0},{48,16},{1,33},{17,49},{33,1},{49,17},{2,34}... | collective-permute-start | bytes 589832 | tf_op jit(solution)/shard_map/ppermute | solution.py:268
  44.3 0.5 collective-permute-start.2
  44.8 0.0 collective-permute-start.1
  44.8 0.0 collective-permute-done.4
  44.8 0.5 collective-permute-start.5
  45.4 2.9 %collective-permute-done.5 = bf16[1,384,128]{2,1,0:T(8,128)(2,1)S(1)} collective-permute-done((bf16[1,384,128]{2,1,0:T(8,128)(2,1)S(1)}, bf16[1,384,128]{2,1,0:T(8,128)(2,1)S(1)}, u32[]{:S(2)}, u32[]{:S(2)}) %collective-permute-start.5) | collective-permute-done | bytes 98336 | tf_op jit(solution)/shard_map/ppermute | solution.py:264
  48.3 1.4 %collective-permute-done.3.refs_2_ = bf16[2,384,128]{2,1,0:T(8,128)(2,1)S(1)} collective-permute-done((bf16[2,384,128]{2,1,0:T(8,128)(2,1)S(1)}, bf16[2,384,128]{2,1,0:T(8,128)(2,1)S(1)}, u32[]{:S(2)}, u32[]{:S(2)}) %collective-permute-start.3) | collective-permute-done | bytes 196640 | tf_op jit(solution)/shard_map/ppermute | solution.py:268
  49.7 3.8 %collective-permute-done.2.refs_3_ = bf16[2,384,128]{2,1,0:T(8,128)(2,1)S(1)} collective-permute-done((bf16[2,384,128]{2,1,0:T(8,128)(2,1)S(1)}, bf16[2,384,128]{2,1,0:T(8,128)(2,1)S(1)}, u32[]{:S(2)}, u32[]{:S(2)}) %collective-permute-start.2) | collective-permute-done | bytes 196640 | tf_op jit(solution)/shard_map/ppermute | solution.py:267
  53.5 0.4 collective-permute-done.1.refs_1_
  53.9 1.1 %collective-permute-start.6 = (bf16[2,384,128]{2,1,0:T(8,128)(2,1)S(1)}, bf16[2,384,128]{2,1,0:T(8,128)(2,1)S(1)}, u32[]{:S(2)}, u32[]{:S(2)}) collective-permute-start(bf16[2,384,128]{2,1,0:T(8,128)(2,1)S(1)} %pad_maximum_fusion.refs_0_), channel_id=1, source_target_pairs={{0,8},{8,0},{1,9},{9,1},{2,10},{10,2},{3,11},{11,3},{4,12},{12,4},... | collective-permute-start | bytes 589832 | tf_op jit(solution)/shard_map/ppermute | solution.py:271
  55.0 0.0 collective-permute-start.8
  55.0 0.5 collective-permute-start.9
  55.5 0.0 collective-permute-start.10
  55.5 0.1 copy.22.refs_8_.refs_3_.refs_2_
  55.6 0.1 copy.23.refs_9_.refs_4_.refs_3_
  55.7 2.1 %collective-permute-start.12 = (bf16[2,384,128]{2,1,0:T(8,128)(2,1)S(1)}, bf16[2,384,128]{2,1,0:T(8,128)(2,1)S(1)}, u32[]{:S(2)}, u32[]{:S(2)}) collective-permute-start(bf16[2,384,128]{2,1,0:T(8,128)(2,1)S(1)} %pad_maximum_fusion.1.l_ref), channel_id=1, source_target_pairs={{0,4},{4,0},{1,5},{5,1},{2,6},{6,2},{3,7},{7,3},{8,12},{12,8},{9,1... | collective-permute-start | bytes 589832 | tf_op jit(solution)/shard_map/ppermute | solution.py:277
  57.8 0.0 collective-permute-done.6.refs_4_
  57.8 2.7 %collective-permute-start.7 = (bf16[2,384,128]{2,1,0:T(8,128)(2,1)S(1)}, bf16[2,384,128]{2,1,0:T(8,128)(2,1)S(1)}, u32[]{:S(2)}, u32[]{:S(2)}) collective-permute-start(bf16[2,384,128]{2,1,0:T(8,128)(2,1)S(1)} %pad_maximum_fusion.1.l_ref), channel_id=1, source_target_pairs={{0,3},{1,2},{2,1},{3,0},{4,7},{5,6},{6,5},{7,4},{8,11},{9,10},{10,... | collective-permute-start | bytes 589832 | tf_op jit(solution)/shard_map/ppermute | solution.py:276
  60.5 6.0 %all-to-all-start.1 = ((bf16[128,24,128]{2,1,0:T(8,128)(2,1)}), bf16[128,24,128]{2,1,0:T(8,128)(2,1)S(1)}, u32[]{:S(2)}, u32[]{:S(2)}) async-start(bf16[128,24,128]{2,1,0:T(8,128)(2,1)} %get-tuple-element.28), calls=%async_computation.1 | async-start | bytes 1572864 | tf_op jit(solution)/shard_map/all_to_all | solution.py:273
  66.4 0.0 collective-permute-done.8.refs_5_
  66.4 0.0 collective-permute-done.9.refs_6_
  66.5 0.0 collective-permute-done.10.refs_7_
  66.5 6.6 %pair_grid.3 = (bf16[96,192,128]{2,1,0:T(8,128)(2,1)}, bf16[16,128,384]{2,1,0:T(8,128)(2,1)S(1)}) custom-call(s32[5]{0:T(128)S(1)} %stack.41.at_ref, bf16[2,384,128]{2,1,0:T(8,128)(2,1)S(1)} %pad_maximum_fusion.1.l_ref, bf16[2,384,128]{2,1,0:T(8,128)(2,1)S(1)} %pad_maximum_fusion.refs_0_, bf16[2,384,128]{2,1,0:T(8,128)(2,1)S(1)} %collective-permute-done.1.refs_1_, ...), custom_call_target="tpu_custom_call" | custom-call | flops 40000000000 | bytes 1000 | tf_op jit(solution)/shard_map/pair_grid/pallas_call | solution.py:205
  73.1 0.0 collective-permute-done.7.refs_0_
  73.1 1.5 %collective-permute-start.11 = (bf16[2,384,128]{2,1,0:T(8,128)(2,1)S(1)}, bf16[2,384,128]{2,1,0:T(8,128)(2,1)S(1)}, u32[]{:S(2)}, u32[]{:S(2)}) collective-permute-start(bf16[2,384,128]{2,1,0:T(8,128)(2,1)S(1)} %collective-permute-done.7.refs_0_), channel_id=1, source_target_pairs={{0,4},{4,0},{1,5},{5,1},{2,6},{6,2},{3,7},{7,3},{8,12},{12,8},{9,1... | collective-permute-start | bytes 589832 | tf_op jit(solution)/shard_map/ppermute | solution.py:280
  74.6 0.0 collective-permute-done.12.refs_1_
  74.6 9.8 %pair_grid.4.refs_4_ = bf16[96,192,128]{2,1,0:T(8,128)(2,1)} custom-call(s32[5]{0:T(128)S(1)} %stack.41.at_ref, bf16[2,384,128]{2,1,0:T(8,128)(2,1)S(1)} %collective-permute-done.7.refs_0_, bf16[2,384,128]{2,1,0:T(8,128)(2,1)S(1)} %collective-permute-done.12.refs_1_, ...), custom_call_target="tpu_custom_call", output_to_operand_aliasing={{}: (6, {})} | custom-call | flops 1000 | bytes 1000 | tf_op jit(solution)/shard_map/pair_grid/pallas_call | solution.py:205
  84.4 0.0 collective-permute-done.11.refs_0_
  84.4 5.7 %pair_grid.5 = bf16[96,192,128]{2,1,0:T(8,128)(2,1)} custom-call(s32[5]{0:T(128)S(1)} %stack.41.at_ref, bf16[2,384,128]{2,1,0:T(8,128)(2,1)S(1)} %collective-permute-done.11.refs_0_, bf16[16,128,384]{2,1,0:T(8,128)(2,1)S(1)} %get-tuple-element.38.refs_2_.refs_1_, bf16[128,512]{1,0:T(8,128)(2,1)S(1)} %copy.22.refs_8_.refs_3_.refs_2_, ...), custom_call_target="tpu_custom_call", output_to_operand_aliasing={{}: (5, {})} | custom-call | flops 1000 | bytes 1000 | tf_op jit(solution)/shard_map/pair_grid/pallas_call | solution.py:205
  90.1 0.0 all-to-all-done.1.x_ref
  90.1 1.0 %unpack.1 = bf16[1536,256]{1,0:T(8,128)(2,1)} custom-call(bf16[128,24,128]{2,1,0:T(8,128)(2,1)S(1)} %all-to-all-done.1.x_ref), custom_call_target="tpu_custom_call" | custom-call | tf_op jit(solution)/shard_map/unpack/pallas_call | solution.py:284
  (18 shorter events, 0.1 us)
Async XLA Ops:
  0.6 1.1 %copy-start = (bf16[1,1536,256]{2,1,0:T(8,128)(2,1)S(1)}, bf16[1,1536,256]{2,1,0:T(8,128)(2,1)}, u32[]{:S(2)}) copy-start(bf16[1,1536,256]{2,1,0:T(8,128)(2,1)} %param.9) | copy-start | bytes 2359300
  1.8 14.3 %copy-start.1 = (bf16[256,256]{1,0:T(8,128)(2,1)S(1)}, bf16[256,256]{1,0:T(8,128)(2,1)}, u32[]{:S(2)}) copy-start(bf16[256,256]{1,0:T(8,128)(2,1)} %param.10) | copy-start | bytes 393220
  1.8 14.3 %copy-start.2 = (bf16[256,256]{1,0:T(8,128)(2,1)S(1)}, bf16[256,256]{1,0:T(8,128)(2,1)}, u32[]{:S(2)}) copy-start(bf16[256,256]{1,0:T(8,128)(2,1)} %param.11) | copy-start | bytes 393220
  1.8 14.4 %copy-start.6 = (bf16[256,32]{0,1:T(8,128)(2,1)S(1)}, bf16[256,32]{0,1:T(8,128)(2,1)}, u32[]{:S(2)}) copy-start(bf16[256,32]{0,1:T(8,128)(2,1)} %param.16) | copy-start | bytes 49156
  1.8 14.4 %copy-start.7 = (bf16[256,32]{0,1:T(8,128)(2,1)S(1)}, bf16[256,32]{0,1:T(8,128)(2,1)}, u32[]{:S(2)}) copy-start(bf16[256,32]{0,1:T(8,128)(2,1)} %param.15) | copy-start | bytes 49156
  1.8 14.4 %copy-start.3 = (bf16[256,256]{1,0:T(8,128)(2,1)S(1)}, bf16[256,256]{1,0:T(8,128)(2,1)}, u32[]{:S(2)}) copy-start(bf16[256,256]{1,0:T(8,128)(2,1)} %param.12) | copy-start | bytes 393220
  1.8 14.4 %copy-start.4 = (bf16[256,256]{1,0:T(8,128)(2,1)S(1)}, bf16[256,256]{1,0:T(8,128)(2,1)}, u32[]{:S(2)}) copy-start(bf16[256,256]{1,0:T(8,128)(2,1)} %param.13) | copy-start | bytes 393220
  1.8 14.4 %copy-start.5 = (bf16[256,256]{1,0:T(8,128)(2,1)S(1)}, bf16[256,256]{1,0:T(8,128)(2,1)}, u32[]{:S(2)}) copy-start(bf16[256,256]{1,0:T(8,128)(2,1)} %param.14) | copy-start | bytes 393220
  2.8 27.5 %all-to-all-start = ((bf16[128,24,128]{2,1,0:T(8,128)(2,1)}), bf16[128,24,128]{2,1,0:T(8,128)(2,1)S(1)}, u32[]{:S(2)}, u32[]{:S(2)}) async-start(bf16[128,24,128]{2,1,0:T(8,128)(2,1)} %pack.1), calls=%async_computation | async-start | bytes 1572864 | tf_op jit(solution)/shard_map/all_to_all | solution.py:255
  36.7 5.0 %collective-permute-start = (bf16[1,384,128]{2,1,0:T(8,128)(2,1)S(1)}, bf16[1,384,128]{2,1,0:T(8,128)(2,1)S(1)}, u32[]{:S(2)}, u32[]{:S(2)}) collective-permute-start(bf16[1,384,128]{2,1,0:T(8,128)(2,1)S(1)} %bitcast.27), channel_id=1, source_target_pairs={{0,64},{64,0},{1,65},{65,1},{2,66},{66,2},{3,67},{67,3},{4,68},{68... | collective-permute-start | bytes 294920 | tf_op jit(solution)/shard_map/ppermute | solution.py:266
  37.0 7.8 %collective-permute-start.4 = (bf16[384,128]{1,0:T(8,128)(2,1)S(1)}, bf16[384,128]{1,0:T(8,128)(2,1)S(1)}, u32[]{:S(2)}, u32[]{:S(2)}) collective-permute-start(bf16[384,128]{1,0:T(8,128)(2,1)S(1)} %get-tuple-element.24), channel_id=1, source_target_pairs={{0,0},{1,16},{2,32},{3,48},{4,64},{5,80},{6,96},{7,112},{8,8},{9,2... | collective-permute-start | bytes 294920 | tf_op jit(solution)/shard_map/ppermute | solution.py:263
  41.7 8.0 %collective-permute-start.3 = (bf16[2,384,128]{2,1,0:T(8,128)(2,1)S(1)}, bf16[2,384,128]{2,1,0:T(8,128)(2,1)S(1)}, u32[]{:S(2)}, u32[]{:S(2)}) collective-permute-start(bf16[2,384,128]{2,1,0:T(8,128)(2,1)S(1)} %pad_maximum_fusion.refs_0_), channel_id=1, source_target_pairs={{0,32},{16,48},{32,0},{48,16},{1,33},{17,49},{33,1},{49,17},{2,34}... | collective-permute-start | bytes 589832 | tf_op jit(solution)/shard_map/ppermute | solution.py:268
  44.3 9.2 %collective-permute-start.2 = (bf16[2,384,128]{2,1,0:T(8,128)(2,1)S(1)}, bf16[2,384,128]{2,1,0:T(8,128)(2,1)S(1)}, u32[]{:S(2)}, u32[]{:S(2)}) collective-permute-start(bf16[2,384,128]{2,1,0:T(8,128)(2,1)S(1)} %pad_maximum_fusion.refs_0_), channel_id=1, source_target_pairs={{0,48},{16,32},{32,16},{48,0},{1,49},{17,33},{33,17},{49,1},{2,50}... | collective-permute-start | bytes 589832 | tf_op jit(solution)/shard_map/ppermute | solution.py:267
  44.8 9.1 %collective-permute-start.1 = (bf16[2,384,128]{2,1,0:T(8,128)(2,1)S(1)}, bf16[2,384,128]{2,1,0:T(8,128)(2,1)S(1)}, u32[]{:S(2)}, u32[]{:S(2)}) collective-permute-start(bf16[2,384,128]{2,1,0:T(8,128)(2,1)S(1)} %pad_maximum_fusion.refs_0_), channel_id=1, source_target_pairs={{0,16},{16,0},{32,48},{48,32},{1,17},{17,1},{33,49},{49,33},{2,18}... | collective-permute-start | bytes 589832 | tf_op jit(solution)/shard_map/ppermute | solution.py:267
  44.8 3.5 %collective-permute-start.5 = (bf16[1,384,128]{2,1,0:T(8,128)(2,1)S(1)}, bf16[1,384,128]{2,1,0:T(8,128)(2,1)S(1)}, u32[]{:S(2)}, u32[]{:S(2)}) collective-permute-start(bf16[1,384,128]{2,1,0:T(8,128)(2,1)S(1)} %bitcast.33), channel_id=1, source_target_pairs={{0,1},{1,0},{2,3},{3,2},{4,5},{5,4},{6,7},{7,6},{8,9},{9,8},{10,11... | collective-permute-start | bytes 294920 | tf_op jit(solution)/shard_map/ppermute | solution.py:264
  53.9 3.9 %collective-permute-start.6 = (bf16[2,384,128]{2,1,0:T(8,128)(2,1)S(1)}, bf16[2,384,128]{2,1,0:T(8,128)(2,1)S(1)}, u32[]{:S(2)}, u32[]{:S(2)}) collective-permute-start(bf16[2,384,128]{2,1,0:T(8,128)(2,1)S(1)} %pad_maximum_fusion.refs_0_), channel_id=1, source_target_pairs={{0,8},{8,0},{1,9},{9,1},{2,10},{10,2},{3,11},{11,3},{4,12},{12,4},... | collective-permute-start | bytes 589832 | tf_op jit(solution)/shard_map/ppermute | solution.py:271
  55.0 11.5 %collective-permute-start.8 = (bf16[2,384,128]{2,1,0:T(8,128)(2,1)S(1)}, bf16[2,384,128]{2,1,0:T(8,128)(2,1)S(1)}, u32[]{:S(2)}, u32[]{:S(2)}) collective-permute-start(bf16[2,384,128]{2,1,0:T(8,128)(2,1)S(1)} %collective-permute-done.1.refs_1_), channel_id=1, source_target_pairs={{0,8},{8,0},{1,9},{9,1},{2,10},{10,2},{3,11},{11,3},{4,12},{12,4},... | collective-permute-start | bytes 589832 | tf_op jit(solution)/shard_map/ppermute | solution.py:271
  55.0 11.5 %collective-permute-start.9 = (bf16[2,384,128]{2,1,0:T(8,128)(2,1)S(1)}, bf16[2,384,128]{2,1,0:T(8,128)(2,1)S(1)}, u32[]{:S(2)}, u32[]{:S(2)}) collective-permute-start(bf16[2,384,128]{2,1,0:T(8,128)(2,1)S(1)} %collective-permute-done.3.refs_2_), channel_id=1, source_target_pairs={{0,8},{8,0},{1,9},{9,1},{2,10},{10,2},{3,11},{11,3},{4,12},{12,4},... | collective-permute-start | bytes 589832 | tf_op jit(solution)/shard_map/ppermute | solution.py:271
  55.5 11.0 %collective-permute-start.10 = (bf16[2,384,128]{2,1,0:T(8,128)(2,1)S(1)}, bf16[2,384,128]{2,1,0:T(8,128)(2,1)S(1)}, u32[]{:S(2)}, u32[]{:S(2)}) collective-permute-start(bf16[2,384,128]{2,1,0:T(8,128)(2,1)S(1)} %collective-permute-done.2.refs_3_), channel_id=1, source_target_pairs={{0,8},{8,0},{1,9},{9,1},{2,10},{10,2},{3,11},{11,3},{4,12},{12,4},... | collective-permute-start | bytes 589832 | tf_op jit(solution)/shard_map/ppermute | solution.py:271
  55.7 18.8 %collective-permute-start.12 = (bf16[2,384,128]{2,1,0:T(8,128)(2,1)S(1)}, bf16[2,384,128]{2,1,0:T(8,128)(2,1)S(1)}, u32[]{:S(2)}, u32[]{:S(2)}) collective-permute-start(bf16[2,384,128]{2,1,0:T(8,128)(2,1)S(1)} %pad_maximum_fusion.1.l_ref), channel_id=1, source_target_pairs={{0,4},{4,0},{1,5},{5,1},{2,6},{6,2},{3,7},{7,3},{8,12},{12,8},{9,1... | collective-permute-start | bytes 589832 | tf_op jit(solution)/shard_map/ppermute | solution.py:277
  57.8 15.3 %collective-permute-start.7 = (bf16[2,384,128]{2,1,0:T(8,128)(2,1)S(1)}, bf16[2,384,128]{2,1,0:T(8,128)(2,1)S(1)}, u32[]{:S(2)}, u32[]{:S(2)}) collective-permute-start(bf16[2,384,128]{2,1,0:T(8,128)(2,1)S(1)} %pad_maximum_fusion.1.l_ref), channel_id=1, source_target_pairs={{0,3},{1,2},{2,1},{3,0},{4,7},{5,6},{6,5},{7,4},{8,11},{9,10},{10,... | collective-permute-start | bytes 589832 | tf_op jit(solution)/shard_map/ppermute | solution.py:276
  60.5 29.6 %all-to-all-start.1 = ((bf16[128,24,128]{2,1,0:T(8,128)(2,1)}), bf16[128,24,128]{2,1,0:T(8,128)(2,1)S(1)}, u32[]{:S(2)}, u32[]{:S(2)}) async-start(bf16[128,24,128]{2,1,0:T(8,128)(2,1)} %get-tuple-element.28), calls=%async_computation.1 | async-start | bytes 1572864 | tf_op jit(solution)/shard_map/all_to_all | solution.py:273
  73.1 11.3 %collective-permute-start.11 = (bf16[2,384,128]{2,1,0:T(8,128)(2,1)S(1)}, bf16[2,384,128]{2,1,0:T(8,128)(2,1)S(1)}, u32[]{:S(2)}, u32[]{:S(2)}) collective-permute-start(bf16[2,384,128]{2,1,0:T(8,128)(2,1)S(1)} %collective-permute-done.7.refs_0_), channel_id=1, source_target_pairs={{0,4},{4,0},{1,5},{5,1},{2,6},{6,2},{3,7},{7,3},{8,12},{12,8},{9,1... | collective-permute-start | bytes 589832 | tf_op jit(solution)/shard_map/ppermute | solution.py:280
